TPU v7x, 256 devices: a whole 4x4x8 slice. The times are simulated.
256 devices in a mesh: lat: 16 (over x_lo, y, core), lon: 16 (over z, x_hi).
Axes of the slice: x: 4 (x_hi: 2, x_lo: 2; x = x_hi * 2 + x_lo), y: 4, z: 8, core: 2. Of those that a mesh axis runs over, the one named last changes fastest.
Arguments:
- tokens: bfloat16 [128, 768, 512], P('lat', 'lon'), may hold values from -45 to 45
- region_ids: int32 [128, 768], P('lat', 'lon'), may hold values from 0 to 3
- bias_one: float32 [16, 64, 64], replicated, may hold values from -2 to 300
- qkv_one: bfloat16 [512, 1536], replicated, may hold values from -0.25 to 0.25
- out_one: bfloat16 [512, 512], replicated, may hold values from -0.25 to 0.25
- merge_proj: bfloat16 [2048, 1024], replicated, may hold values from -0.125 to 0.125
- bias_two: float32 [8, 64, 64], replicated, may hold values from -2 to 300
- qkv_two: bfloat16 [1024, 1536], replicated, may hold values from -0.1875 to 0.1875
- out_two: bfloat16 [512, 1024], replicated, may hold values from -0.25 to 0.25
Outputs:
- level_one: bfloat16 [128, 768, 512], P('lat', 'lon')
- level_two: bfloat16 [64, 384, 1024], P('lat', 'lon')
All inputs are finite; a program needn't handle non-finite values.
Results may differ from a plain program's by a relative error of at most 0.0095.
Values may be sent and summed in bfloat16 or wider, within the bound.
No kernel may reach another device: no remote copies, remote signals or barrier semaphores. Data moves between devices by JAX's collectives and lax.ppermute only.
A program may use at most 192 MiB of HBM per device.

v0:
```python
import math

import jax
import jax.numpy as jnp
from jax import lax
from jax.experimental import pallas as pl
from jax.experimental.pallas import tpu as pltpu
from jax.sharding import PartitionSpec as P

EPSILON = 1e-05
LOG2E = math.log2(math.e)
BF = jnp.bfloat16
F32 = jnp.float32
ROWS = 8
COLS = 48
TILES = 7
FRAME = 56
D1 = 512
D2 = 1024
VMEM_BYTES = 44 * 1024 * 1024

NT = (((1,), (1,)), ((), ()))
TN = (((0,), (0,)), ((), ()))


def params():
    return pltpu.CompilerParams(vmem_limit_bytes=VMEM_BYTES)


def layer_norm(x):
    width = x.shape[-1]
    mean = jnp.sum(x, axis=-1, keepdims=True) * (1.0 / width)
    c = x - mean
    var = jnp.sum(c * c, axis=-1, keepdims=True) * (1.0 / width)
    return c * lax.rsqrt(var + EPSILON)


def id_rows(ids_ref):
    ids = ids_ref[...].astype(F32)
    return jnp.concatenate([ids, jnp.zeros((ROWS, 128 - COLS), F32)], axis=1)


def edge_kernel(tok_ref, ids_ref, east_ref, west_ref):
    last, first = [], []
    for r in range(ROWS):
        last.append(tok_ref[r, 32:48, :].astype(F32)[12:16])
        first.append(tok_ref[r, 0:16, :].astype(F32)[0:4])
    ids = id_rows(ids_ref)
    wide = jnp.concatenate([ids, jnp.zeros((ROWS, D1 - 128), F32)], axis=1)
    rolled = jnp.concatenate(
        [pltpu.roll(ids, 128 - (COLS - 4), 1), jnp.zeros((ROWS, D1 - 128), F32)], axis=1
    )
    pad = jnp.zeros((ROWS, D1), F32)
    east_ref[...] = jnp.concatenate(last + [rolled, pad], axis=0).astype(BF)
    west_ref[...] = jnp.concatenate(first + [wide, pad], axis=0).astype(BF)


def framed_row(tok_ref, west_ref, east_ref, r):
    start = (r // 4) * 16
    w = west_ref[start : start + 16, :].astype(F32)[(r % 4) * 4 : (r % 4) * 4 + 4]
    e = east_ref[start : start + 16, :].astype(F32)[(r % 4) * 4 : (r % 4) * 4 + 4]
    return jnp.concatenate([w, tok_ref[r].astype(F32), e], axis=0)


def framed_ids(ids_ref, west_ref, east_ref):
    lane = lax.broadcasted_iota(jnp.int32, (ROWS, 128), 1)
    own = pltpu.roll(id_rows(ids_ref), 4, 1)
    w = west_ref[32:48, 0:128].astype(F32)[0:8]
    e = pltpu.roll(east_ref[32:48, 0:128].astype(F32)[0:8], COLS + 4, 1)
    return jnp.where(lane < 4, w, jnp.where(lane < COLS + 4, own, e))


def band_kernel(tok_ref, ids_ref, west_ref, east_ref, cross_ref, pair_ref):
    ids = framed_ids(ids_ref, west_ref, east_ref)
    parity = lax.rem(lax.axis_index("lat"), 2)
    halves = []
    for h in range(2):
        rows = [framed_row(tok_ref, west_ref, east_ref, 4 * h + r) for r in range(4)]
        id_part = ids if h == 0 else pltpu.roll(ids, 4, 0)
        id_part = jnp.concatenate([id_part, jnp.zeros((ROWS, D1 - 128), F32)], axis=1)
        rows += [id_part, jnp.zeros((ROWS, D1), F32)]
        halves.append(jnp.concatenate(rows, axis=0).astype(BF))

    @pl.when(parity == 0)
    def _():
        cross_ref[...] = halves[0]
        pair_ref[...] = halves[1]

    @pl.when(parity == 1)
    def _():
        cross_ref[...] = halves[1]
        pair_ref[...] = halves[0]


def bias_kernel(one_ref, two_ref, one_out, two_out):
    for half in range(2):
        low = 32 * (1 - half)
        for g in range(4):
            part = one_ref[4 * g : 4 * g + 4, low : low + 32, :].reshape(128, 64)
            one_out[half, g] = part.T * LOG2E
    parity = lax.rem(lax.axis_index("lat"), 2)
    low = pl.multiple_of(parity * 32, 32)
    for g in range(2):
        part = two_ref[4 * g : 4 * g + 4, pl.ds(low, 32), :].reshape(128, 64)
        two_out[g] = part.T * LOG2E


def masked_heads(q, head_dim, count):
    lane = lax.broadcasted_iota(jnp.int32, q.shape, 1) // head_dim
    zero = jnp.zeros_like(q)
    return jnp.concatenate([jnp.where(lane == h, q, zero) for h in range(count)], axis=0)


def pick_heads(o, head_dim, count):
    rows = o.shape[0] // count
    lane = lax.broadcasted_iota(jnp.int32, (rows, o.shape[1]), 1) // head_dim
    out = o[0:rows]
    for h in range(1, count):
        out = jnp.where(lane == h, o[h * rows : (h + 1) * rows], out)
    return out


def softmax_keys(s, allowed):
    if allowed is not None:
        s = jnp.where(allowed, s, -1e30)
    p = jnp.exp2(s - jnp.max(s, axis=0, keepdims=True))
    return p * (1.0 / jnp.sum(p, axis=0, keepdims=True))


def main_kernel(
    tok_ref, ids_ref, west_ref, east_ref, cross_ref, pair_ref, bias_ref, qkv_ref,
    out_hbm, merge_hbm, two_hbm,
    one_out, merged_out, query_out, kv_out,
    normed, hot, kv, query, attended, projected, level, parts, out_w, merge_w, two_w, sems,
):
    loads = [
        pltpu.make_async_copy(out_hbm, out_w, sems.at[0]),
        pltpu.make_async_copy(merge_hbm, merge_w, sems.at[1]),
        pltpu.make_async_copy(two_hbm, two_w, sems.at[2]),
    ]
    for load in loads:
        load.start()
    lat = lax.axis_index("lat")
    last = lax.axis_size("lat") - 1
    parity = lax.rem(lat, 2)

    def halo_ids(ref):
        return ref[224:240, 0:128].astype(F32)[0:8]

    cross_ids, pair_ids = halo_ids(cross_ref), halo_ids(pair_ref)
    above = jnp.where(parity == 0, cross_ids, pair_ids)
    below = jnp.where(parity == 0, pair_ids, cross_ids)
    above = jnp.where(lat == 0, -1.0, above)
    below = jnp.where(lat == last, -1.0, below)
    own = framed_ids(ids_ref, west_ref, east_ref)
    frame = jnp.concatenate([above[0:4], own, below[0:4]], axis=0)
    frame = jnp.concatenate([frame, jnp.zeros((112, 128), F32)], axis=0)
    turned = frame.T
    lane = lax.broadcasted_iota(jnp.int32, (FRAME, 128), 1).astype(F32)
    for half in range(2):
        for r in range(0, ROWS, 2):
            pair = []
            for k in range(2):
                at = half * 8 + r + k
                col = jnp.broadcast_to(turned[0:FRAME, at : at + 1], (FRAME, 128))
                pair.append(jnp.where(col == lane, 1.0, 0.0).reshape(TILES, 8, 128))
            hot[half, :, r // 2] = jnp.concatenate(pair, axis=1).astype(BF)

    def put(half, r, rows):
        pair = [layer_norm(x).reshape(TILES, 8, D1) for x in rows]
        normed[half, :, r // 2] = jnp.concatenate(pair, axis=1).astype(BF)

    for r in range(0, ROWS, 2):
        rows = [framed_row(tok_ref, west_ref, east_ref, r + k) for k in range(2)]
        put(r // 4, (r + 4) % 8, rows)
    for r in range(0, 4, 2):
        block = slice(r * FRAME, (r + 2) * FRAME)
        c = cross_ref[block, :].astype(F32)
        p = pair_ref[block, :].astype(F32)
        a = jnp.where(parity == 0, c, p)
        b = jnp.where(parity == 0, p, c)
        put(0, r, [a[0:FRAME], a[FRAME:]])
        put(1, 4 + r, [b[0:FRAME], b[FRAME:]])

    for half in range(2):
        x = normed[half].reshape(TILES * 64, D1)
        kv[half] = jnp.dot(x, qkv_ref[:, D1:], preferred_element_type=F32).astype(BF).reshape(
            TILES, 64, 2 * D1
        )
        low = 2 * (1 - half)
        x = normed[half, :, low : low + 2].reshape(TILES * 32, D1)
        query[half] = jnp.dot(x, qkv_ref[:, :D1], preferred_element_type=F32).astype(BF).reshape(
            TILES, 32, D1
        )

    scale = LOG2E / math.sqrt(32)

    def window(j, carry):
        for half in range(2):
            keys_hot = hot[half, j].reshape(64, 128)
            low = 32 * (1 - half)
            q_hot = keys_hot[low : low + 32]
            same = lax.dot_general(
                keys_hot, jnp.concatenate([q_hot] * 4, axis=0), NT, preferred_element_type=F32
            )
            allowed = same > 0.5
            for g in range(4):
                lanes = slice(g * 128, g * 128 + 128)
                v_lanes = slice(D1 + g * 128, D1 + g * 128 + 128)
                q = masked_heads(query[half, j, :, lanes], 32, 4)
                s = lax.dot_general(kv[half, j, :, lanes], q, NT, preferred_element_type=F32)
                p = softmax_keys(s * scale + bias_ref[half, g], allowed)
                o = lax.dot_general(
                    p.astype(BF), kv[half, j, :, v_lanes], TN, preferred_element_type=F32
                )
                attended[half, j, :, lanes] = pick_heads(o, 32, 4).astype(BF)
        return carry

    lax.fori_loop(0, TILES, window, 0)

    loads[0].wait()
    for half in range(2):
        x = attended[half].reshape(TILES * 32, D1)
        projected[half] = jnp.dot(x, out_w[...], preferred_element_type=F32).reshape(
            TILES, 4, 8, D1
        )
    for r in range(ROWS):
        add = projected[r // 4, :, r % 4].reshape(FRAME, D1)[4 : 4 + COLS]
        done = (tok_ref[r].astype(F32) + add).astype(BF)
        one_out[r] = done
        for n in range(4):
            level[n, r] = done[:, n * 128 : n * 128 + 128].astype(F32)

    for i in range(4):
        quartet = [
            jnp.concatenate(
                [level[n, 2 * i + dr, pl.ds(dc, COLS // 2, 2), :] for n in range(4)], axis=1
            )
            for dc in range(2)
            for dr in range(2)
        ]
        total = sum(jnp.sum(x, axis=-1, keepdims=True) for x in quartet)
        quartet = [x - total * (1.0 / (4 * D1)) for x in quartet]
        total = sum(jnp.sum(x * x, axis=-1, keepdims=True) for x in quartet)
        factor = lax.rsqrt(total * (1.0 / (4 * D1)) + EPSILON)
        for n in range(4):
            parts[n, :, i] = (quartet[n] * factor).reshape(3, 8, D1)
    loads[1].wait()
    merged = jnp.zeros((96, D2), F32)
    for n in range(4):
        merged += jnp.dot(
            parts[n].reshape(96, D1).astype(BF),
            merge_w[n * D1 : (n + 1) * D1, :],
            preferred_element_type=F32,
        )
    merged = merged.astype(BF)
    merged_out[...] = merged
    x = layer_norm(merged.astype(F32)).astype(BF)
    loads[2].wait()
    kv_out[...] = jnp.dot(x, two_w[:, 512:], preferred_element_type=F32).astype(BF)
    query_out[...] = jnp.dot(x, two_w[:, :512], preferred_element_type=F32).astype(BF)


def level_two_kernel(
    query_ref, kv_ref, other_ref, merged_ref, bias_ref, out_ref, two_out, keys, attended, result
):
    parity = lax.rem(lax.axis_index("lat"), 2)
    mine = pl.multiple_of(parity * 32, 32)
    theirs = pl.multiple_of(32 - parity * 32, 32)
    scale = LOG2E / math.sqrt(64)
    for w in range(3):
        keys[w, pl.ds(mine, 32), :] = kv_ref[w * 32 : w * 32 + 32, :]
        keys[w, pl.ds(theirs, 32), :] = other_ref[w * 32 : w * 32 + 32, :]
    for w in range(3):
        for g in range(2):
            lanes = slice(g * 256, g * 256 + 256)
            v_lanes = slice(512 + g * 256, 512 + g * 256 + 256)
            q = masked_heads(query_ref[w * 32 : w * 32 + 32, lanes], 64, 4)
            s = lax.dot_general(keys[w, :, lanes], q, NT, preferred_element_type=F32)
            p = softmax_keys(s * scale + bias_ref[g], None)
            o = lax.dot_general(p.astype(BF), keys[w, :, v_lanes], TN, preferred_element_type=F32)
            attended[w * 32 : w * 32 + 32, lanes] = pick_heads(o, 64, 4).astype(BF)
    add = jnp.dot(attended[...], out_ref[...], preferred_element_type=F32)
    result[...] = (merged_ref[...].astype(F32) + add).reshape(3, 4, 8, D2)
    for i in range(4):
        two_out[i] = result[:, i].reshape(24, D2).astype(BF)


def vmem(count):
    return [pl.BlockSpec(memory_space=pltpu.VMEM)] * count


def call(kernel, outs, args, hbm=0, scratch=(), flops=1000, size=1000):
    shapes = [jax.ShapeDtypeStruct(s, d) for s, d in outs]
    return pl.pallas_call(
        kernel,
        out_shape=shapes,
        in_specs=vmem(len(args) - hbm) + [pl.BlockSpec(memory_space=pl.ANY)] * hbm,
        out_specs=vmem(len(outs)),
        scratch_shapes=list(scratch),
        compiler_params=params(),
        cost_estimate=pl.CostEstimate(flops=flops, bytes_accessed=size, transcendentals=0),
    )(*args)


def on_device(
    tokens, region_ids, bias_one, qkv_one, out_one, merge_proj, bias_two, qkv_two, out_two
):
    lat_count = lax.axis_size("lat")
    lon_count = lax.axis_size("lon")
    pairs = [(i, i ^ 1) for i in range(lat_count)]
    across = [(i, (i + (1 if i % 2 else -1)) % lat_count) for i in range(lat_count)]
    eastward = [(i, (i + 1) % lon_count) for i in range(lon_count)]
    westward = [(i, (i - 1) % lon_count) for i in range(lon_count)]

    to_east, to_west = call(edge_kernel, [((48, D1), BF)] * 2, [tokens, region_ids])
    from_west = lax.ppermute(to_east, "lon", eastward)
    from_east = lax.ppermute(to_west, "lon", westward)
    table_one, table_two = call(
        bias_kernel, [((2, 4, 64, 128), F32), ((2, 64, 128), F32)], [bias_one, bias_two],
        flops=10**9, size=10**6,
    )
    to_cross, to_pair = call(
        band_kernel, [((240, D1), BF)] * 2, [tokens, region_ids, from_west, from_east]
    )
    from_cross = lax.ppermute(to_cross, "lat", across)
    from_pair = lax.ppermute(to_pair, "lat", pairs)
    level_one, merged, query, kv = call(
        main_kernel,
        [((ROWS, COLS, D1), BF), ((96, D2), BF), ((96, 512), BF), ((96, 1024), BF)],
        [
            tokens, region_ids, from_west, from_east, from_cross, from_pair, table_one, qkv_one,
            out_one, merge_proj, qkv_two,
        ],
        hbm=3,
        scratch=[
            pltpu.VMEM((2, TILES, 4, 16, D1), BF),
            pltpu.VMEM((2, TILES, 4, 16, 128), BF),
            pltpu.VMEM((2, TILES, 64, 2 * D1), BF),
            pltpu.VMEM((2, TILES, 32, D1), BF),
            pltpu.VMEM((2, TILES, 32, D1), BF),
            pltpu.VMEM((2, TILES, 4, 8, D1), F32),
            pltpu.VMEM((4, ROWS, COLS, 128), F32),
            pltpu.VMEM((4, 3, 4, 8, D1), F32),
            pltpu.VMEM((D1, D1), BF),
            pltpu.VMEM((4 * D1, D2), BF),
            pltpu.VMEM((D2, 1536), BF),
            pltpu.SemaphoreType.DMA((3,)),
        ],
        flops=3 * 10**9, size=10**7,
    )
    other = lax.ppermute(kv, "lat", pairs)
    (level_two,) = call(
        level_two_kernel,
        [((4, 24, D2), BF)],
        [query, kv, other, merged, table_two, out_two],
        scratch=[
            pltpu.VMEM((3, 64, 1024), BF),
            pltpu.VMEM((96, 512), BF),
            pltpu.VMEM((3, 4, 8, D2), F32),
        ],
        flops=10**9, size=10**6,
    )
    return (level_one, level_two)


def solution(mesh):
    placed = (P("lat", "lon", None), P("lat", "lon"), P(), P(), P(), P(), P(), P(), P())
    return jax.shard_map(
        on_device,
        mesh=mesh,
        in_specs=placed,
        out_specs=(P("lat", "lon", None), P("lat", "lon", None)),
        check_vma=False,
    )
```

profile of v0, /device:TPU:1, one launch (start us, length us, event | category | flops | bytes accessed | tf_op | source)
XLA Modules:
  0.0 46.5 jit_solution(15381838549149172290)
XLA Ops:
  0.6 0.0 copy-start
  0.6 1.0 %copy-done = bf16[8,48,512]{2,1,0:T(8,128)(2,1)S(1)} copy-done((bf16[8,48,512]{2,1,0:T(8,128)(2,1)S(1)}, bf16[8,48,512]{2,1,0:T(8,128)(2,1)}, u32[]{:S(2)}) %copy-start) | copy-done | bytes 393240
  1.6 0.0 copy-start.2
  1.6 0.7 %copy-done.2 = s32[8,48]{1,0:T(8,128)S(1)} copy-done((s32[8,48]{1,0:T(8,128)S(1)}, s32[8,48]{1,0:T(8,128)}, u32[]{:S(2)}) %copy-start.2) | copy-done | bytes 1560
  2.3 0.0 copy-start.1
  2.3 0.0 copy-start.3
  2.3 0.0 copy-start.4
  2.3 0.1 shard_map.104
  2.4 3.6 %collective-permute-start = (bf16[48,512]{1,0:T(8,128)(2,1)S(1)}, bf16[48,512]{1,0:T(8,128)(2,1)S(1)}, u32[]{:S(2)}, u32[]{:S(2)}) collective-permute-start(bf16[48,512]{1,0:T(8,128)(2,1)S(1)} %get-tuple-element.12), channel_id=1, source_target_pairs={{0,1},{1,2},{2,3},{3,4},{4,5},{5,6},{6,7},{7,8},{8,9},{9,10},{10,1... | collective-permute-start | bytes 147464 | tf_op jit(solution)/shard_map/ppermute | solution.py:317
  6.0 5.4 %collective-permute-start.1 = (bf16[48,512]{1,0:T(8,128)(2,1)S(1)}, bf16[48,512]{1,0:T(8,128)(2,1)S(1)}, u32[]{:S(2)}, u32[]{:S(2)}) collective-permute-start(bf16[48,512]{1,0:T(8,128)(2,1)S(1)} %get-tuple-element.13), channel_id=1, source_target_pairs={{0,15},{1,0},{2,1},{3,2},{4,3},{5,4},{6,5},{7,6},{8,7},{9,8},{10,9... | collective-permute-start | bytes 147464 | tf_op jit(solution)/shard_map/ppermute | solution.py:318
  11.4 1.4 %collective-permute-done.west_ref = bf16[48,512]{1,0:T(8,128)(2,1)S(1)} collective-permute-done((bf16[48,512]{1,0:T(8,128)(2,1)S(1)}, bf16[48,512]{1,0:T(8,128)(2,1)S(1)}, u32[]{:S(2)}, u32[]{:S(2)}) %collective-permute-start) | collective-permute-done | bytes 49184 | tf_op jit(solution)/shard_map/ppermute | solution.py:317
  12.8 0.0 collective-permute-done.1.east_ref
  12.8 0.1 shard_map.105
  12.9 2.8 %collective-permute-start.2 = (bf16[240,512]{1,0:T(8,128)(2,1)S(1)}, bf16[240,512]{1,0:T(8,128)(2,1)S(1)}, u32[]{:S(2)}, u32[]{:S(2)}) collective-permute-start(bf16[240,512]{1,0:T(8,128)(2,1)S(1)} %get-tuple-element.14), channel_id=1, source_target_pairs={{0,240},{16,32},{32,16},{48,64},{64,48},{80,96},{96,80},{112,128},... | collective-permute-start | bytes 737288 | tf_op jit(solution)/shard_map/ppermute | solution.py:326
  15.7 0.4 collective-permute-start.3
  16.2 0.0 copy-start.7
  16.2 1.0 %copy-done.7 = f32[16,64,64]{2,1,0:T(8,128)S(1)} copy-done((f32[16,64,64]{2,1,0:T(8,128)S(1)}, f32[16,64,64]{2,1,0:T(8,128)}, u32[]{:S(2)}) %copy-start.7) | copy-done | bytes 262168
  17.2 0.0 copy-start.9
  17.2 0.9 %copy-done.9 = f32[8,64,64]{2,1,0:T(8,128)S(1)} copy-done((f32[8,64,64]{2,1,0:T(8,128)S(1)}, f32[8,64,64]{2,1,0:T(8,128)}, u32[]{:S(2)}) %copy-start.9) | copy-done | bytes 131096
  18.2 0.0 copy-start.8
  18.2 0.2 shard_map.106
  18.4 1.5 %collective-permute-done.2.cross_ref = bf16[240,512]{1,0:T(8,128)(2,1)S(1)} collective-permute-done((bf16[240,512]{1,0:T(8,128)(2,1)S(1)}, bf16[240,512]{1,0:T(8,128)(2,1)S(1)}, u32[]{:S(2)}, u32[]{:S(2)}) %collective-permute-start.2) | collective-permute-done | bytes 245792 | tf_op jit(solution)/shard_map/ppermute | solution.py:326
  19.9 0.0 collective-permute-done.3.pair_ref
  19.9 0.0 copy-done.1
  19.9 0.0 copy-done.3
  19.9 0.0 copy-done.4
  19.9 0.0 copy-done.8
  19.9 0.0 copy-start.5
  20.0 1.4 %copy-done.5 = bf16[512,1536]{1,0:T(8,128)(2,1)S(1)} copy-done((bf16[512,1536]{1,0:T(8,128)(2,1)S(1)}, bf16[512,1536]{1,0:T(8,128)(2,1)}, u32[]{:S(2)}) %copy-start.5) | copy-done | bytes 1572888
  21.4 0.0 copy-start.6
  21.4 19.9 %shard_map.107 = (bf16[8,48,512]{2,1,0:T(8,128)(2,1)}, bf16[96,1024]{1,0:T(8,128)(2,1)S(1)}, bf16[96,512]{1,0:T(8,128)(2,1)S(1)}, bf16[96,1024]{1,0:T(8,128)(2,1)S(1)}) custom-call(bf16[8,48,512]{2,1,0:T(8,128)(2,1)S(1)} %copy-done.1, s32[8,48]{1,0:T(8,128)S(1)} %copy-done.3, bf16[48,512]{1,0:T(8,128)(2,1)S(1)} %collective-permute-done.west_ref, ...), custom_call_target="tpu_custom_call" | custom-call | flops 3000000000 | bytes 10000000 | tf_op jit(solution)/shard_map/pallas_call | solution.py:295
  41.3 2.5 %collective-permute-start.4 = (bf16[96,1024]{1,0:T(8,128)(2,1)S(1)}, bf16[96,1024]{1,0:T(8,128)(2,1)S(1)}, u32[]{:S(2)}, u32[]{:S(2)}) collective-permute-start(bf16[96,1024]{1,0:T(8,128)(2,1)S(1)} %get-tuple-element.19.kv_ref), channel_id=1, source_target_pairs={{0,16},{16,0},{32,48},{48,32},{64,80},{80,64},{96,112},{112,96},{1... | collective-permute-start | bytes 589832 | tf_op jit(solution)/shard_map/ppermute | solution.py:352
  43.8 1.1 %collective-permute-done.4.other_ref = bf16[96,1024]{1,0:T(8,128)(2,1)S(1)} collective-permute-done((bf16[96,1024]{1,0:T(8,128)(2,1)S(1)}, bf16[96,1024]{1,0:T(8,128)(2,1)S(1)}, u32[]{:S(2)}, u32[]{:S(2)}) %collective-permute-start.4) | collective-permute-done | bytes 196640 | tf_op jit(solution)/shard_map/ppermute | solution.py:352
  44.8 0.0 copy-done.6
  44.8 1.7 %shard_map.108 = bf16[4,24,1024]{2,1,0:T(8,128)(2,1)} custom-call(bf16[96,512]{1,0:T(8,128)(2,1)S(1)} %get-tuple-element.18.query_ref, bf16[96,1024]{1,0:T(8,128)(2,1)S(1)} %get-tuple-element.19.kv_ref, bf16[96,1024]{1,0:T(8,128)(2,1)S(1)} %collective-permute-done.4.other_ref, bf16[96,1024]{1,0:T(8,128)(2,1)S(1)} %get-tuple-element.20.merged_ref, ...), custom_call_target="tpu_custom_call" | custom-call | flops 1000000000 | bytes 1000000 | tf_op jit(solution)/shard_map/pallas_call | solution.py:295
Async XLA Ops:
  0.6 1.0 %copy-start = (bf16[8,48,512]{2,1,0:T(8,128)(2,1)S(1)}, bf16[8,48,512]{2,1,0:T(8,128)(2,1)}, u32[]{:S(2)}) copy-start(bf16[8,48,512]{2,1,0:T(8,128)(2,1)} %tok_ref.5) | copy-start | bytes 1179652
  1.6 0.7 %copy-start.2 = (s32[8,48]{1,0:T(8,128)S(1)}, s32[8,48]{1,0:T(8,128)}, u32[]{:S(2)}) copy-start(s32[8,48]{1,0:T(8,128)} %ids_ref.5) | copy-start | bytes 4612
  2.3 17.6 %copy-start.1 = (bf16[8,48,512]{2,1,0:T(8,128)(2,1)S(1)}, bf16[8,48,512]{2,1,0:T(8,128)(2,1)}, u32[]{:S(2)}) copy-start(bf16[8,48,512]{2,1,0:T(8,128)(2,1)} %tok_ref.5) | copy-start | bytes 1179652
  2.3 17.6 %copy-start.3 = (s32[8,48]{1,0:T(8,128)S(1)}, s32[8,48]{1,0:T(8,128)}, u32[]{:S(2)}) copy-start(s32[8,48]{1,0:T(8,128)} %ids_ref.5) | copy-start | bytes 4612
  2.3 17.6 %copy-start.4 = (bf16[1024,1536]{1,0:T(8,128)(2,1)S(1)}, bf16[1024,1536]{1,0:T(8,128)(2,1)}, u32[]{:S(2)}) copy-start(bf16[1024,1536]{1,0:T(8,128)(2,1)} %two_hbm.1) | copy-start | bytes 9437188
  2.4 10.4 %collective-permute-start = (bf16[48,512]{1,0:T(8,128)(2,1)S(1)}, bf16[48,512]{1,0:T(8,128)(2,1)S(1)}, u32[]{:S(2)}, u32[]{:S(2)}) collective-permute-start(bf16[48,512]{1,0:T(8,128)(2,1)S(1)} %get-tuple-element.12), channel_id=1, source_target_pairs={{0,1},{1,2},{2,3},{3,4},{4,5},{5,6},{6,7},{7,8},{8,9},{9,10},{10,1... | collective-permute-start | bytes 147464 | tf_op jit(solution)/shard_map/ppermute | solution.py:317
  6.0 6.8 %collective-permute-start.1 = (bf16[48,512]{1,0:T(8,128)(2,1)S(1)}, bf16[48,512]{1,0:T(8,128)(2,1)S(1)}, u32[]{:S(2)}, u32[]{:S(2)}) collective-permute-start(bf16[48,512]{1,0:T(8,128)(2,1)S(1)} %get-tuple-element.13), channel_id=1, source_target_pairs={{0,15},{1,0},{2,1},{3,2},{4,3},{5,4},{6,5},{7,6},{8,7},{9,8},{10,9... | collective-permute-start | bytes 147464 | tf_op jit(solution)/shard_map/ppermute | solution.py:318
  12.9 7.0 %collective-permute-start.2 = (bf16[240,512]{1,0:T(8,128)(2,1)S(1)}, bf16[240,512]{1,0:T(8,128)(2,1)S(1)}, u32[]{:S(2)}, u32[]{:S(2)}) collective-permute-start(bf16[240,512]{1,0:T(8,128)(2,1)S(1)} %get-tuple-element.14), channel_id=1, source_target_pairs={{0,240},{16,32},{32,16},{48,64},{64,48},{80,96},{96,80},{112,128},... | collective-permute-start | bytes 737288 | tf_op jit(solution)/shard_map/ppermute | solution.py:326
  15.7 4.2 %collective-permute-start.3 = (bf16[240,512]{1,0:T(8,128)(2,1)S(1)}, bf16[240,512]{1,0:T(8,128)(2,1)S(1)}, u32[]{:S(2)}, u32[]{:S(2)}) collective-permute-start(bf16[240,512]{1,0:T(8,128)(2,1)S(1)} %get-tuple-element.15), channel_id=1, source_target_pairs={{0,16},{16,0},{32,48},{48,32},{64,80},{80,64},{96,112},{112,96},{1... | collective-permute-start | bytes 737288 | tf_op jit(solution)/shard_map/ppermute | solution.py:327
  16.2 1.0 %copy-start.7 = (f32[16,64,64]{2,1,0:T(8,128)S(1)}, f32[16,64,64]{2,1,0:T(8,128)}, u32[]{:S(2)}) copy-start(f32[16,64,64]{2,1,0:T(8,128)} %one_ref.1) | copy-start | bytes 786436
  17.2 0.9 %copy-start.9 = (f32[8,64,64]{2,1,0:T(8,128)S(1)}, f32[8,64,64]{2,1,0:T(8,128)}, u32[]{:S(2)}) copy-start(f32[8,64,64]{2,1,0:T(8,128)} %two_ref.1) | copy-start | bytes 393220
  18.2 1.8 %copy-start.8 = (bf16[512,512]{1,0:T(8,128)(2,1)S(1)}, bf16[512,512]{1,0:T(8,128)(2,1)}, u32[]{:S(2)}) copy-start(bf16[512,512]{1,0:T(8,128)(2,1)} %out_hbm.1) | copy-start | bytes 1572868
  19.9 1.4 %copy-start.5 = (bf16[512,1536]{1,0:T(8,128)(2,1)S(1)}, bf16[512,1536]{1,0:T(8,128)(2,1)}, u32[]{:S(2)}) copy-start(bf16[512,1536]{1,0:T(8,128)(2,1)} %qkv_ref.1) | copy-start | bytes 4718596
  21.4 23.5 %copy-start.6 = (bf16[512,1024]{1,0:T(8,128)(2,1)S(1)}, bf16[512,1024]{1,0:T(8,128)(2,1)}, u32[]{:S(2)}) copy-start(bf16[512,1024]{1,0:T(8,128)(2,1)} %out_ref.1) | copy-start | bytes 3145732
  41.3 3.5 %collective-permute-start.4 = (bf16[96,1024]{1,0:T(8,128)(2,1)S(1)}, bf16[96,1024]{1,0:T(8,128)(2,1)S(1)}, u32[]{:S(2)}, u32[]{:S(2)}) collective-permute-start(bf16[96,1024]{1,0:T(8,128)(2,1)S(1)} %get-tuple-element.19.kv_ref), channel_id=1, source_target_pairs={{0,16},{16,0},{32,48},{48,32},{64,80},{80,64},{96,112},{112,96},{1... | collective-permute-start | bytes 589832 | tf_op jit(solution)/shard_map/ppermute | solution.py:352
where the time goes:
time: 47.3 us; the launch traced here: 46.5 us
  Pallas kernels  22.1 us (47%)
  starting transfers between devices  14.7 us (31%)
  local copies, waits for them, and re-layouts  5.09 us (11%)
  waiting for transfers between devices  4 us (8%)
  between operations  0.7 us (1%)
    pallas_call x5, Pallas kernels, call(): pl.pallas_call(kernel, out_shape=shapes, in_specs=vmem(len(args) - hbm) +...  22.1 us
    ppermute x1, starting transfers between devices, on_device(): from_east = lax.ppermute(to_west, 'lon', westward)  5.38 us
    unnamed x20, local copies, waits for them, and re-layouts  5.09 us
    ppermute x1, starting transfers between devices, on_device(): from_west = lax.ppermute(to_east, 'lon', eastward)  3.6 us
    ppermute x1, starting transfers between devices, on_device(): from_cross = lax.ppermute(to_cross, 'lat', across)  2.82 us
    ppermute x1, starting transfers between devices, on_device(): other = lax.ppermute(kv, 'lat', pairs)  2.46 us
    ppermute x1, waiting for transfers between devices, on_device(): from_cross = lax.ppermute(to_cross, 'lat', across)  1.53 us
    ppermute x1, waiting for transfers between devices, on_device(): from_west = lax.ppermute(to_east, 'lon', eastward)  1.39 us
  transfers between devices with their start and end apart: 5, of which 3 were waited for; matrix products, arithmetic and copies ran while one was open for 0% of the time, Pallas kernels for 0%

commit v1 on v0

v1 whole, which is shorter than its diff:
```python
import math

import jax
import jax.numpy as jnp
from jax import lax
from jax.experimental import pallas as pl
from jax.experimental.pallas import tpu as pltpu
from jax.sharding import PartitionSpec as P

EPSILON = 1e-05
LOG2E = math.log2(math.e)
BF = jnp.bfloat16
F32 = jnp.float32
ROWS = 8
COLS = 48
TILES = 7
INSIDE = 5
FRAME = 56
D1 = 512
D2 = 1024
MIB = 1024 * 1024

NT = (((1,), (1,)), ((), ()))
TN = (((0,), (0,)), ((), ()))


def layer_norm(x):
    width = x.shape[-1]
    mean = jnp.sum(x, axis=-1, keepdims=True) * (1.0 / width)
    c = x - mean
    var = jnp.sum(c * c, axis=-1, keepdims=True) * (1.0 / width)
    return c * lax.rsqrt(var + EPSILON)


def lanes_to(x, width):
    return jnp.concatenate([x, jnp.zeros((x.shape[0], width - x.shape[1]), x.dtype)], axis=1)


def lat_parity():
    return lax.rem(lax.axis_index("lat"), 2)


def lon_parity():
    return lax.rem(lax.axis_index("lon"), 2)


def start_all(pairs, sems):
    copies = [pltpu.make_async_copy(src, dst, sems.at[n]) for n, (src, dst) in enumerate(pairs)]
    for copy in copies:
        copy.start()
    return copies


def edge_kernel(tok_hbm, ids_hbm, inner_ref, outer_ref, tok_ref, ids_ref, sems):
    copies = start_all(
        [
            (ids_hbm, ids_ref),
            (tok_hbm.at[:, 0:16], tok_ref.at[:, 0:16]),
            (tok_hbm.at[:, 32:48], tok_ref.at[:, 32:48]),
            (tok_hbm.at[:, 16:32], tok_ref.at[:, 16:32]),
        ],
        sems,
    )
    for copy in copies[:3]:
        copy.wait()
    first = [tok_ref[r, 0:16].astype(F32)[0:4] for r in range(ROWS)]
    last = [tok_ref[r, 32:48].astype(F32)[12:16] for r in range(ROWS)]
    ids = lanes_to(ids_ref[...].astype(F32), 128)
    pad = jnp.zeros((ROWS, D1), F32)
    first = jnp.concatenate(first + [lanes_to(ids, D1), pad], axis=0).astype(BF)
    ids = pltpu.roll(ids, 128 - (COLS - 4), 1)
    last = jnp.concatenate(last + [lanes_to(ids, D1), pad], axis=0).astype(BF)
    even = lon_parity() == 0
    inner_ref[...] = jnp.where(even, last, first)
    outer_ref[...] = jnp.where(even, first, last)
    copies[3].wait()


def sides(inner_ref, outer_ref):
    inner, outer = inner_ref[...].astype(F32), outer_ref[...].astype(F32)
    even = lon_parity() == 0
    return jnp.where(even, outer, inner), jnp.where(even, inner, outer)


def own_kernel(
    qkv_hbm, one_hbm, two_hbm, out_hbm, next_hbm, tok_ref,
    inside_out, one_out, two_out, qkv_ref, out_ref, next_ref,
    normed, one_ref, two_ref, sems,
):
    copies = start_all(
        [
            (one_hbm, one_ref),
            (two_hbm, two_ref),
            (qkv_hbm, qkv_ref),
            (out_hbm, out_ref),
            (next_hbm, next_ref),
        ],
        sems,
    )
    for r in range(0, ROWS, 2):
        pair = []
        for k in range(2):
            x = layer_norm(tok_ref[r + k].astype(F32))
            pair.append(x[4 : COLS - 4].reshape(INSIDE, 8, D1))
        normed[r // 4, :, (r % 4) // 2] = jnp.concatenate(pair, axis=1).astype(BF)
    copies[0].wait()
    copies[1].wait()
    for half in range(2):
        low = 32 * (1 - half)
        for g in range(4):
            turned = one_ref[4 * g : 4 * g + 4, low : low + 32, :].reshape(128, 64).T * LOG2E
            one_out[half, g, 0:32] = turned[low : low + 32]
            one_out[half, g, 32:64] = turned[32 - low : 64 - low]
    low = pl.multiple_of(lat_parity() * 32, 32)
    for g in range(2):
        part = two_ref[4 * g : 4 * g + 4, pl.ds(low, 32), :].reshape(128, 64)
        two_out[g] = part.T * LOG2E
    copies[2].wait()
    x = normed[...].reshape(2 * INSIDE * 32, D1)
    inside_out[...] = (
        jnp.dot(x, qkv_ref[...], preferred_element_type=F32)
        .astype(BF)
        .reshape(2, INSIDE, 32, 3 * D1)
    )
    copies[3].wait()
    copies[4].wait()


def band_kernel(
    tok_ref, ids_ref, inner_ref, outer_ref, after_ref, cross_ref, pair_ref, frame_ref
):
    west, east = sides(inner_ref, outer_ref)
    lane = lax.broadcasted_iota(jnp.int32, (ROWS, 128), 1)
    own = pltpu.roll(lanes_to(ids_ref[...].astype(F32), 128), 4, 1)
    far = pltpu.roll(east[32:40, 0:128], COLS + 4, 1)
    ids = jnp.where(lane < 4, west[32:40, 0:128], jnp.where(lane < COLS + 4, own, far))
    frame_ref[...] = ids
    halves = []
    for h in range(2):
        rows = []
        for r in range(4 * h, 4 * h + 4):
            rows += [west[4 * r : 4 * r + 4], tok_ref[r].astype(F32), east[4 * r : 4 * r + 4]]
        rows.append(lanes_to(ids if h == 0 else pltpu.roll(ids, 4, 0), D1))
        rows.append(jnp.zeros((ROWS, D1), F32))
        halves.append(jnp.concatenate(rows, axis=0).astype(BF))
    even = lat_parity() == 0
    cross_ref[...] = jnp.where(even, halves[0], halves[1])
    pair_ref[...] = jnp.where(even, halves[1], halves[0])


def side_kernel(
    merge_hbm, last_hbm, tok_ref, inner_ref, outer_ref, qkv_ref, after_ref,
    qkv_out, merge_ref, last_ref, sems,
):
    copies = start_all([(merge_hbm, merge_ref), (last_hbm, last_ref)], sems)
    west, east = sides(inner_ref, outer_ref)
    rows = []
    for half in range(2):
        for r in range(4 * half, 4 * half + 4):
            rows += [west[4 * r : 4 * r + 4], tok_ref[r, 0:16].astype(F32)[0:4]]
        for r in range(4 * half, 4 * half + 4):
            rows += [tok_ref[r, 32:48].astype(F32)[12:16], east[4 * r : 4 * r + 4]]
    x = layer_norm(jnp.concatenate(rows, axis=0)).astype(BF)
    qkv_out[...] = (
        jnp.dot(x, qkv_ref[...], preferred_element_type=F32).astype(BF).reshape(2, 2, 32, 3 * D1)
    )
    for copy in copies:
        copy.wait()


def masked_heads(q, head_dim, count):
    lane = lax.broadcasted_iota(jnp.int32, q.shape, 1) // head_dim
    zero = jnp.zeros_like(q)
    return jnp.concatenate([jnp.where(lane == h, q, zero) for h in range(count)], axis=0)


def pick_heads(o, head_dim, count):
    rows = o.shape[0] // count
    lane = lax.broadcasted_iota(jnp.int32, (rows, o.shape[1]), 1) // head_dim
    out = o[0:rows]
    for h in range(1, count):
        out = jnp.where(lane == h, o[h * rows : (h + 1) * rows], out)
    return out


def softmax_keys(s, allowed):
    if allowed is not None:
        s = jnp.where(allowed, s, -1e30)
    p = jnp.exp2(s - jnp.max(s, axis=0, keepdims=True))
    return p * (1.0 / jnp.sum(p, axis=0, keepdims=True))


def half_attend(half, halo_ref, frame_ref, inside_ref, side_ref, qkv_ref, bias_ref, outside, normed):
    ids = frame_ref[...]
    own = jnp.where(half == 0, ids, pltpu.roll(ids, 4, 0))
    halo = jnp.where(outside, -1.0, halo_ref[224:240, 0:128].astype(F32)[0:8])
    frame = jnp.concatenate([own[0:4], halo[0:4], jnp.zeros((120, 128), F32)], axis=0)
    turned = frame.T
    lane = lax.broadcasted_iota(jnp.int32, (FRAME, 128), 1).astype(F32)
    hot = []
    for r in range(8):
        col = jnp.broadcast_to(turned[0:FRAME, r : r + 1], (FRAME, 128))
        hot.append(jnp.where(col == lane, 1.0, 0.0))

    def tile_of(rows, j):
        return jnp.concatenate([x[8 * j : 8 * j + 8] for x in rows], axis=0)

    for r in range(0, 4, 2):
        x = layer_norm(halo_ref[r * FRAME : (r + 2) * FRAME, :].astype(F32))
        pair = [x[k * FRAME : (k + 1) * FRAME].reshape(TILES, 8, D1) for k in range(2)]
        normed[:, r // 2] = jnp.concatenate(pair, axis=1).astype(BF)
    halo_kv = jnp.dot(
        normed[...].reshape(TILES * 32, D1), qkv_ref[:, D1:], preferred_element_type=F32
    ).astype(BF)

    scale = LOG2E / math.sqrt(32)
    units = [(j, g) for j in range(TILES) for g in range(4)]

    def own_part(j, block, g):
        lanes = slice(block * D1 + g * 128, block * D1 + g * 128 + 128)
        if 0 < j < TILES - 1:
            return inside_ref[half, j - 1, :, lanes]
        return side_ref[half, j // (TILES - 1), :, lanes]

    def both(j, block, g):
        lanes = slice((block - 1) * D1 + g * 128, (block - 1) * D1 + g * 128 + 128)
        return jnp.concatenate([own_part(j, block, g), halo_kv[32 * j : 32 * j + 32, lanes]], axis=0)

    allowed = []
    for j in range(TILES):
        keys_hot = tile_of(hot, j).astype(BF)
        queries_hot = jnp.concatenate([keys_hot[0:32]] * 4, axis=0)
        allowed.append(lax.dot_general(keys_hot, queries_hot, NT, preferred_element_type=F32) > 0.5)
    scores = [
        lax.dot_general(
            both(j, 1, g), masked_heads(own_part(j, 0, g), 32, 4), NT, preferred_element_type=F32
        )
        for j, g in units
    ]
    probs = [
        softmax_keys(s * scale + bias_ref[half, g], allowed[j]).astype(BF)
        for s, (j, g) in zip(scores, units)
    ]
    outs = [
        lax.dot_general(p, both(j, 2, g), TN, preferred_element_type=F32)
        for p, (j, g) in zip(probs, units)
    ]
    picked = [pick_heads(o, 32, 4).astype(BF) for o in outs]
    return jnp.concatenate(
        [jnp.concatenate(picked[4 * j : 4 * j + 4], axis=1) for j in range(TILES)], axis=0
    )


def half_finish(half, attended, tok_ref, out_ref):
    y = jnp.dot(attended, out_ref[...], preferred_element_type=F32)
    rows = []
    for r in range(4):
        tiles = [y[32 * j + 8 * r : 32 * j + 8 * r + 8] for j in range(TILES)]
        add = jnp.concatenate(tiles, axis=0)[4 : 4 + COLS]
        rows.append((tok_ref[4 * half + r].astype(F32) + add).astype(BF))
    return rows


def pair_kernel(
    halo_ref, frame_ref, inside_ref, side_ref, qkv_ref, bias_ref, tok_ref, out_ref, rows_out, normed
):
    half = 1 - lat_parity()
    attended = half_attend(
        half, halo_ref, frame_ref, inside_ref, side_ref, qkv_ref, bias_ref, False, normed
    )
    for r, row in enumerate(half_finish(half, attended, tok_ref, out_ref)):
        rows_out[r] = row


def cross_kernel(
    halo_ref, frame_ref, inside_ref, side_ref, qkv_ref, bias_ref, tok_ref, out_ref, rows_ref,
    merge_ref, two_ref,
    one_out, merged_out, query_out, kv_out,
    normed, level, parts,
):
    lat = lax.axis_index("lat")
    half = lat_parity()
    outside = (lat == 0) | (lat == lax.axis_size("lat") - 1)
    attended = half_attend(
        half, halo_ref, frame_ref, inside_ref, side_ref, qkv_ref, bias_ref, outside, normed
    )

    def put(row, value):
        one_out[row] = value
        for n in range(4):
            level[n, row] = value[:, n * 128 : n * 128 + 128].astype(F32)

    for r in range(4):
        put(4 * (1 - half) + r, rows_ref[r])
    for r, row in enumerate(half_finish(half, attended, tok_ref, out_ref)):
        put(4 * half + r, row)

    for i in range(4):
        quartet = [
            jnp.concatenate(
                [level[n, 2 * i + dr, pl.ds(dc, COLS // 2, 2), :] for n in range(4)], axis=1
            )
            for dc in range(2)
            for dr in range(2)
        ]
        total = sum(jnp.sum(x, axis=-1, keepdims=True) for x in quartet)
        quartet = [x - total * (1.0 / (4 * D1)) for x in quartet]
        total = sum(jnp.sum(x * x, axis=-1, keepdims=True) for x in quartet)
        factor = lax.rsqrt(total * (1.0 / (4 * D1)) + EPSILON)
        for n in range(4):
            parts[n, :, i] = (quartet[n] * factor).reshape(3, 8, D1)
    merged = jnp.zeros((96, D2), F32)
    for n in range(4):
        merged += jnp.dot(
            parts[n].reshape(96, D1).astype(BF),
            merge_ref[n * D1 : (n + 1) * D1, :],
            preferred_element_type=F32,
        )
    merged = merged.astype(BF)
    merged_out[...] = merged
    x = layer_norm(merged.astype(F32)).astype(BF)
    kv_out[...] = jnp.dot(x, two_ref[:, 512:], preferred_element_type=F32).astype(BF)
    query_out[...] = jnp.dot(x, two_ref[:, :512], preferred_element_type=F32).astype(BF)


def level_two_kernel(
    query_ref, kv_ref, other_ref, merged_ref, bias_ref, out_ref, two_out, keys, result
):
    parity = lat_parity()
    mine = pl.multiple_of(parity * 32, 32)
    theirs = pl.multiple_of(32 - parity * 32, 32)
    scale = LOG2E / math.sqrt(64)
    for w in range(3):
        keys[w, pl.ds(mine, 32), :] = kv_ref[w * 32 : w * 32 + 32, :]
        keys[w, pl.ds(theirs, 32), :] = other_ref[w * 32 : w * 32 + 32, :]
    units = [(w, g) for w in range(3) for g in range(2)]
    scores = [
        lax.dot_general(
            keys[w, :, g * 256 : g * 256 + 256],
            masked_heads(query_ref[w * 32 : w * 32 + 32, g * 256 : g * 256 + 256], 64, 4),
            NT,
            preferred_element_type=F32,
        )
        for w, g in units
    ]
    probs = [
        softmax_keys(s * scale + bias_ref[g], None).astype(BF) for s, (w, g) in zip(scores, units)
    ]
    outs = [
        lax.dot_general(
            p, keys[w, :, 512 + g * 256 : 768 + g * 256], TN, preferred_element_type=F32
        )
        for p, (w, g) in zip(probs, units)
    ]
    picked = [pick_heads(o, 64, 4).astype(BF) for o in outs]
    attended = jnp.concatenate(
        [jnp.concatenate(picked[2 * w : 2 * w + 2], axis=1) for w in range(3)], axis=0
    )
    add = jnp.dot(attended, out_ref[...], preferred_element_type=F32)
    result[...] = (merged_ref[...].astype(F32) + add).reshape(3, 4, 8, D2)
    for i in range(4):
        two_out[i] = result[:, i].reshape(24, D2).astype(BF)


def call(kernel, outs, args, hbm=0, scratch=(), mib=16):
    shapes = [jax.ShapeDtypeStruct(s, d) for s, d in outs]
    place = [pl.BlockSpec(memory_space=pltpu.HBM)] * hbm
    place += [pl.BlockSpec(memory_space=pltpu.VMEM)] * (len(args) - hbm)
    args = [
        pltpu.with_memory_space_constraint(x, pltpu.HBM) if n < hbm else x
        for n, x in enumerate(args)
    ]
    return pl.pallas_call(
        kernel,
        out_shape=shapes,
        in_specs=place,
        out_specs=[pl.BlockSpec(memory_space=pltpu.VMEM)] * len(outs),
        scratch_shapes=list(scratch),
        compiler_params=pltpu.CompilerParams(vmem_limit_bytes=mib * MIB),
        cost_estimate=pl.CostEstimate(flops=1000, bytes_accessed=1000, transcendentals=0),
        name=kernel.__name__,
    )(*args)


def on_device(
    tokens, region_ids, bias_one, qkv_one, out_one, merge_proj, bias_two, qkv_two, out_two
):
    lats, lons = lax.axis_size("lat"), lax.axis_size("lon")
    lat_inner = [(i, i ^ 1) for i in range(lats)]
    lat_outer = [(i, (i + (1 if i % 2 else -1)) % lats) for i in range(lats)]
    lon_inner = [(i, i ^ 1) for i in range(lons)]
    lon_outer = [(i, (i + (1 if i % 2 else -1)) % lons) for i in range(lons)]

    inner, outer, tokens, region_ids = call(
        edge_kernel,
        [((48, D1), BF)] * 2 + [((ROWS, COLS, D1), BF), ((ROWS, COLS), jnp.int32)],
        [tokens, region_ids],
        hbm=2,
        scratch=[pltpu.SemaphoreType.DMA((4,))],
        mib=4,
    )
    inner = lax.ppermute(inner, "lon", lon_inner)
    outer = lax.ppermute(outer, "lon", lon_outer)
    inside, table_one, table_two, qkv_one, out_one, qkv_two = call(
        own_kernel,
        [
            ((2, INSIDE, 32, 3 * D1), BF), ((2, 4, 64, 128), F32), ((2, 64, 128), F32),
            (qkv_one.shape, BF), (out_one.shape, BF), (qkv_two.shape, BF),
        ],
        [qkv_one, bias_one, bias_two, out_one, qkv_two, tokens],
        hbm=5,
        scratch=[
            pltpu.VMEM((2, INSIDE, 2, 16, D1), BF),
            pltpu.VMEM(bias_one.shape, F32),
            pltpu.VMEM(bias_two.shape, F32),
            pltpu.SemaphoreType.DMA((5,)),
        ],
    )
    cross, pair, frame = call(
        band_kernel,
        [((240, D1), BF), ((240, D1), BF), ((ROWS, 128), F32)],
        [tokens, region_ids, inner, outer, table_two],
        mib=8,
    )
    cross = lax.ppermute(cross, "lat", lat_outer)
    pair = lax.ppermute(pair, "lat", lat_inner)
    side, merge_proj, out_two = call(
        side_kernel,
        [((2, 2, 32, 3 * D1), BF), (merge_proj.shape, BF), (out_two.shape, BF)],
        [merge_proj, out_two, tokens, inner, outer, qkv_one, frame],
        hbm=2,
        scratch=[pltpu.SemaphoreType.DMA((2,))],
        mib=8,
    )
    normed = pltpu.VMEM((TILES, 2, 16, D1), BF)
    (pair_rows,) = call(
        pair_kernel,
        [((4, COLS, D1), BF)],
        [pair, frame, inside, side, qkv_one, table_one, tokens, out_one],
        scratch=[normed],
    )
    level_one, merged, query, kv = call(
        cross_kernel,
        [((ROWS, COLS, D1), BF), ((96, D2), BF), ((96, 512), BF), ((96, 1024), BF)],
        [
            cross, frame, inside, side, qkv_one, table_one, tokens, out_one, pair_rows,
            merge_proj, qkv_two,
        ],
        scratch=[
            normed,
            pltpu.VMEM((4, ROWS, COLS, 128), F32),
            pltpu.VMEM((4, 3, 4, 8, D1), F32),
        ],
    )
    other = lax.ppermute(kv, "lat", lat_inner)
    (level_two,) = call(
        level_two_kernel,
        [((4, 24, D2), BF)],
        [query, kv, other, merged, table_two, out_two],
        scratch=[pltpu.VMEM((3, 64, 1024), BF), pltpu.VMEM((3, 4, 8, D2), F32)],
    )
    return (level_one, level_two)


def solution(mesh):
    placed = (P("lat", "lon", None), P("lat", "lon"), P(), P(), P(), P(), P(), P(), P())
    return jax.shard_map(
        on_device,
        mesh=mesh,
        in_specs=placed,
        out_specs=(P("lat", "lon", None), P("lat", "lon", None)),
        check_vma=False,
    )
```

time: 47.3 us -> 30.8 us (0.65); the launches traced: 46.5 us -> 30.7 us
  Pallas kernels: 22.1 us -> 14.3 us
  local copies, waits for them, and re-layouts: 5.09 us -> 0 us
  waiting for transfers between devices: 4 us -> 1.35 us
    pallas_call x5 -> x7, Pallas kernels: 22.1 us -> 14.3 us  [call(): pl.pallas_call(kernel, out_shape=shapes, in_specs=place, out_specs=[pl.Bl...]
    unnamed x20 -> x0, local copies, waits for them, and re-layouts: 5.09 us -> none
    ppermute x5, waiting for transfers between devices: 4 us -> 1.35 us  [the longest x1 1.07 us: on_device(): other = lax.ppermute(kv, 'lat', lat_inner)]
  transfers between devices with their start and end apart: 5 -> 5, of which waited for: 3 -> 2; matrix products, arithmetic and copies ran while one was open for 0% -> 0% of each run, Pallas kernels for 0% -> 23%
where the time goes in v1:
time: 30.8 us; the launch traced here: 30.7 us
  Pallas kernels  14.3 us (46%)
  starting transfers between devices  14.3 us (46%)
  waiting for transfers between devices  1.35 us (4%)
  between operations  0.69 us (2%)
    pallas_call x7, Pallas kernels, call(): pl.pallas_call(kernel, out_shape=shapes, in_specs=place, out_specs=[pl.Bl...  14.3 us
    ppermute x1, starting transfers between devices, on_device(): outer = lax.ppermute(outer, 'lon', lon_outer)  5.52 us
    ppermute x1, starting transfers between devices, on_device(): inner = lax.ppermute(inner, 'lon', lon_inner)  3.66 us
    ppermute x1, starting transfers between devices, on_device(): other = lax.ppermute(kv, 'lat', lat_inner)  2.52 us
    ppermute x1, starting transfers between devices, on_device(): pair = lax.ppermute(pair, 'lat', lat_inner)  1.32 us
    ppermute x1, starting transfers between devices, on_device(): cross = lax.ppermute(cross, 'lat', lat_outer)  1.28 us
    ppermute x1, waiting for transfers between devices, on_device(): other = lax.ppermute(kv, 'lat', lat_inner)  1.07 us
  transfers between devices with their start and end apart: 5, of which 2 were waited for; matrix products, arithmetic and copies ran while one was open for 0% of the time, Pallas kernels for 23%

profile of v1, /device:TPU:1, one launch (start us, length us, event | category | flops | bytes accessed | tf_op | source)
XLA Modules:
  0.0 30.7 jit_solution(5481918299792370670)
XLA Ops:
  0.6 1.1 %edge_kernel.1 = (bf16[48,512]{1,0:T(8,128)(2,1)S(1)}, bf16[48,512]{1,0:T(8,128)(2,1)S(1)}, bf16[8,48,512]{2,1,0:T(8,128)(2,1)S(1)}, s32[8,48]{1,0:T(8,128)S(1)}) custom-call(bf16[8,48,512]{2,1,0:T(8,128)(2,1)} %tok_hbm.1, s32[8,48]{1,0:T(8,128)} %ids_hbm.1), custom_call_target="tpu_custom_call" | custom-call | flops 1000 | bytes 1000 | tf_op jit(solution)/shard_map/edge_kernel/pallas_call | solution.py:373
  1.7 3.7 %collective-permute-start = (bf16[48,512]{1,0:T(8,128)(2,1)S(1)}, bf16[48,512]{1,0:T(8,128)(2,1)S(1)}, u32[]{:S(2)}, u32[]{:S(2)}) collective-permute-start(bf16[48,512]{1,0:T(8,128)(2,1)S(1)} %get-tuple-element.24), channel_id=1, source_target_pairs={{0,1},{1,0},{2,3},{3,2},{4,5},{5,4},{6,7},{7,6},{8,9},{9,8},{10,11... | collective-permute-start | bytes 147464 | tf_op jit(solution)/shard_map/ppermute | solution.py:402
  5.4 5.5 %collective-permute-start.1 = (bf16[48,512]{1,0:T(8,128)(2,1)S(1)}, bf16[48,512]{1,0:T(8,128)(2,1)S(1)}, u32[]{:S(2)}, u32[]{:S(2)}) collective-permute-start(bf16[48,512]{1,0:T(8,128)(2,1)S(1)} %get-tuple-element.25), channel_id=1, source_target_pairs={{0,15},{1,2},{2,1},{3,4},{4,3},{5,6},{6,5},{7,8},{8,7},{9,10},{10,... | collective-permute-start | bytes 147464 | tf_op jit(solution)/shard_map/ppermute | solution.py:403
  10.9 2.9 %own_kernel.1 = (bf16[2,5,32,1536]{3,2,1,0:T(8,128)(2,1)S(1)}, f32[2,4,64,128]{3,2,1,0:T(8,128)S(1)}, f32[2,64,128]{2,1,0:T(8,128)S(1)}, bf16[512,1536]{1,0:T(8,...) custom-call(bf16[512,1536]{1,0:T(8,128)(2,1)} %qkv_hbm.1, f32[16,64,64]{2,1,0:T(8,128)} %one_hbm.1, ...), custom_call_target="tpu_custom_call" | custom-call | flops 1000 | bytes 1000 | tf_op jit(solution)/shard_map/own_kernel/pallas_call | solution.py:373
  13.8 0.0 collective-permute-done.inner_ref
  13.8 0.0 collective-permute-done.1.outer_ref
  13.8 0.2 band_kernel.1
  14.0 1.3 %collective-permute-start.3 = (bf16[240,512]{1,0:T(8,128)(2,1)S(1)}, bf16[240,512]{1,0:T(8,128)(2,1)S(1)}, u32[]{:S(2)}, u32[]{:S(2)}) collective-permute-start(bf16[240,512]{1,0:T(8,128)(2,1)S(1)} %get-tuple-element.34), channel_id=1, source_target_pairs={{0,16},{16,0},{32,48},{48,32},{64,80},{80,64},{96,112},{112,96},{1... | collective-permute-start | bytes 737288 | tf_op jit(solution)/shard_map/ppermute | solution.py:426
  15.3 1.3 %collective-permute-start.2 = (bf16[240,512]{1,0:T(8,128)(2,1)S(1)}, bf16[240,512]{1,0:T(8,128)(2,1)S(1)}, u32[]{:S(2)}, u32[]{:S(2)}) collective-permute-start(bf16[240,512]{1,0:T(8,128)(2,1)S(1)} %get-tuple-element.27), channel_id=1, source_target_pairs={{0,240},{16,32},{32,16},{48,64},{64,48},{80,96},{96,80},{112,128},... | collective-permute-start | bytes 737288 | tf_op jit(solution)/shard_map/ppermute | solution.py:425
  16.6 2.5 %side_kernel.1 = (bf16[2,2,32,1536]{3,2,1,0:T(8,128)(2,1)S(1)}, bf16[2048,1024]{1,0:T(8,128)(2,1)S(1)}, bf16[512,1024]{1,0:T(8,128)(2,1)S(1)}) custom-call(bf16[2048,1024]{1,0:T(8,128)(2,1)} %merge_hbm.1, bf16[512,1024]{1,0:T(8,128)(2,1)} %last_hbm.1, bf16[8,48,512]{2,1,0:T(8,128)(2,1)S(1)} %get-tuple-element.22.tok_ref, ...), custom_call_target="tpu_custom_call" | custom-call | flops 1000 | bytes 1000 | tf_op jit(solution)/shard_map/side_kernel/pallas_call | solution.py:373
  19.1 0.0 collective-permute-done.3.halo_ref
  19.1 1.8 %pair_kernel.1.rows_ref = bf16[4,48,512]{2,1,0:T(8,128)(2,1)S(1)} custom-call(bf16[240,512]{1,0:T(8,128)(2,1)S(1)} %collective-permute-done.3.halo_ref, f32[8,128]{1,0:T(8,128)S(1)} %get-tuple-element.28.after_ref.frame_ref, bf16[2,5,32,1536]{3,2,1,0:T(8,128)(2,1)S(1)} %get-tuple-element.29.inside_ref, ...), custom_call_target="tpu_custom_call" | custom-call | flops 1000 | bytes 1000 | tf_op jit(solution)/shard_map/pair_kernel/pallas_call | solution.py:373
  21.0 0.3 collective-permute-done.2.halo_ref
  21.3 4.3 %cross_kernel.1 = (bf16[8,48,512]{2,1,0:T(8,128)(2,1)}, bf16[96,1024]{1,0:T(8,128)(2,1)S(1)}, bf16[96,512]{1,0:T(8,128)(2,1)S(1)}, bf16[96,1024]{1,0:T(8,128)(2,1)S(1)}) custom-call(bf16[240,512]{1,0:T(8,128)(2,1)S(1)} %collective-permute-done.2.halo_ref, f32[8,128]{1,0:T(8,128)S(1)} %get-tuple-element.28.after_ref.frame_ref, ...), custom_call_target="tpu_custom_call" | custom-call | flops 1000 | bytes 1000 | tf_op jit(solution)/shard_map/cross_kernel/pallas_call | solution.py:373
  25.6 2.5 %collective-permute-start.4 = (bf16[96,1024]{1,0:T(8,128)(2,1)S(1)}, bf16[96,1024]{1,0:T(8,128)(2,1)S(1)}, u32[]{:S(2)}, u32[]{:S(2)}) collective-permute-start(bf16[96,1024]{1,0:T(8,128)(2,1)S(1)} %get-tuple-element.39.kv_ref), channel_id=1, source_target_pairs={{0,16},{16,0},{32,48},{48,32},{64,80},{80,64},{96,112},{112,96},{1... | collective-permute-start | bytes 589832 | tf_op jit(solution)/shard_map/ppermute | solution.py:455
  28.1 1.1 %collective-permute-done.4.other_ref = bf16[96,1024]{1,0:T(8,128)(2,1)S(1)} collective-permute-done((bf16[96,1024]{1,0:T(8,128)(2,1)S(1)}, bf16[96,1024]{1,0:T(8,128)(2,1)S(1)}, u32[]{:S(2)}, u32[]{:S(2)}) %collective-permute-start.4) | collective-permute-done | bytes 196640 | tf_op jit(solution)/shard_map/ppermute | solution.py:455
  29.2 1.5 %level_two_kernel.1 = bf16[4,24,1024]{2,1,0:T(8,128)(2,1)} custom-call(bf16[96,512]{1,0:T(8,128)(2,1)S(1)} %get-tuple-element.38.query_ref, bf16[96,1024]{1,0:T(8,128)(2,1)S(1)} %get-tuple-element.39.kv_ref, bf16[96,1024]{1,0:T(8,128)(2,1)S(1)} %collective-permute-done.4.other_ref, bf16[96,1024]{1,0:T(8,128)(2,1)S(1)} %get-tuple-element.40.merged_ref, ...), custom_call_target="tpu_custom_call" | custom-call | flops 1000 | bytes 1000 | tf_op jit(solution)/shard_map/level_two_kernel/pallas_call | solution.py:373
Async XLA Ops:
  1.7 12.1 %collective-permute-start = (bf16[48,512]{1,0:T(8,128)(2,1)S(1)}, bf16[48,512]{1,0:T(8,128)(2,1)S(1)}, u32[]{:S(2)}, u32[]{:S(2)}) collective-permute-start(bf16[48,512]{1,0:T(8,128)(2,1)S(1)} %get-tuple-element.24), channel_id=1, source_target_pairs={{0,1},{1,0},{2,3},{3,2},{4,5},{5,4},{6,7},{7,6},{8,9},{9,8},{10,11... | collective-permute-start | bytes 147464 | tf_op jit(solution)/shard_map/ppermute | solution.py:402
  5.4 8.4 %collective-permute-start.1 = (bf16[48,512]{1,0:T(8,128)(2,1)S(1)}, bf16[48,512]{1,0:T(8,128)(2,1)S(1)}, u32[]{:S(2)}, u32[]{:S(2)}) collective-permute-start(bf16[48,512]{1,0:T(8,128)(2,1)S(1)} %get-tuple-element.25), channel_id=1, source_target_pairs={{0,15},{1,2},{2,1},{3,4},{4,3},{5,6},{6,5},{7,8},{8,7},{9,10},{10,... | collective-permute-start | bytes 147464 | tf_op jit(solution)/shard_map/ppermute | solution.py:403
  14.0 5.1 %collective-permute-start.3 = (bf16[240,512]{1,0:T(8,128)(2,1)S(1)}, bf16[240,512]{1,0:T(8,128)(2,1)S(1)}, u32[]{:S(2)}, u32[]{:S(2)}) collective-permute-start(bf16[240,512]{1,0:T(8,128)(2,1)S(1)} %get-tuple-element.34), channel_id=1, source_target_pairs={{0,16},{16,0},{32,48},{48,32},{64,80},{80,64},{96,112},{112,96},{1... | collective-permute-start | bytes 737288 | tf_op jit(solution)/shard_map/ppermute | solution.py:426
  15.3 5.9 %collective-permute-start.2 = (bf16[240,512]{1,0:T(8,128)(2,1)S(1)}, bf16[240,512]{1,0:T(8,128)(2,1)S(1)}, u32[]{:S(2)}, u32[]{:S(2)}) collective-permute-start(bf16[240,512]{1,0:T(8,128)(2,1)S(1)} %get-tuple-element.27), channel_id=1, source_target_pairs={{0,240},{16,32},{32,16},{48,64},{64,48},{80,96},{96,80},{112,128},... | collective-permute-start | bytes 737288 | tf_op jit(solution)/shard_map/ppermute | solution.py:425
  25.6 3.6 %collective-permute-start.4 = (bf16[96,1024]{1,0:T(8,128)(2,1)S(1)}, bf16[96,1024]{1,0:T(8,128)(2,1)S(1)}, u32[]{:S(2)}, u32[]{:S(2)}) collective-permute-start(bf16[96,1024]{1,0:T(8,128)(2,1)S(1)} %get-tuple-element.39.kv_ref), channel_id=1, source_target_pairs={{0,16},{16,0},{32,48},{48,32},{64,80},{80,64},{96,112},{112,96},{1... | collective-permute-start | bytes 589832 | tf_op jit(solution)/shard_map/ppermute | solution.py:455

commit v2 on v1

v2 whole, which is shorter than its diff:
```python
import math

import jax
import jax.numpy as jnp
from jax import lax
from jax.experimental import pallas as pl
from jax.experimental.pallas import tpu as pltpu
from jax.sharding import PartitionSpec as P

EPSILON = 1e-05
LOG2E = math.log2(math.e)
BF = jnp.bfloat16
F32 = jnp.float32
ROWS = 8
COLS = 48
TILES = 7
INSIDE = 5
FRAME = 56
D1 = 512
D2 = 1024
MIB = 1024 * 1024

NT = (((1,), (1,)), ((), ()))
TN = (((0,), (0,)), ((), ()))


def layer_norm(x):
    width = x.shape[-1]
    mean = jnp.sum(x, axis=-1, keepdims=True) * (1.0 / width)
    c = x - mean
    var = jnp.sum(c * c, axis=-1, keepdims=True) * (1.0 / width)
    return c * lax.rsqrt(var + EPSILON)


def lanes_to(x, width):
    return jnp.concatenate([x, jnp.zeros((x.shape[0], width - x.shape[1]), x.dtype)], axis=1)


def lat_parity():
    return lax.rem(lax.axis_index("lat"), 2)


def lon_parity():
    return lax.rem(lax.axis_index("lon"), 2)


def start_all(pairs, sems):
    copies = [pltpu.make_async_copy(src, dst, sems.at[n]) for n, (src, dst) in enumerate(pairs)]
    for copy in copies:
        copy.start()
    return copies


def load_kernel(tok_hbm, ids_hbm, cross_ref, tok_ref, ids_ref, sems):
    for copy in start_all([(ids_hbm, ids_ref), (tok_hbm, tok_ref)], sems):
        copy.wait()
    for r in range(4):
        cross_ref[r * COLS : (r + 1) * COLS] = tok_ref[4 * lat_parity() + r]
    ids = lanes_to(ids_ref[...].astype(F32), D1)
    cross_ref[4 * COLS :] = jnp.where(lat_parity() == 0, ids, pltpu.roll(ids, 4, 0)).astype(BF)


def next_row(r):
    return 4 * lat_parity() + r


def edge_kernel(
    tok_ref, ids_ref, pair_ref, pair_ids_ref, cross_ref, after_ref, inner_ref, outer_ref, all_ids_ref
):
    first = [tok_ref[r, 0:16].astype(F32)[0:4] for r in range(ROWS)]
    first += [pair_ref[next_row(r), 0:16].astype(F32)[0:4] for r in range(4)]
    first += [cross_ref[COLS * r : COLS * r + 16].astype(F32)[0:4] for r in range(4)]
    last = [tok_ref[r, 32:48].astype(F32)[12:16] for r in range(ROWS)]
    last += [pair_ref[next_row(r), 32:48].astype(F32)[12:16] for r in range(4)]
    last += [cross_ref[COLS * r + 32 : COLS * r + 48].astype(F32)[12:16] for r in range(4)]
    own = lanes_to(ids_ref[...].astype(F32), 128)
    pair = lanes_to(pair_ids_ref[...].astype(F32), 128)
    pair = jnp.where(lat_parity() == 0, pair, pltpu.roll(pair, 4, 0))
    cross = cross_ref[4 * COLS :, 0:128].astype(F32)
    halo = jnp.concatenate([pair[0:4], cross[0:4]], axis=0)
    all_ids_ref[...] = jnp.concatenate([own, halo], axis=0)
    ids = jnp.concatenate([own, halo], axis=1)
    first = jnp.concatenate(first + [lanes_to(ids, D1)], axis=0).astype(BF)
    ids = pltpu.roll(ids, 256 - (COLS - 4), 1)
    last = jnp.concatenate(last + [lanes_to(ids, D1)], axis=0).astype(BF)
    even = lon_parity() == 0
    inner_ref[...] = jnp.where(even, last, first)
    outer_ref[...] = jnp.where(even, first, last)


def sides(inner_ref, outer_ref):
    inner, outer = inner_ref[...].astype(F32), outer_ref[...].astype(F32)
    even = lon_parity() == 0
    return jnp.where(even, outer, inner), jnp.where(even, inner, outer)


def own_kernel(qkv_ref, one_ref, two_ref, tok_ref, inside_out, one_out, two_out, normed):
    for r in range(0, ROWS, 2):
        pair = []
        for k in range(2):
            x = layer_norm(tok_ref[r + k].astype(F32))
            pair.append(x[4 : COLS - 4].reshape(INSIDE, 8, D1))
        normed[r // 4, :, (r % 4) // 2] = jnp.concatenate(pair, axis=1).astype(BF)
    for half in range(2):
        low = 32 * (1 - half)
        for g in range(4):
            turned = one_ref[4 * g : 4 * g + 4, low : low + 32, :].reshape(128, 64).T * LOG2E
            one_out[half, g, 0:32] = turned[low : low + 32]
            one_out[half, g, 32:64] = turned[32 - low : 64 - low]
    low = pl.multiple_of(lat_parity() * 32, 32)
    for g in range(2):
        turned = two_ref[4 * g : 4 * g + 4, pl.ds(low, 32), :].reshape(128, 64).T * LOG2E
        even = lat_parity() == 0
        two_out[g, 0:32] = jnp.where(even, turned[0:32], turned[32:64])
        two_out[g, 32:64] = jnp.where(even, turned[32:64], turned[0:32])
    x = normed[...].reshape(2 * INSIDE * 32, D1)
    inside_out[...] = (
        jnp.dot(x, qkv_ref[...], preferred_element_type=F32)
        .astype(BF)
        .reshape(2, INSIDE, 32, 3 * D1)
    )


def masked_heads(q, head_dim, count):
    lane = lax.broadcasted_iota(jnp.int32, q.shape, 1) // head_dim
    zero = jnp.zeros_like(q)
    return jnp.concatenate([jnp.where(lane == h, q, zero) for h in range(count)], axis=0)


def pick_heads(o, head_dim, count):
    rows = o.shape[0] // count
    lane = lax.broadcasted_iota(jnp.int32, (rows, o.shape[1]), 1) // head_dim
    out = o[0:rows]
    for h in range(1, count):
        out = jnp.where(lane == h, o[h * rows : (h + 1) * rows], out)
    return out


def softmax_keys(s, allowed):
    if allowed is not None:
        s = jnp.where(allowed, s, -1e30)
    p = jnp.exp2(s - jnp.max(s, axis=0, keepdims=True))
    return p * (1.0 / jnp.sum(p, axis=0, keepdims=True))


def region_masks(ids):
    lat = lax.axis_index("lat")
    outside = (lat == 0) | (lat == lax.axis_size("lat") - 1)
    pair = ids[8:12]
    cross = jnp.where(outside, -1.0, ids[12:16])
    even = lat_parity() == 0
    above, below = jnp.where(even, cross, pair), jnp.where(even, pair, cross)
    rows = [ids[0:4], above, ids[4:8], below, jnp.zeros((112, 128), F32)]
    turned = jnp.concatenate(rows, axis=0).T

    def window(half, j):
        tiles = [
            jnp.broadcast_to(turned[8 * j : 8 * j + 8, r : r + 1], (8, 128))
            for r in range(8 * half, 8 * half + 8)
        ]
        queries = jnp.concatenate(tiles[0:4] * 4, axis=0).T[0:1]
        return jnp.concatenate(tiles, axis=0) == queries

    return window


def attend_one(windows, mask, bias_ref, query, keys, values):
    scale = LOG2E / math.sqrt(32)
    units = [(w, g) for w in range(len(windows)) for g in range(4)]
    allowed = [mask(half, j) for half, j in windows]
    scores = [
        lax.dot_general(
            keys(w, g), masked_heads(query(w, g), 32, 4), NT, preferred_element_type=F32
        )
        for w, g in units
    ]
    probs = [
        softmax_keys(s * scale + bias_ref[windows[w][0], g], allowed[w]).astype(BF)
        for s, (w, g) in zip(scores, units)
    ]
    outs = [
        lax.dot_general(p, values(w, g), TN, preferred_element_type=F32)
        for p, (w, g) in zip(probs, units)
    ]
    picked = [pick_heads(o, 32, 4).astype(BF) for o in outs]
    return [jnp.concatenate(picked[4 * w : 4 * w + 4], axis=1) for w in range(len(windows))]


def lanes_of(block, g):
    return slice(block * D1 + g * 128, block * D1 + g * 128 + 128)


def inner_kernel(
    pair_ref, cross_ref, ids_ref, inside_ref, qkv_ref, bias_ref, out_ref, add_out, normed
):
    even = lat_parity() == 0
    for half in range(2):
        for r in range(0, 4, 2):
            rows = []
            for k in range(r, r + 2):
                pair = pair_ref[next_row(k)].astype(F32)
                cross = cross_ref[COLS * k : COLS * k + COLS].astype(F32)
                x = jnp.where(even, cross, pair) if half == 0 else jnp.where(even, pair, cross)
                rows.append(layer_norm(x)[4 : COLS - 4].reshape(INSIDE, 8, D1))
            normed[half, :, r // 2] = jnp.concatenate(rows, axis=1).astype(BF)
    halo = jnp.dot(
        normed[...].reshape(2 * INSIDE * 32, D1), qkv_ref[:, D1:], preferred_element_type=F32
    ).astype(BF)
    windows = [(half, j) for half in range(2) for j in range(1, TILES - 1)]

    def both(w, block, g):
        half, j = windows[w]
        own = inside_ref[half, j - 1, :, lanes_of(block, g)]
        return jnp.concatenate([own, halo[32 * w : 32 * w + 32, lanes_of(block - 1, g)]], axis=0)

    attended = attend_one(
        windows,
        region_masks(pltpu.roll(ids_ref[...], 4, 1)),
        bias_ref,
        lambda w, g: inside_ref[windows[w][0], windows[w][1] - 1, :, lanes_of(0, g)],
        lambda w, g: both(w, 1, g),
        lambda w, g: both(w, 2, g),
    )
    add_out[...] = jnp.dot(
        jnp.concatenate(attended, axis=0), out_ref[...], preferred_element_type=F32
    )


def final_kernel(
    tok_ref, pair_ref, cross_ref, inner_ref, outer_ref, ids_ref, qkv_ref, bias_ref, out_ref,
    add_ref, merge_ref, two_ref,
    one_out, merged_out, normed_out, kv_out,
    level, parts,
):
    even = lat_parity() == 0
    west, east = sides(inner_ref, outer_ref)
    lane = lax.broadcasted_iota(jnp.int32, (2 * ROWS, 128), 1)
    own = pltpu.roll(ids_ref[...], 4, 1)
    near = jnp.concatenate([west[64:72, 0:128], west[64:72, 128:256]], axis=0)
    far = jnp.concatenate([east[64:72, 0:128], east[64:72, 128:256]], axis=0)
    far = pltpu.roll(far, COLS + 4, 1)
    ids = jnp.where(lane < 4, near, jnp.where(lane < COLS + 4, own, far))

    first = [tok_ref[r, 0:16].astype(F32)[0:4] for r in range(ROWS)]
    first += [pair_ref[next_row(r), 0:16].astype(F32)[0:4] for r in range(4)]
    first += [cross_ref[COLS * r : COLS * r + 16].astype(F32)[0:4] for r in range(4)]
    last = [tok_ref[r, 32:48].astype(F32)[12:16] for r in range(ROWS)]
    last += [pair_ref[next_row(r), 32:48].astype(F32)[12:16] for r in range(4)]
    last += [cross_ref[COLS * r + 32 : COLS * r + 48].astype(F32)[12:16] for r in range(4)]
    tiles = []
    for side in range(2):
        rows = []
        for r in range(2 * ROWS):
            if side == 0:
                rows += [west[4 * r : 4 * r + 4], first[r]]
            else:
                rows += [last[r], east[4 * r : 4 * r + 4]]
        tiles.append(layer_norm(jnp.concatenate(rows, axis=0)))
    windows = [(half, j) for half in range(2) for j in (0, TILES - 1)]
    ordered = []
    for half, j in windows:
        x = tiles[j // (TILES - 1)]
        a, b = (x[96:128], x[64:96]) if half == 0 else (x[64:96], x[96:128])
        ordered += [x[32 * half : 32 * half + 32], jnp.where(even, a, b)]
    qkv = jnp.dot(
        jnp.concatenate(ordered, axis=0).astype(BF), qkv_ref[...], preferred_element_type=F32
    ).astype(BF)
    attended = attend_one(
        windows,
        region_masks(ids),
        bias_ref,
        lambda w, g: qkv[64 * w : 64 * w + 32, lanes_of(0, g)],
        lambda w, g: qkv[64 * w : 64 * w + 64, lanes_of(1, g)],
        lambda w, g: qkv[64 * w : 64 * w + 64, lanes_of(2, g)],
    )
    edge = jnp.dot(jnp.concatenate(attended, axis=0), out_ref[...], preferred_element_type=F32)
    for row in range(ROWS):
        half, r = row // 4, row % 4
        adds = [edge[64 * half + 8 * r : 64 * half + 8 * r + 8]]
        for j in range(INSIDE):
            at = 32 * (INSIDE * half + j) + 8 * r
            adds.append(add_ref[at : at + 8])
        adds.append(edge[64 * half + 32 + 8 * r : 64 * half + 40 + 8 * r])
        add = jnp.concatenate(adds, axis=0)[4 : 4 + COLS]
        value = (tok_ref[row].astype(F32) + add).astype(BF)
        one_out[row] = value
        for n in range(4):
            level[n, row] = value[:, n * 128 : n * 128 + 128].astype(F32)

    for i in range(4):
        quartet = [
            jnp.concatenate(
                [level[n, 2 * i + dr, pl.ds(dc, COLS // 2, 2), :] for n in range(4)], axis=1
            )
            for dc in range(2)
            for dr in range(2)
        ]
        total = sum(jnp.sum(x, axis=-1, keepdims=True) for x in quartet)
        quartet = [x - total * (1.0 / (4 * D1)) for x in quartet]
        total = sum(jnp.sum(x * x, axis=-1, keepdims=True) for x in quartet)
        factor = lax.rsqrt(total * (1.0 / (4 * D1)) + EPSILON)
        for n in range(4):
            parts[n, :, i] = (quartet[n] * factor).reshape(3, 8, D1)
    merged = jnp.zeros((96, D2), F32)
    for n in range(4):
        merged += jnp.dot(
            parts[n].reshape(96, D1).astype(BF),
            merge_ref[n * D1 : (n + 1) * D1, :],
            preferred_element_type=F32,
        )
    merged = merged.astype(BF)
    merged_out[...] = merged
    x = layer_norm(merged.astype(F32)).astype(BF)
    normed_out[...] = x
    kv_out[...] = jnp.dot(x, two_ref[:, 512:], preferred_element_type=F32).astype(BF)


TWO_UNITS = [(w, g) for w in range(3) for g in range(2)]


def scores_two(keys_ref, queries, bias):
    scale = LOG2E / math.sqrt(64)
    return [
        lax.dot_general(
            keys_ref[w * 32 : w * 32 + 32, g * 256 : g * 256 + 256],
            masked_heads(queries[w * 32 : w * 32 + 32, g * 256 : g * 256 + 256], 64, 4),
            NT,
            preferred_element_type=F32,
        )
        * scale
        + bias[g]
        for w, g in TWO_UNITS
    ]


def query_kernel(normed_ref, kv_ref, bias_ref, two_ref, query_out, score_out):
    q = jnp.dot(normed_ref[...], two_ref[:, :512], preferred_element_type=F32).astype(BF)
    query_out[...] = q
    for n, s in enumerate(scores_two(kv_ref, q, [bias_ref[g, 0:32] for g in range(2)])):
        score_out[n] = s


def level_two_kernel(
    query_ref, score_ref, kv_ref, other_ref, merged_ref, bias_ref, out_ref, two_out
):
    far = scores_two(other_ref, query_ref[...], [bias_ref[g, 32:64] for g in range(2)])
    probs = [
        softmax_keys(jnp.concatenate([score_ref[n], s], axis=0), None).astype(BF)
        for n, s in enumerate(far)
    ]
    outs = []
    for p, (w, g) in zip(probs, TWO_UNITS):
        block = (slice(w * 32, w * 32 + 32), slice(512 + g * 256, 768 + g * 256))
        values = jnp.concatenate([kv_ref[block], other_ref[block]], axis=0)
        outs.append(lax.dot_general(p, values, TN, preferred_element_type=F32))
    picked = [pick_heads(o, 64, 4).astype(BF) for o in outs]
    attended = jnp.concatenate(
        [jnp.concatenate(picked[2 * w : 2 * w + 2], axis=1) for w in range(3)], axis=0
    )
    y = merged_ref[...].astype(F32) + jnp.dot(
        attended, out_ref[...], preferred_element_type=F32
    )
    for i in range(4):
        tiles = [y[32 * w + 8 * i : 32 * w + 8 * i + 8] for w in range(3)]
        two_out[i] = jnp.concatenate(tiles, axis=0).astype(BF)


def call(kernel, outs, args, hbm=0, scratch=(), mib=16, us=1.0):
    shapes = [jax.ShapeDtypeStruct(s, d) for s, d in outs]
    place = [pl.BlockSpec(memory_space=pltpu.HBM)] * hbm
    place += [pl.BlockSpec(memory_space=pltpu.VMEM)] * (len(args) - hbm)
    args = [
        pltpu.with_memory_space_constraint(x, pltpu.HBM) if n < hbm else x
        for n, x in enumerate(args)
    ]
    return pl.pallas_call(
        kernel,
        out_shape=shapes,
        in_specs=place,
        out_specs=[pl.BlockSpec(memory_space=pltpu.VMEM)] * len(outs),
        scratch_shapes=list(scratch),
        compiler_params=pltpu.CompilerParams(vmem_limit_bytes=mib * MIB),
        cost_estimate=pl.CostEstimate(
            flops=int(us * 10**9), bytes_accessed=10**6, transcendentals=0
        ),
        name=kernel.__name__,
    )(*args)


def on_device(
    tokens, region_ids, bias_one, qkv_one, out_one, merge_proj, bias_two, qkv_two, out_two
):
    lats, lons = lax.axis_size("lat"), lax.axis_size("lon")
    lat_inner = [(i, i ^ 1) for i in range(lats)]
    lat_outer = [(i, (i + (1 if i % 2 else -1)) % lats) for i in range(lats)]
    lon_inner = [(i, i ^ 1) for i in range(lons)]
    lon_outer = [(i, (i + (1 if i % 2 else -1)) % lons) for i in range(lons)]

    pair = lax.ppermute(tokens, "lat", lat_inner)
    pair_ids = lax.ppermute(region_ids, "lat", lat_inner)
    cross, tokens, region_ids = call(
        load_kernel,
        [((200, D1), BF), ((ROWS, COLS, D1), BF), ((ROWS, COLS), jnp.int32)],
        [tokens, region_ids],
        hbm=2,
        scratch=[pltpu.SemaphoreType.DMA((2,))],
        mib=4,
        us=4.0,
    )
    cross = lax.ppermute(cross, "lat", lat_outer)
    inside, table_one, table_two = call(
        own_kernel,
        [((2, INSIDE, 32, 3 * D1), BF), ((2, 4, 64, 128), F32), ((2, 64, 128), F32)],
        [qkv_one, bias_one, bias_two, tokens],
        scratch=[pltpu.VMEM((2, INSIDE, 2, 16, D1), BF)],
        us=1.5,
    )
    inner, outer, ids = call(
        edge_kernel,
        [((72, D1), BF), ((72, D1), BF), ((2 * ROWS, 128), F32)],
        [tokens, region_ids, pair, pair_ids, cross, table_two],
        mib=4,
    )
    inner = lax.ppermute(inner, "lon", lon_inner)
    outer = lax.ppermute(outer, "lon", lon_outer)
    (added,) = call(
        inner_kernel,
        [((2 * INSIDE * 32, D1), F32)],
        [pair, cross, ids, inside, qkv_one, table_one, out_one],
        scratch=[pltpu.VMEM((2, INSIDE, 2, 16, D1), BF)],
        us=0.3,
    )
    level_one, merged, normed, kv = call(
        final_kernel,
        [((ROWS, COLS, D1), BF), ((96, D2), BF), ((96, D2), BF), ((96, 1024), BF)],
        [
            tokens, pair, cross, inner, outer, ids, qkv_one, table_one, out_one, added,
            merge_proj, qkv_two,
        ],
        scratch=[pltpu.VMEM((4, ROWS, COLS, 128), F32), pltpu.VMEM((4, 3, 4, 8, D1), F32)],
    )
    other_kv = lax.ppermute(kv, "lat", lat_inner)
    query, scores = call(
        query_kernel,
        [((96, 512), BF), ((6, 32, 128), F32)],
        [normed, kv, table_two, qkv_two],
    )
    (level_two,) = call(
        level_two_kernel,
        [((4, 24, D2), BF)],
        [query, scores, kv, other_kv, merged, table_two, out_two],
    )
    return (level_one, level_two)


def solution(mesh):
    placed = (P("lat", "lon", None), P("lat", "lon"), P(), P(), P(), P(), P(), P(), P())
    return jax.shard_map(
        on_device,
        mesh=mesh,
        in_specs=placed,
        out_specs=(P("lat", "lon", None), P("lat", "lon", None)),
        check_vma=False,
    )
```

time: 30.8 us -> 28.6 us (0.929)
  Pallas kernels: 14.3 us -> 9.93 us
  waiting for transfers between devices: 1.35 us -> 2.81 us
  starting transfers between devices: 14.3 us -> 15 us
    ppermute x2 -> x3, starting transfers between devices: 3.84 us -> 8.28 us  [the longest x1 3.33 us: on_device(): pair = lax.ppermute(tokens, 'lat', lat_inner)]
    pallas_call x7, Pallas kernels: 14.3 us -> 9.93 us  [call(): pl.pallas_call(kernel, out_shape=shapes, in_specs=place, out_specs=[pl.Bl...]
    ppermute x1, starting transfers between devices: 3.66 us -> 1.09 us  [on_device(): inner = lax.ppermute(inner, 'lon', lon_inner)]
    ppermute x1, waiting for transfers between devices: 0.27 us -> 2.22 us  [on_device(): cross = lax.ppermute(cross, 'lat', lat_outer)]
    ppermute x1, starting transfers between devices: 1.28 us -> 0.09 us  [on_device(): cross = lax.ppermute(cross, 'lat', lat_outer)]
    ppermute x2 -> x3, waiting for transfers between devices: 1.07 us -> 0.59 us  [the longest x1 0.58 us: on_device(): other_kv = lax.ppermute(kv, 'lat', lat_inner)]
  transfers between devices with their start and end apart: 5 -> 6, of which waited for: 2 -> 2; matrix products, arithmetic and copies ran while one was open for 0% -> 0% of each run, Pallas kernels for 23% -> 16%
where the time goes in v2:
time: 28.6 us; the launch traced here: 28.5 us
  starting transfers between devices  15 us (52%)
  Pallas kernels  9.93 us (35%)
  waiting for transfers between devices  2.81 us (10%)
  between operations  0.76 us (3%)
    pallas_call x7, Pallas kernels, call(): pl.pallas_call(kernel, out_shape=shapes, in_specs=place, out_specs=[pl.Bl...  9.93 us
    ppermute x1, starting transfers between devices, on_device(): outer = lax.ppermute(outer, 'lon', lon_outer)  5.52 us
    ppermute x1, starting transfers between devices, on_device(): pair = lax.ppermute(tokens, 'lat', lat_inner)  3.33 us
    ppermute x1, starting transfers between devices, on_device(): other_kv = lax.ppermute(kv, 'lat', lat_inner)  2.65 us
    ppermute x1, starting transfers between devices, on_device(): pair_ids = lax.ppermute(region_ids, 'lat', lat_inner)  2.3 us
    ppermute x1, waiting for transfers between devices, on_device(): cross = lax.ppermute(cross, 'lat', lat_outer)  2.22 us
    ppermute x1, starting transfers between devices, on_device(): inner = lax.ppermute(inner, 'lon', lon_inner)  1.09 us
    ppermute x1, waiting for transfers between devices, on_device(): other_kv = lax.ppermute(kv, 'lat', lat_inner)  0.58 us
  transfers between devices with their start and end apart: 6, of which 2 were waited for; matrix products, arithmetic and copies ran while one was open for 0% of the time, Pallas kernels for 16%

profile of v2, /device:TPU:1, one launch (start us, length us, event | category | flops | bytes accessed | tf_op | source)
XLA Modules:
  0.0 28.5 jit_solution(12326650846294715384)
XLA Ops:
  0.6 0.0 copy-start.7
  0.6 0.0 copy-start
  0.7 0.0 copy-start.6
  0.7 0.0 copy-start.5
  0.7 3.3 %collective-permute-start = (bf16[8,48,512]{2,1,0:T(8,128)(2,1)}, bf16[8,48,512]{2,1,0:T(8,128)(2,1)S(1)}, u32[]{:S(2)}, u32[]{:S(2)}) collective-permute-start(bf16[8,48,512]{2,1,0:T(8,128)(2,1)} %tok_hbm.1), channel_id=1, source_target_pairs={{0,16},{16,0},{32,48},{48,32},{64,80},{80,64},{96,112},{112,96},{1... | collective-permute-start | bytes 1179656 | tf_op jit(solution)/shard_map/ppermute | solution.py:399
  4.0 1.0 %load_kernel.1 = (bf16[200,512]{1,0:T(8,128)(2,1)S(1)}, bf16[8,48,512]{2,1,0:T(8,128)(2,1)S(1)}, s32[8,48]{1,0:T(8,128)S(1)}) custom-call(bf16[8,48,512]{2,1,0:T(8,128)(2,1)} %tok_hbm.1, s32[8,48]{1,0:T(8,128)} %ids_hbm.1), custom_call_target="tpu_custom_call" | custom-call | flops 4000000000 | bytes 1000000 | tf_op jit(solution)/shard_map/load_kernel/pallas_call | solution.py:376
  5.0 0.1 collective-permute-start.1
  5.2 0.0 copy-done.7
  5.2 2.3 %collective-permute-start.2 = (s32[8,48]{1,0:T(8,128)S(1)}, s32[8,48]{1,0:T(8,128)S(1)}, u32[]{:S(2)}, u32[]{:S(2)}) collective-permute-start(s32[8,48]{1,0:T(8,128)S(1)} %copy-done.7), channel_id=1, source_target_pairs={{0,16},{16,0},{32,48},{48,32},{64,80},{80,64},{96,112},{112,96},{1... | collective-permute-start | bytes 4616 | tf_op jit(solution)/shard_map/ppermute | solution.py:400
  7.5 0.0 copy-done
  7.5 0.0 copy-done.6
  7.5 0.0 copy-done.5
  7.5 0.9 %own_kernel.1 = (bf16[2,5,32,1536]{3,2,1,0:T(8,128)(2,1)S(1)}, f32[2,4,64,128]{3,2,1,0:T(8,128)S(1)}, f32[2,64,128]{2,1,0:T(8,128)S(1)}) custom-call(bf16[512,1536]{1,0:T(8,128)(2,1)S(1)} %copy-done, f32[16,64,64]{2,1,0:T(8,128)S(1)} %copy-done.5, f32[8,64,64]{2,1,0:T(8,128)S(1)} %copy-done.6, bf16[8,48,512]{2,1,0:T(8,128)(2,1)S(1)} %get-tuple-element.17.tok_ref), custom_call_target="tpu_custom_call" | custom-call | flops 1500000000 | bytes 1000000 | tf_op jit(solution)/shard_map/own_kernel/pallas_call | solution.py:376
  8.4 0.0 copy-start.3
  8.4 0.0 collective-permute-done.2.pair_ids_ref
  8.4 2.2 %collective-permute-done.1.cross_ref = bf16[200,512]{1,0:T(8,128)(2,1)S(1)} collective-permute-done((bf16[200,512]{1,0:T(8,128)(2,1)S(1)}, bf16[200,512]{1,0:T(8,128)(2,1)S(1)}, u32[]{:S(2)}, u32[]{:S(2)}) %collective-permute-start.1) | collective-permute-done | bytes 204832 | tf_op jit(solution)/shard_map/ppermute | solution.py:410
  10.6 0.0 collective-permute-done.pair_ref
  10.6 0.0 copy-start.2
  10.6 0.1 edge_kernel.1
  10.7 0.0 copy-start.1
  10.7 1.1 %collective-permute-start.3 = (bf16[72,512]{1,0:T(8,128)(2,1)S(1)}, bf16[72,512]{1,0:T(8,128)(2,1)S(1)}, u32[]{:S(2)}, u32[]{:S(2)}) collective-permute-start(bf16[72,512]{1,0:T(8,128)(2,1)S(1)} %get-tuple-element.21), channel_id=1, source_target_pairs={{0,1},{1,0},{2,3},{3,2},{4,5},{5,4},{6,7},{7,6},{8,9},{9,8},{10,11... | collective-permute-start | bytes 221192 | tf_op jit(solution)/shard_map/ppermute | solution.py:424
  11.8 5.5 %collective-permute-start.4 = (bf16[72,512]{1,0:T(8,128)(2,1)S(1)}, bf16[72,512]{1,0:T(8,128)(2,1)S(1)}, u32[]{:S(2)}, u32[]{:S(2)}) collective-permute-start(bf16[72,512]{1,0:T(8,128)(2,1)S(1)} %get-tuple-element.22), channel_id=1, source_target_pairs={{0,15},{1,2},{2,1},{3,4},{4,3},{5,6},{6,5},{7,8},{8,7},{9,10},{10,... | collective-permute-start | bytes 221192 | tf_op jit(solution)/shard_map/ppermute | solution.py:425
  17.3 0.0 copy-done.3
  17.3 2.2 %inner_kernel.1.add_ref = f32[320,512]{1,0:T(8,128)S(1)} custom-call(bf16[8,48,512]{2,1,0:T(8,128)(2,1)S(1)} %collective-permute-done.pair_ref, bf16[200,512]{1,0:T(8,128)(2,1)S(1)} %collective-permute-done.1.cross_ref, f32[16,128]{1,0:T(8,128)S(1)} %get-tuple-element.23.ids_ref, bf16[2,5,32,1536]{3,2,1,0:T(8,128)(2,1)S(1)} %get-tuple-element.25.inside_ref, ...), custom_call_target="tpu_custom_call" | custom-call | flops 300000000 | bytes 1000000 | tf_op jit(solution)/shard_map/inner_kernel/pallas_call | solution.py:376
  19.5 0.0 collective-permute-done.3.inner_ref
  19.5 0.0 collective-permute-done.4.outer_ref
  19.6 0.0 copy-done.2
  19.6 0.0 copy-done.1
  19.6 3.8 %final_kernel.1 = (bf16[8,48,512]{2,1,0:T(8,128)(2,1)}, bf16[96,1024]{1,0:T(8,128)(2,1)S(1)}, bf16[96,1024]{1,0:T(8,128)(2,1)S(1)}, bf16[96,1024]{1,0:T(8,128)(2,1)S(1)}) custom-call(bf16[8,48,512]{2,1,0:T(8,128)(2,1)S(1)} %get-tuple-element.17.tok_ref, bf16[8,48,512]{2,1,0:T(8,128)(2,1)S(1)} %collective-permute-done.pair_ref, ...), custom_call_target="tpu_custom_call" | custom-call | flops 1000000000 | bytes 1000000 | tf_op jit(solution)/shard_map/final_kernel/pallas_call | solution.py:376
  23.3 0.0 copy-start.4
  23.3 2.7 %collective-permute-start.5 = (bf16[96,1024]{1,0:T(8,128)(2,1)S(1)}, bf16[96,1024]{1,0:T(8,128)(2,1)S(1)}, u32[]{:S(2)}, u32[]{:S(2)}) collective-permute-start(bf16[96,1024]{1,0:T(8,128)(2,1)S(1)} %get-tuple-element.28.kv_ref), channel_id=1, source_target_pairs={{0,16},{16,0},{32,48},{48,32},{64,80},{80,64},{96,112},{112,96},{1... | collective-permute-start | bytes 589832 | tf_op jit(solution)/shard_map/ppermute | solution.py:442
  26.0 0.5 %query_kernel.1 = (bf16[96,512]{1,0:T(8,128)(2,1)S(1)}, f32[6,32,128]{2,1,0:T(8,128)S(1)}) custom-call(bf16[96,1024]{1,0:T(8,128)(2,1)S(1)} %get-tuple-element.27.normed_ref, bf16[96,1024]{1,0:T(8,128)(2,1)S(1)} %get-tuple-element.28.kv_ref, f32[2,64,128]{2,1,0:T(8,128)S(1)} %get-tuple-element.20.after_ref.bias_ref, bf16[1024,1536]{1,0:T(8,128)(2,1)S(1)} %copy-done.2), custom_call_target="tpu_custom_call" | custom-call | flops 1000000000 | bytes 1000000 | tf_op jit(solution)/shard_map/query_kernel/pallas_call | solution.py:376
  26.5 0.6 %collective-permute-done.5.other_ref = bf16[96,1024]{1,0:T(8,128)(2,1)S(1)} collective-permute-done((bf16[96,1024]{1,0:T(8,128)(2,1)S(1)}, bf16[96,1024]{1,0:T(8,128)(2,1)S(1)}, u32[]{:S(2)}, u32[]{:S(2)}) %collective-permute-start.5) | collective-permute-done | bytes 196640 | tf_op jit(solution)/shard_map/ppermute | solution.py:442
  27.1 0.0 copy-done.4
  27.1 1.5 %level_two_kernel.1 = bf16[4,24,1024]{2,1,0:T(8,128)(2,1)} custom-call(bf16[96,512]{1,0:T(8,128)(2,1)S(1)} %get-tuple-element.29.query_ref, f32[6,32,128]{2,1,0:T(8,128)S(1)} %get-tuple-element.30.score_ref, bf16[96,1024]{1,0:T(8,128)(2,1)S(1)} %get-tuple-element.28.kv_ref, bf16[96,1024]{1,0:T(8,128)(2,1)S(1)} %collective-permute-done.5.other_ref, ...), custom_call_target="tpu_custom_call" | custom-call | flops 1000000000 | bytes 1000000 | tf_op jit(solution)/shard_map/level_two_kernel/pallas_call | solution.py:376
Async XLA Ops:
  0.6 4.5 %copy-start.7 = (s32[8,48]{1,0:T(8,128)S(1)}, s32[8,48]{1,0:T(8,128)}, u32[]{:S(2)}) copy-start(s32[8,48]{1,0:T(8,128)} %ids_hbm.1) | copy-start | bytes 4612
  0.6 6.8 %copy-start = (bf16[512,1536]{1,0:T(8,128)(2,1)S(1)}, bf16[512,1536]{1,0:T(8,128)(2,1)}, u32[]{:S(2)}) copy-start(bf16[512,1536]{1,0:T(8,128)(2,1)} %qkv_ref.5) | copy-start | bytes 4718596
  0.7 6.8 %copy-start.6 = (f32[8,64,64]{2,1,0:T(8,128)S(1)}, f32[8,64,64]{2,1,0:T(8,128)}, u32[]{:S(2)}) copy-start(f32[8,64,64]{2,1,0:T(8,128)} %two_ref.3) | copy-start | bytes 393220
  0.7 6.8 %copy-start.5 = (f32[16,64,64]{2,1,0:T(8,128)S(1)}, f32[16,64,64]{2,1,0:T(8,128)}, u32[]{:S(2)}) copy-start(f32[16,64,64]{2,1,0:T(8,128)} %one_ref.1) | copy-start | bytes 786436
  0.7 9.9 %collective-permute-start = (bf16[8,48,512]{2,1,0:T(8,128)(2,1)}, bf16[8,48,512]{2,1,0:T(8,128)(2,1)S(1)}, u32[]{:S(2)}, u32[]{:S(2)}) collective-permute-start(bf16[8,48,512]{2,1,0:T(8,128)(2,1)} %tok_hbm.1), channel_id=1, source_target_pairs={{0,16},{16,0},{32,48},{48,32},{64,80},{80,64},{96,112},{112,96},{1... | collective-permute-start | bytes 1179656 | tf_op jit(solution)/shard_map/ppermute | solution.py:399
  5.0 5.6 %collective-permute-start.1 = (bf16[200,512]{1,0:T(8,128)(2,1)S(1)}, bf16[200,512]{1,0:T(8,128)(2,1)S(1)}, u32[]{:S(2)}, u32[]{:S(2)}) collective-permute-start(bf16[200,512]{1,0:T(8,128)(2,1)S(1)} %get-tuple-element.18), channel_id=1, source_target_pairs={{0,240},{16,32},{32,16},{48,64},{64,48},{80,96},{96,80},{112,128},... | collective-permute-start | bytes 614408 | tf_op jit(solution)/shard_map/ppermute | solution.py:410
  5.2 3.2 %collective-permute-start.2 = (s32[8,48]{1,0:T(8,128)S(1)}, s32[8,48]{1,0:T(8,128)S(1)}, u32[]{:S(2)}, u32[]{:S(2)}) collective-permute-start(s32[8,48]{1,0:T(8,128)S(1)} %copy-done.7), channel_id=1, source_target_pairs={{0,16},{16,0},{32,48},{48,32},{64,80},{80,64},{96,112},{112,96},{1... | collective-permute-start | bytes 4616 | tf_op jit(solution)/shard_map/ppermute | solution.py:400
  8.4 8.9 %copy-start.3 = (bf16[512,512]{1,0:T(8,128)(2,1)S(1)}, bf16[512,512]{1,0:T(8,128)(2,1)}, u32[]{:S(2)}) copy-start(bf16[512,512]{1,0:T(8,128)(2,1)} %out_ref.4) | copy-start | bytes 1572868
  10.6 8.9 %copy-start.2 = (bf16[1024,1536]{1,0:T(8,128)(2,1)S(1)}, bf16[1024,1536]{1,0:T(8,128)(2,1)}, u32[]{:S(2)}) copy-start(bf16[1024,1536]{1,0:T(8,128)(2,1)} %two_ref.5) | copy-start | bytes 9437188
  10.7 8.9 %copy-start.1 = (bf16[2048,1024]{1,0:T(8,128)(2,1)S(1)}, bf16[2048,1024]{1,0:T(8,128)(2,1)}, u32[]{:S(2)}) copy-start(bf16[2048,1024]{1,0:T(8,128)(2,1)} %merge_ref.1) | copy-start | bytes 12582916
  10.7 8.8 %collective-permute-start.3 = (bf16[72,512]{1,0:T(8,128)(2,1)S(1)}, bf16[72,512]{1,0:T(8,128)(2,1)S(1)}, u32[]{:S(2)}, u32[]{:S(2)}) collective-permute-start(bf16[72,512]{1,0:T(8,128)(2,1)S(1)} %get-tuple-element.21), channel_id=1, source_target_pairs={{0,1},{1,0},{2,3},{3,2},{4,5},{5,4},{6,7},{7,6},{8,9},{9,8},{10,11... | collective-permute-start | bytes 221192 | tf_op jit(solution)/shard_map/ppermute | solution.py:424
  11.8 7.7 %collective-permute-start.4 = (bf16[72,512]{1,0:T(8,128)(2,1)S(1)}, bf16[72,512]{1,0:T(8,128)(2,1)S(1)}, u32[]{:S(2)}, u32[]{:S(2)}) collective-permute-start(bf16[72,512]{1,0:T(8,128)(2,1)S(1)} %get-tuple-element.22), channel_id=1, source_target_pairs={{0,15},{1,2},{2,1},{3,4},{4,3},{5,6},{6,5},{7,8},{8,7},{9,10},{10,... | collective-permute-start | bytes 221192 | tf_op jit(solution)/shard_map/ppermute | solution.py:425
  23.3 3.7 %copy-start.4 = (bf16[512,1024]{1,0:T(8,128)(2,1)S(1)}, bf16[512,1024]{1,0:T(8,128)(2,1)}, u32[]{:S(2)}) copy-start(bf16[512,1024]{1,0:T(8,128)(2,1)} %out_ref.5) | copy-start | bytes 3145732
  23.3 3.7 %collective-permute-start.5 = (bf16[96,1024]{1,0:T(8,128)(2,1)S(1)}, bf16[96,1024]{1,0:T(8,128)(2,1)S(1)}, u32[]{:S(2)}, u32[]{:S(2)}) collective-permute-start(bf16[96,1024]{1,0:T(8,128)(2,1)S(1)} %get-tuple-element.28.kv_ref), channel_id=1, source_target_pairs={{0,16},{16,0},{32,48},{48,32},{64,80},{80,64},{96,112},{112,96},{1... | collective-permute-start | bytes 589832 | tf_op jit(solution)/shard_map/ppermute | solution.py:442

commit v3 on v2

v3 whole, which is shorter than its diff:
```python
import math

import jax
import jax.numpy as jnp
from jax import lax
from jax.experimental import pallas as pl
from jax.experimental.pallas import tpu as pltpu
from jax.sharding import PartitionSpec as P

EPSILON = 1e-05
LOG2E = math.log2(math.e)
BF = jnp.bfloat16
F32 = jnp.float32
ROWS = 8
COLS = 48
TILES = 7
INSIDE = 5
FRAME = 56
D1 = 512
D2 = 1024
MIB = 1024 * 1024

NT = (((1,), (1,)), ((), ()))
TN = (((0,), (0,)), ((), ()))


def layer_norm(x):
    width = x.shape[-1]
    mean = jnp.sum(x, axis=-1, keepdims=True) * (1.0 / width)
    c = x - mean
    var = jnp.sum(c * c, axis=-1, keepdims=True) * (1.0 / width)
    return c * lax.rsqrt(var + EPSILON)


def row_stats(blocks):
    width = sum(x.shape[-1] for x in blocks)
    mean = sum(jnp.sum(x, axis=-1, keepdims=True) for x in blocks) * (1.0 / width)
    centered = [x - mean for x in blocks]
    var = sum(jnp.sum(c * c, axis=-1, keepdims=True) for c in centered) * (1.0 / width)
    return mean, lax.rsqrt(var + EPSILON)


def lanes_to(x, width):
    return jnp.concatenate([x, jnp.zeros((x.shape[0], width - x.shape[1]), x.dtype)], axis=1)


def lat_parity():
    return lax.rem(lax.axis_index("lat"), 2)


def lon_parity():
    return lax.rem(lax.axis_index("lon"), 2)


def start_all(pairs, sems):
    copies = [pltpu.make_async_copy(src, dst, sems.at[n]) for n, (src, dst) in enumerate(pairs)]
    for copy in copies:
        copy.start()
    return copies


def load_kernel(tok_hbm, ids_hbm, cross_ref, tok_ref, ids_ref, sems):
    copies = start_all([(ids_hbm, ids_ref), (tok_hbm, tok_ref)], sems)
    copies[0].wait()
    ids = lanes_to(ids_ref[...].astype(F32), D1)
    cross_ref[4 * COLS :] = jnp.where(lat_parity() == 0, ids, pltpu.roll(ids, 4, 0)).astype(BF)
    copies[1].wait()
    for r in range(4):
        cross_ref[r * COLS : (r + 1) * COLS] = tok_ref[4 * lat_parity() + r]


def next_row(r):
    return 4 * lat_parity() + r


def edge_kernel(
    tok_ref, ids_ref, pair_ref, pair_ids_ref, cross_ref, after_ref, inner_ref, outer_ref, all_ids_ref
):
    first = [tok_ref[r, 0:16].astype(F32)[0:4] for r in range(ROWS)]
    first += [pair_ref[next_row(r), 0:16].astype(F32)[0:4] for r in range(4)]
    first += [cross_ref[COLS * r : COLS * r + 16].astype(F32)[0:4] for r in range(4)]
    last = [tok_ref[r, 32:48].astype(F32)[12:16] for r in range(ROWS)]
    last += [pair_ref[next_row(r), 32:48].astype(F32)[12:16] for r in range(4)]
    last += [cross_ref[COLS * r + 32 : COLS * r + 48].astype(F32)[12:16] for r in range(4)]
    own = lanes_to(ids_ref[...].astype(F32), 128)
    pair = lanes_to(pair_ids_ref[...].astype(F32), 128)
    pair = jnp.where(lat_parity() == 0, pair, pltpu.roll(pair, 4, 0))
    cross = cross_ref[4 * COLS :, 0:128].astype(F32)
    halo = jnp.concatenate([pair[0:4], cross[0:4]], axis=0)
    all_ids_ref[...] = jnp.concatenate([own, halo], axis=0)
    ids = jnp.concatenate([own, halo], axis=1)
    first = jnp.concatenate(first + [lanes_to(ids, D1)], axis=0).astype(BF)
    ids = pltpu.roll(ids, 256 - (COLS - 4), 1)
    last = jnp.concatenate(last + [lanes_to(ids, D1)], axis=0).astype(BF)
    even = lon_parity() == 0
    inner_ref[...] = jnp.where(even, last, first)
    outer_ref[...] = jnp.where(even, first, last)


def sides(inner_ref, outer_ref):
    inner, outer = inner_ref[...].astype(F32), outer_ref[...].astype(F32)
    even = lon_parity() == 0
    return jnp.where(even, outer, inner), jnp.where(even, inner, outer)


def side_pieces(x, row):
    order = [row + r for r in range(4)] + [4 - row + r for r in range(4)]
    west = [x[8 * r + c : 8 * r + c + 4] for c in (4, 0) for r in order]
    east = [x[8 * r + c : 8 * r + c + 4] for c in (0, 4) for r in order]
    return west, east


def own_kernel(
    qkv_ref, one_ref, two_ref, tok_ref, inside_out, edge_out, one_out, side_out, two_out, normed
):
    first, last = [], []
    for r in range(0, ROWS, 2):
        pair = []
        for k in range(2):
            x = layer_norm(tok_ref[r + k].astype(F32))
            pair.append(x[4 : COLS - 4].reshape(INSIDE, 8, D1))
            first.append(x[0:4])
            last.append(x[COLS - 4 :])
        normed[r // 4, :, (r % 4) // 2] = jnp.concatenate(pair, axis=1).astype(BF)
    edge = jnp.concatenate(first[0:4] + last[0:4] + first[4:8] + last[4:8], axis=0).astype(BF)
    for half in range(2):
        low = 32 * (1 - half)
        for g in range(4):
            turned = one_ref[4 * g : 4 * g + 4, low : low + 32, :].reshape(128, 64).T * LOG2E
            one_out[half, g, 0:32] = turned[low : low + 32]
            one_out[half, g, 32:64] = turned[32 - low : 64 - low]
    for half in range(2):
        row = 4 * (1 - half)
        for g in range(2):
            heads = [side_pieces(one_ref[8 * g + h], row) for h in range(8)]
            for side in range(2):
                part = jnp.concatenate([x for h in heads for x in h[side][0:4]], axis=0)
                pieces = side_pieces(part.T * LOG2E, row)[side]
                side_out[half, side, g] = jnp.concatenate(pieces, axis=0)
    low = pl.multiple_of(lat_parity() * 32, 32)
    for g in range(2):
        turned = two_ref[4 * g : 4 * g + 4, pl.ds(low, 32), :].reshape(128, 64).T * LOG2E
        even = lat_parity() == 0
        two_out[g, 0:32] = jnp.where(even, turned[0:32], turned[32:64])
        two_out[g, 32:64] = jnp.where(even, turned[32:64], turned[0:32])
    x = jnp.concatenate([normed[...].reshape(2 * INSIDE * 32, D1), edge], axis=0)
    qkv = jnp.dot(x, qkv_ref[...], preferred_element_type=F32).astype(BF)
    inside_out[...] = qkv[0 : 2 * INSIDE * 32].reshape(2, INSIDE, 32, 3 * D1)
    edge_out[...] = qkv[2 * INSIDE * 32 :]


def masked_heads(q, head_dim, count):
    lane = lax.broadcasted_iota(jnp.int32, q.shape, 1) // head_dim
    zero = jnp.zeros_like(q)
    return jnp.concatenate([jnp.where(lane == h, q, zero) for h in range(count)], axis=0)


def pick_heads(o, head_dim, count):
    rows = o.shape[0] // count
    lane = lax.broadcasted_iota(jnp.int32, (rows, o.shape[1]), 1) // head_dim
    out = o[0:rows]
    for h in range(1, count):
        out = jnp.where(lane == h, o[h * rows : (h + 1) * rows], out)
    return out


def softmax_keys(s, allowed):
    if allowed is not None:
        s = jnp.where(allowed, s, -1e30)
    p = jnp.exp2(s - jnp.max(s, axis=0, keepdims=True))
    return p * (1.0 / jnp.sum(p, axis=0, keepdims=True))


def region_masks(own, halo):
    turned = jnp.concatenate([own, halo, jnp.zeros((120, 128), F32)], axis=0).T

    def window(j):
        tiles = [
            jnp.broadcast_to(turned[8 * j : 8 * j + 8, r : r + 1], (8, 128)) for r in range(8)
        ]
        queries = jnp.concatenate(tiles[0:4] * 4, axis=0).T[0:1]
        return jnp.concatenate(tiles, axis=0) == queries

    return window


def in_range(cross_ids):
    lat = lax.axis_index("lat")
    outside = (lat == 0) | (lat == lax.axis_size("lat") - 1)
    return jnp.where(outside, -1.0, cross_ids)


def attend_one(halves, allowed, bias_ref, query, keys, values):
    scale = LOG2E / math.sqrt(32)
    units = [(w, g) for w in range(len(halves)) for g in range(4)]
    scores = [
        lax.dot_general(
            keys(w, g), masked_heads(query(w, g), 32, 4), NT, preferred_element_type=F32
        )
        for w, g in units
    ]
    probs = [
        softmax_keys(s * scale + bias_ref[halves[w], g], allowed[w]).astype(BF)
        for s, (w, g) in zip(scores, units)
    ]
    outs = [
        lax.dot_general(p, values(w, g), TN, preferred_element_type=F32)
        for p, (w, g) in zip(probs, units)
    ]
    picked = [pick_heads(o, 32, 4).astype(BF) for o in outs]
    return [jnp.concatenate(picked[4 * w : 4 * w + 4], axis=1) for w in range(len(halves))]


def lanes_of(block, g):
    return slice(block * D1 + g * 128, block * D1 + g * 128 + 128)


def half_inner(half, halo_rows, own_ids, halo_ids, inside_ref, qkv_ref, bias_ref, out_ref, normed):
    rows = [layer_norm(x) for x in halo_rows]
    for r in range(0, 4, 2):
        pair = [rows[k][4 : COLS - 4].reshape(INSIDE, 8, D1) for k in (r, r + 1)]
        normed[:, r // 2] = jnp.concatenate(pair, axis=1).astype(BF)
    edge = jnp.concatenate([x[0:4] for x in rows] + [x[COLS - 4 :] for x in rows], axis=0)
    halo = jnp.dot(
        jnp.concatenate([normed[...].reshape(INSIDE * 32, D1), edge.astype(BF)], axis=0),
        qkv_ref[:, D1:],
        preferred_element_type=F32,
    ).astype(BF)
    mask = region_masks(pltpu.roll(own_ids, 4, 1), pltpu.roll(halo_ids, 4, 1))

    def both(w, block, g):
        own = inside_ref[half, w, :, lanes_of(block, g)]
        return jnp.concatenate([own, halo[32 * w : 32 * w + 32, lanes_of(block - 1, g)]], axis=0)

    attended = attend_one(
        [half] * INSIDE,
        [mask(j) for j in range(1, TILES - 1)],
        bias_ref,
        lambda w, g: inside_ref[half, w, :, lanes_of(0, g)],
        lambda w, g: both(w, 1, g),
        lambda w, g: both(w, 2, g),
    )
    add = jnp.dot(jnp.concatenate(attended, axis=0), out_ref[...], preferred_element_type=F32)
    return add, halo[INSIDE * 32 :]


def pair_kernel(
    pair_ref, pair_ids_ref, ids_ref, inside_ref, qkv_ref, bias_ref, out_ref, add_out, edge_out,
    normed,
):
    even = lat_parity() == 0
    own = lanes_to(ids_ref[...].astype(F32), 128)
    pair = lanes_to(pair_ids_ref[...].astype(F32), 128)
    own = jnp.where(even, pltpu.roll(own, 4, 0), own)
    pair = jnp.where(even, pair, pltpu.roll(pair, 4, 0))
    rows = [pair_ref[next_row(r)].astype(F32) for r in range(4)]
    add_out[...], edge_out[...] = half_inner(
        1 - lat_parity(), rows, own[0:4], pair[0:4], inside_ref, qkv_ref, bias_ref, out_ref, normed
    )


def cross_kernel(
    cross_ref, ids_ref, inside_ref, qkv_ref, bias_ref, out_ref, add_out, edge_out, normed
):
    ids = ids_ref[...]
    own = jnp.where(lat_parity() == 0, ids[0:4], ids[4:8])
    rows = [cross_ref[COLS * r : COLS * r + COLS].astype(F32) for r in range(4)]
    add_out[...], edge_out[...] = half_inner(
        lat_parity(), rows, own, in_range(ids[12:16]), inside_ref, qkv_ref, bias_ref, out_ref, normed
    )


def final_kernel(
    tok_ref, inner_ref, outer_ref, ids_ref, qkv_ref, bias_ref, out_ref, own_edge_ref,
    pair_edge_ref, cross_edge_ref, pair_add_ref, cross_add_ref, merge_ref, two_ref,
    merge_sum_ref, two_sum_ref,
    one_out, merged_out, kv_out,
    level, parts, done, sem,
):
    even = lat_parity() == 0
    west, east = sides(inner_ref, outer_ref)
    x = layer_norm(jnp.concatenate([west[0:64], east[0:64]], axis=0)).astype(BF)
    new = jnp.dot(x, qkv_ref[:, D1:], preferred_element_type=F32).astype(BF)

    lane = lax.broadcasted_iota(jnp.int32, (2 * ROWS, 128), 1)
    own = pltpu.roll(ids_ref[...], 4, 1)
    near = jnp.concatenate([west[64:72, 0:128], west[64:72, 128:256]], axis=0)
    far = jnp.concatenate([east[64:72, 0:128], east[64:72, 128:256]], axis=0)
    far = pltpu.roll(far, COLS + 4, 1)
    ids = jnp.where(lane < 4, near, jnp.where(lane < COLS + 4, own, far))
    pair_ids, cross_ids = ids[8:12], in_range(ids[12:16])
    above, below = jnp.where(even, cross_ids, pair_ids), jnp.where(even, pair_ids, cross_ids)
    rows = [ids[0:4], above, ids[4:8], below, jnp.zeros((112, 128), F32)]
    turned = jnp.concatenate(rows, axis=0).T

    windows = [(half, side) for half in range(2) for side in range(2)]
    keys, values, queries, allowed = [], [], [], []
    for half, side in windows:
        at = 16 * (2 * half + side)
        a, b = cross_edge_ref, pair_edge_ref
        c, d = new[64 * side + 48 : 64 * side + 64], new[64 * side + 32 : 64 * side + 48]
        if half == 1:
            a, b, c, d = b, a, d, c
        lines = slice(16 * side, 16 * side + 16)
        kv = jnp.concatenate(
            [
                own_edge_ref[at : at + 16, D1:],
                jnp.where(even, a[lines], b[lines]),
                new[64 * side + 16 * half : 64 * side + 16 * half + 16],
                jnp.where(even, c, d),
            ],
            axis=0,
        )
        keys.append(kv[:, 0:D1])
        values.append(kv[:, D1:])
        queries.append(own_edge_ref[at : at + 16, 0:D1])
        starts = (4, 0) if side == 0 else (COLS, COLS + 4)
        pieces = [
            jnp.broadcast_to(turned[c0 : c0 + 4, r : r + 1], (4, 128))
            for c0 in starts
            for r in range(8 * half, 8 * half + 8)
        ]
        own_ids = jnp.concatenate(pieces[0:4] * 8, axis=0).T[0:1]
        allowed.append(jnp.concatenate(pieces, axis=0) == own_ids)
    scale = LOG2E / math.sqrt(32)
    units = [(w, g) for w in range(4) for g in range(2)]
    scores = [
        lax.dot_general(
            keys[w][:, 256 * g : 256 * g + 256],
            masked_heads(queries[w][:, 256 * g : 256 * g + 256], 32, 8),
            NT,
            preferred_element_type=F32,
        )
        for w, g in units
    ]
    probs = [
        softmax_keys(s * scale + bias_ref[windows[w][0], windows[w][1], g], allowed[w]).astype(BF)
        for s, (w, g) in zip(scores, units)
    ]
    outs = [
        lax.dot_general(p, values[w][:, 256 * g : 256 * g + 256], TN, preferred_element_type=F32)
        for p, (w, g) in zip(probs, units)
    ]
    picked = [pick_heads(o, 32, 8).astype(BF) for o in outs]
    attended = [jnp.concatenate(picked[2 * w : 2 * w + 2], axis=1) for w in range(4)]
    edge = jnp.dot(jnp.concatenate(attended, axis=0), out_ref[...], preferred_element_type=F32)
    for row in range(ROWS):
        half, r = row // 4, row % 4
        at = 32 * half + 4 * r
        adds = [edge[at : at + 4]]
        for j in range(INSIDE):
            tile = slice(32 * j + 8 * r, 32 * j + 8 * r + 8)
            upper, lower = cross_add_ref[tile], pair_add_ref[tile]
            if half == 1:
                upper, lower = lower, upper
            adds.append(jnp.where(even, upper, lower))
        adds.append(edge[at + 16 : at + 20])
        value = (tok_ref[row].astype(F32) + jnp.concatenate(adds, axis=0)).astype(BF)
        done[row] = value
        for n in range(4):
            level[n, row] = value[:, n * 128 : n * 128 + 128].astype(F32)
    store = pltpu.make_async_copy(done, one_out, sem)
    store.start()

    means, factors = [], []
    for i in range(4):
        quartet = [
            jnp.concatenate(
                [level[n, 2 * i + dr, pl.ds(dc, COLS // 2, 2), :] for n in range(4)], axis=1
            )
            for dc in range(2)
            for dr in range(2)
        ]
        for n in range(4):
            parts[n, :, i] = quartet[n].reshape(3, 8, D1)
        mean, factor = row_stats(quartet)
        means.append(mean)
        factors.append(factor)
    order = [(i, slice(8 * w, 8 * w + 8)) for w in range(3) for i in range(4)]
    mean = jnp.concatenate([means[i][at] for i, at in order], axis=0)
    factor = jnp.concatenate([factors[i][at] for i, at in order], axis=0)
    total = jnp.zeros((96, D2), F32)
    for n in range(4):
        total += jnp.dot(
            parts[n].reshape(96, D1).astype(BF),
            merge_ref[n * D1 : (n + 1) * D1, :],
            preferred_element_type=F32,
        )
    merged = ((total - mean * merge_sum_ref[0:1]) * factor).astype(BF)
    merged_out[...] = merged
    mean, factor = row_stats([merged.astype(F32)])
    total = jnp.dot(merged, two_ref[:, 512:], preferred_element_type=F32)
    kv_out[...] = ((total - mean * two_sum_ref[0:1, 512:]) * factor).astype(BF)
    store.wait()


def sums_kernel(merge_ref, two_ref, after_ref, merge_out, two_out):
    ones = jnp.ones((16, 4 * D1), BF)
    merge_out[...] = jnp.dot(ones, merge_ref[...], preferred_element_type=F32)[0:8]
    two_out[...] = jnp.dot(ones[:, 0:D2], two_ref[...], preferred_element_type=F32)[0:8]


TWO_UNITS = [(w, g) for w in range(3) for g in range(2)]


def scores_two(keys_ref, queries, bias):
    scale = LOG2E / math.sqrt(64)
    return [
        lax.dot_general(
            keys_ref[w * 32 : w * 32 + 32, g * 256 : g * 256 + 256],
            masked_heads(queries[w * 32 : w * 32 + 32, g * 256 : g * 256 + 256], 64, 4),
            NT,
            preferred_element_type=F32,
        )
        * scale
        + bias[g]
        for w, g in TWO_UNITS
    ]


def query_kernel(merged_ref, kv_ref, bias_ref, two_ref, two_sum_ref, query_out, score_out):
    merged = merged_ref[...]
    mean, factor = row_stats([merged.astype(F32)])
    total = jnp.dot(merged, two_ref[:, :512], preferred_element_type=F32)
    q = ((total - mean * two_sum_ref[0:1, :512]) * factor).astype(BF)
    query_out[...] = q
    for n, s in enumerate(scores_two(kv_ref, q, [bias_ref[g, 0:32] for g in range(2)])):
        score_out[n] = s


def level_two_kernel(
    query_ref, score_ref, kv_ref, other_ref, merged_ref, bias_ref, out_ref, two_out, result, sems
):
    far = scores_two(other_ref, query_ref[...], [bias_ref[g, 32:64] for g in range(2)])
    probs = [
        softmax_keys(jnp.concatenate([score_ref[n], s], axis=0), None).astype(BF)
        for n, s in enumerate(far)
    ]
    outs = []
    for p, (w, g) in zip(probs, TWO_UNITS):
        block = (slice(w * 32, w * 32 + 32), slice(512 + g * 256, 768 + g * 256))
        values = jnp.concatenate([kv_ref[block], other_ref[block]], axis=0)
        outs.append(lax.dot_general(p, values, TN, preferred_element_type=F32))
    picked = [pick_heads(o, 64, 4).astype(BF) for o in outs]
    attended = jnp.concatenate(
        [jnp.concatenate(picked[2 * w : 2 * w + 2], axis=1) for w in range(3)], axis=0
    )
    stores = []
    for part in range(2):
        lanes = slice(part * 512, part * 512 + 512)
        y = merged_ref[:, lanes].astype(F32) + jnp.dot(
            attended, out_ref[:, lanes], preferred_element_type=F32
        )
        for i in range(4):
            tiles = [y[32 * w + 8 * i : 32 * w + 8 * i + 8] for w in range(3)]
            result[i, :, lanes] = jnp.concatenate(tiles, axis=0).astype(BF)
        stores.append(
            pltpu.make_async_copy(result.at[:, :, lanes], two_out.at[:, :, lanes], sems.at[part])
        )
        stores[-1].start()
    for store in stores:
        store.wait()


def call(kernel, outs, args, hbm=0, scratch=(), mib=16, us=1.0, hbm_outs=0):
    shapes = [jax.ShapeDtypeStruct(s, d) for s, d in outs]
    place = [pl.BlockSpec(memory_space=pltpu.HBM)] * hbm
    place += [pl.BlockSpec(memory_space=pltpu.VMEM)] * (len(args) - hbm)
    args = [
        pltpu.with_memory_space_constraint(x, pltpu.HBM) if n < hbm else x
        for n, x in enumerate(args)
    ]
    return pl.pallas_call(
        kernel,
        out_shape=shapes,
        in_specs=place,
        out_specs=[pl.BlockSpec(memory_space=pltpu.HBM)] * hbm_outs
        + [pl.BlockSpec(memory_space=pltpu.VMEM)] * (len(outs) - hbm_outs),
        scratch_shapes=list(scratch),
        compiler_params=pltpu.CompilerParams(vmem_limit_bytes=mib * MIB),
        cost_estimate=pl.CostEstimate(
            flops=int(us * 10**9), bytes_accessed=10**6, transcendentals=0
        ),
        name=kernel.__name__,
    )(*args)


def on_device(
    tokens, region_ids, bias_one, qkv_one, out_one, merge_proj, bias_two, qkv_two, out_two
):
    lats, lons = lax.axis_size("lat"), lax.axis_size("lon")
    lat_inner = [(i, i ^ 1) for i in range(lats)]
    lat_outer = [(i, (i + (1 if i % 2 else -1)) % lats) for i in range(lats)]
    lon_inner = [(i, i ^ 1) for i in range(lons)]
    lon_outer = [(i, (i + (1 if i % 2 else -1)) % lons) for i in range(lons)]

    pair = lax.ppermute(tokens, "lat", lat_inner)
    pair_ids = lax.ppermute(region_ids, "lat", lat_inner)
    cross, tokens, region_ids = call(
        load_kernel,
        [((200, D1), BF), ((ROWS, COLS, D1), BF), ((ROWS, COLS), jnp.int32)],
        [tokens, region_ids],
        hbm=2,
        scratch=[pltpu.SemaphoreType.DMA((2,))],
        mib=4,
        us=4.0,
    )
    cross = lax.ppermute(cross, "lat", lat_outer)
    inside, own_edge, table_one, table_side, table_two = call(
        own_kernel,
        [
            ((2, INSIDE, 32, 3 * D1), BF), ((64, 3 * D1), BF), ((2, 4, 64, 128), F32),
            ((2, 2, 2, 64, 128), F32), ((2, 64, 128), F32),
        ],
        [qkv_one, bias_one, bias_two, tokens],
        scratch=[pltpu.VMEM((2, INSIDE, 2, 16, D1), BF)],
        us=1.5,
    )
    half_shape = pltpu.VMEM((INSIDE, 2, 16, D1), BF)
    pair_add, pair_edge = call(
        pair_kernel,
        [((INSIDE * 32, D1), F32), ((32, 2 * D1), BF)],
        [pair, pair_ids, region_ids, inside, qkv_one, table_one, out_one],
        scratch=[half_shape],
        us=0.3,
    )
    inner, outer, ids = call(
        edge_kernel,
        [((72, D1), BF), ((72, D1), BF), ((2 * ROWS, 128), F32)],
        [tokens, region_ids, pair, pair_ids, cross, pair_add],
        mib=4,
    )
    inner = lax.ppermute(inner, "lon", lon_inner)
    outer = lax.ppermute(outer, "lon", lon_outer)
    cross_add, cross_edge = call(
        cross_kernel,
        [((INSIDE * 32, D1), F32), ((32, 2 * D1), BF)],
        [cross, ids, inside, qkv_one, table_one, out_one],
        scratch=[half_shape],
        us=0.3,
    )
    merge_sum, two_sum = call(
        sums_kernel,
        [((8, D2), F32), ((8, 1536), F32)],
        [merge_proj, qkv_two, cross_edge],
        us=0.3,
    )
    level_one, merged, kv = call(
        final_kernel,
        [((ROWS, COLS, D1), BF), ((96, D2), BF), ((96, 1024), BF)],
        [
            tokens, inner, outer, ids, qkv_one, table_side, out_one, own_edge, pair_edge,
            cross_edge, pair_add, cross_add, merge_proj, qkv_two, merge_sum, two_sum,
        ],
        scratch=[
            pltpu.VMEM((4, ROWS, COLS, 128), F32),
            pltpu.VMEM((4, 3, 4, 8, D1), F32),
            pltpu.VMEM((ROWS, COLS, D1), BF),
            pltpu.SemaphoreType.DMA,
        ],
        hbm_outs=1,
    )
    other_kv = lax.ppermute(kv, "lat", lat_inner)
    query, scores = call(
        query_kernel,
        [((96, 512), BF), ((6, 32, 128), F32)],
        [merged, kv, table_two, qkv_two, two_sum],
    )
    (level_two,) = call(
        level_two_kernel,
        [((4, 24, D2), BF)],
        [query, scores, kv, other_kv, merged, table_two, out_two],
        scratch=[pltpu.VMEM((4, 24, D2), BF), pltpu.SemaphoreType.DMA((2,))],
        hbm_outs=1,
    )
    return (level_one, level_two)


def solution(mesh):
    placed = (P("lat", "lon", None), P("lat", "lon"), P(), P(), P(), P(), P(), P(), P())
    return jax.shard_map(
        on_device,
        mesh=mesh,
        in_specs=placed,
        out_specs=(P("lat", "lon", None), P("lat", "lon", None)),
        check_vma=False,
    )
```

time: 28.6 us -> 28.1 us (0.983)
  waiting for transfers between devices: 2.81 us -> 1.26 us
  Pallas kernels: 9.93 us -> 10.9 us
    ppermute x1, waiting for transfers between devices: 2.22 us -> 0.72 us  [on_device(): cross = lax.ppermute(cross, 'lat', lat_outer)]
    ppermute x1, starting transfers between devices: 2.65 us -> 1.63 us  [on_device(): other_kv = lax.ppermute(kv, 'lat', lat_inner)]
    pallas_call x7 -> x9, Pallas kernels: 9.93 us -> 10.9 us  [call(): pl.pallas_call(kernel, out_shape=shapes, in_specs=place, out_specs=[pl.Bl...]
    ppermute x1, starting transfers between devices: 1.09 us -> 1.82 us  [on_device(): inner = lax.ppermute(inner, 'lon', lon_inner)]
    ppermute x1, starting transfers between devices: 5.52 us -> 5.82 us  [on_device(): outer = lax.ppermute(outer, 'lon', lon_outer)]
  transfers between devices with their start and end apart: 6 -> 6, of which waited for: 2 -> 2; matrix products, arithmetic and copies ran while one was open for 0% -> 0% of each run, Pallas kernels for 16% -> 23%
where the time goes in v3:
time: 28.1 us; the launch traced here: 28 us
  starting transfers between devices  15 us (53%)
  Pallas kernels  10.9 us (39%)
  waiting for transfers between devices  1.26 us (4%)
  between operations  0.78 us (3%)
    pallas_call x9, Pallas kernels, call(): pl.pallas_call(kernel, out_shape=shapes, in_specs=place, out_specs=[pl.Bl...  10.9 us
    ppermute x1, starting transfers between devices, on_device(): outer = lax.ppermute(outer, 'lon', lon_outer)  5.82 us
    ppermute x1, starting transfers between devices, on_device(): pair = lax.ppermute(tokens, 'lat', lat_inner)  3.33 us
    ppermute x1, starting transfers between devices, on_device(): pair_ids = lax.ppermute(region_ids, 'lat', lat_inner)  2.3 us
    ppermute x1, starting transfers between devices, on_device(): inner = lax.ppermute(inner, 'lon', lon_inner)  1.82 us
    ppermute x1, starting transfers between devices, on_device(): other_kv = lax.ppermute(kv, 'lat', lat_inner)  1.63 us
    ppermute x1, waiting for transfers between devices, on_device(): cross = lax.ppermute(cross, 'lat', lat_outer)  0.72 us
  transfers between devices with their start and end apart: 6, of which 2 were waited for; matrix products, arithmetic and copies ran while one was open for 0% of the time, Pallas kernels for 23%

profile of v3, /device:TPU:1, one launch (start us, length us, event | category | flops | bytes accessed | tf_op | source)
XLA Modules:
  0.0 28.0 jit_solution(3549310405666254743)
XLA Ops:
  0.6 0.0 copy-start.7
  0.6 0.0 copy-start.1
  0.7 0.0 copy-start.6
  0.7 0.0 copy-start.5
  0.7 3.3 %collective-permute-start = (bf16[8,48,512]{2,1,0:T(8,128)(2,1)}, bf16[8,48,512]{2,1,0:T(8,128)(2,1)S(1)}, u32[]{:S(2)}, u32[]{:S(2)}) collective-permute-start(bf16[8,48,512]{2,1,0:T(8,128)(2,1)} %tok_hbm.1), channel_id=1, source_target_pairs={{0,16},{16,0},{32,48},{48,32},{64,80},{80,64},{96,112},{112,96},{1... | collective-permute-start | bytes 1179656 | tf_op jit(solution)/shard_map/ppermute | solution.py:497
  4.0 1.0 %load_kernel.1 = (bf16[200,512]{1,0:T(8,128)(2,1)S(1)}, bf16[8,48,512]{2,1,0:T(8,128)(2,1)S(1)}, s32[8,48]{1,0:T(8,128)S(1)}) custom-call(bf16[8,48,512]{2,1,0:T(8,128)(2,1)} %tok_hbm.1, s32[8,48]{1,0:T(8,128)} %ids_hbm.1), custom_call_target="tpu_custom_call" | custom-call | flops 4000000000 | bytes 1000000 | tf_op jit(solution)/shard_map/load_kernel/pallas_call | solution.py:473
  5.0 0.0 copy-start.3
  5.1 0.1 collective-permute-start.2
  5.2 0.0 copy-done.7
  5.2 2.3 %collective-permute-start.1 = (s32[8,48]{1,0:T(8,128)S(1)}, s32[8,48]{1,0:T(8,128)S(1)}, u32[]{:S(2)}, u32[]{:S(2)}) collective-permute-start(s32[8,48]{1,0:T(8,128)S(1)} %copy-done.7), channel_id=1, source_target_pairs={{0,16},{16,0},{32,48},{48,32},{64,80},{80,64},{96,112},{112,96},{1... | collective-permute-start | bytes 4616 | tf_op jit(solution)/shard_map/ppermute | solution.py:498
  7.5 0.0 copy-done.1
  7.5 0.0 copy-done.6
  7.5 0.0 copy-done.5
  7.5 1.0 %own_kernel.1 = (bf16[2,5,32,1536]{3,2,1,0:T(8,128)(2,1)S(1)}, bf16[64,1536]{1,0:T(8,128)(2,1)S(1)}, f32[2,4,64,128]{3,2,1,0:T(8,128)S(1)}, f32[2,2,2,64,128]{4,3,2,1,0:T(8,128)S(1)}, f32[2,64,128]{2,1,0:T(8,128)S(1)}) custom-call(bf16[512,1536]{1,0:T(8,128)(2,1)S(1)} %copy-done.1, f32[16,64,64]{2,1,0:T(8,128)S(1)} %copy-done.5, f32[8,64,64]{2,1,0:T(8,128)S(1)} %copy-done.6, ...), custom_call_target="tpu_custom_call" | custom-call | flops 1500000000 | bytes 1000000 | tf_op jit(solution)/shard_map/own_kernel/pallas_call | solution.py:473
  8.5 0.0 collective-permute-done.1.pair_ids_ref
  8.5 0.0 collective-permute-done.pair_ref
  8.5 0.0 copy-done.3
  8.5 0.0 copy-start.2
  8.5 1.4 %pair_kernel.1 = (f32[160,512]{1,0:T(8,128)S(1)}, bf16[32,1024]{1,0:T(8,128)(2,1)S(1)}) custom-call(bf16[8,48,512]{2,1,0:T(8,128)(2,1)S(1)} %collective-permute-done.pair_ref, s32[8,48]{1,0:T(8,128)S(1)} %collective-permute-done.1.pair_ids_ref, s32[8,48]{1,0:T(8,128)S(1)} %get-tuple-element.25.ids_ref, ...), custom_call_target="tpu_custom_call" | custom-call | flops 300000000 | bytes 1000000 | tf_op jit(solution)/shard_map/pair_kernel/pallas_call | solution.py:473
  9.9 0.7 %collective-permute-done.2.cross_ref = bf16[200,512]{1,0:T(8,128)(2,1)S(1)} collective-permute-done((bf16[200,512]{1,0:T(8,128)(2,1)S(1)}, bf16[200,512]{1,0:T(8,128)(2,1)S(1)}, u32[]{:S(2)}, u32[]{:S(2)}) %collective-permute-start.2) | collective-permute-done | bytes 204832 | tf_op jit(solution)/shard_map/ppermute | solution.py:508
  10.6 0.0 copy-start
  10.6 0.1 edge_kernel.1
  10.7 1.8 %collective-permute-start.3 = (bf16[72,512]{1,0:T(8,128)(2,1)S(1)}, bf16[72,512]{1,0:T(8,128)(2,1)S(1)}, u32[]{:S(2)}, u32[]{:S(2)}) collective-permute-start(bf16[72,512]{1,0:T(8,128)(2,1)S(1)} %get-tuple-element.30), channel_id=1, source_target_pairs={{0,1},{1,0},{2,3},{3,2},{4,5},{5,4},{6,7},{7,6},{8,9},{9,8},{10,11... | collective-permute-start | bytes 221192 | tf_op jit(solution)/shard_map/ppermute | solution.py:533
  12.5 5.8 %collective-permute-start.4 = (bf16[72,512]{1,0:T(8,128)(2,1)S(1)}, bf16[72,512]{1,0:T(8,128)(2,1)S(1)}, u32[]{:S(2)}, u32[]{:S(2)}) collective-permute-start(bf16[72,512]{1,0:T(8,128)(2,1)S(1)} %get-tuple-element.31), channel_id=1, source_target_pairs={{0,15},{1,2},{2,1},{3,4},{4,3},{5,6},{6,5},{7,8},{8,7},{9,10},{10,... | collective-permute-start | bytes 221192 | tf_op jit(solution)/shard_map/ppermute | solution.py:534
  18.3 1.4 %cross_kernel.1 = (f32[160,512]{1,0:T(8,128)S(1)}, bf16[32,1024]{1,0:T(8,128)(2,1)S(1)}) custom-call(bf16[200,512]{1,0:T(8,128)(2,1)S(1)} %collective-permute-done.2.cross_ref, f32[16,128]{1,0:T(8,128)S(1)} %get-tuple-element.32.ids_ref, bf16[2,5,32,1536]{3,2,1,0:T(8,128)(2,1)S(1)} %get-tuple-element.27.inside_ref, bf16[512,1536]{1,0:T(8,128)(2,1)S(1)} %copy-done.1, ...), custom_call_target="tpu_custom_call" | custom-call | flops 300000000 | bytes 1000000 | tf_op jit(solution)/shard_map/cross_kernel/pallas_call | solution.py:473
  19.7 0.0 copy-done.2
  19.7 0.0 copy-done
  19.7 1.1 %sums_kernel.1 = (f32[8,1024]{1,0:T(8,128)S(1)}, f32[8,1536]{1,0:T(8,128)S(1)}) custom-call(bf16[2048,1024]{1,0:T(8,128)(2,1)S(1)} %copy-done, bf16[1024,1536]{1,0:T(8,128)(2,1)S(1)} %copy-done.2, bf16[32,1024]{1,0:T(8,128)(2,1)S(1)} %get-tuple-element.36.after_ref.cross_edge_ref), custom_call_target="tpu_custom_call" | custom-call | flops 300000000 | bytes 1000000 | tf_op jit(solution)/shard_map/sums_kernel/pallas_call | solution.py:473
  20.8 0.0 collective-permute-done.3.inner_ref
  20.8 0.0 collective-permute-done.4.outer_ref
  20.8 3.0 %final_kernel.1 = (bf16[8,48,512]{2,1,0:T(8,128)(2,1)}, bf16[96,1024]{1,0:T(8,128)(2,1)S(1)}, bf16[96,1024]{1,0:T(8,128)(2,1)S(1)}) custom-call(bf16[8,48,512]{2,1,0:T(8,128)(2,1)S(1)} %get-tuple-element.24.tok_ref, bf16[72,512]{1,0:T(8,128)(2,1)S(1)} %collective-permute-done.3.inner_ref, bf16[72,512]{1,0:T(8,128)(2,1)S(1)} %collective-permute-done.4.outer_ref, ...), custom_call_target="tpu_custom_call" | custom-call | flops 1000000000 | bytes 1000000 | tf_op jit(solution)/shard_map/final_kernel/pallas_call | solution.py:473
  23.8 0.0 copy-start.4
  23.8 1.6 %collective-permute-start.5 = (bf16[96,1024]{1,0:T(8,128)(2,1)S(1)}, bf16[96,1024]{1,0:T(8,128)(2,1)S(1)}, u32[]{:S(2)}, u32[]{:S(2)}) collective-permute-start(bf16[96,1024]{1,0:T(8,128)(2,1)S(1)} %get-tuple-element.42.kv_ref), channel_id=1, source_target_pairs={{0,16},{16,0},{32,48},{48,32},{64,80},{80,64},{96,112},{112,96},{1... | collective-permute-start | bytes 589832 | tf_op jit(solution)/shard_map/ppermute | solution.py:563
  25.5 0.5 %query_kernel.1 = (bf16[96,512]{1,0:T(8,128)(2,1)S(1)}, f32[6,32,128]{2,1,0:T(8,128)S(1)}) custom-call(bf16[96,1024]{1,0:T(8,128)(2,1)S(1)} %get-tuple-element.41.merged_ref, bf16[96,1024]{1,0:T(8,128)(2,1)S(1)} %get-tuple-element.42.kv_ref, f32[2,64,128]{2,1,0:T(8,128)S(1)} %get-tuple-element.43.bias_ref, bf16[1024,1536]{1,0:T(8,128)(2,1)S(1)} %copy-done.2, ...), custom_call_target="tpu_custom_call" | custom-call | flops 1000000000 | bytes 1000000 | tf_op jit(solution)/shard_map/query_kernel/pallas_call | solution.py:473
  26.0 0.5 %collective-permute-done.5.other_ref = bf16[96,1024]{1,0:T(8,128)(2,1)S(1)} collective-permute-done((bf16[96,1024]{1,0:T(8,128)(2,1)S(1)}, bf16[96,1024]{1,0:T(8,128)(2,1)S(1)}, u32[]{:S(2)}, u32[]{:S(2)}) %collective-permute-start.5) | collective-permute-done | bytes 196640 | tf_op jit(solution)/shard_map/ppermute | solution.py:563
  26.5 0.0 copy-done.4
  26.5 1.4 %level_two_kernel.1 = bf16[4,24,1024]{2,1,0:T(8,128)(2,1)} custom-call(bf16[96,512]{1,0:T(8,128)(2,1)S(1)} %get-tuple-element.44.query_ref, f32[6,32,128]{2,1,0:T(8,128)S(1)} %get-tuple-element.45.score_ref, bf16[96,1024]{1,0:T(8,128)(2,1)S(1)} %get-tuple-element.42.kv_ref, bf16[96,1024]{1,0:T(8,128)(2,1)S(1)} %collective-permute-done.5.other_ref, ...), custom_call_target="tpu_custom_call" | custom-call | flops 1000000000 | bytes 1000000 | tf_op jit(solution)/shard_map/level_two_kernel/pallas_call | solution.py:473
Async XLA Ops:
  0.6 4.5 %copy-start.7 = (s32[8,48]{1,0:T(8,128)S(1)}, s32[8,48]{1,0:T(8,128)}, u32[]{:S(2)}) copy-start(s32[8,48]{1,0:T(8,128)} %ids_hbm.1) | copy-start | bytes 4612
  0.6 6.8 %copy-start.1 = (bf16[512,1536]{1,0:T(8,128)(2,1)S(1)}, bf16[512,1536]{1,0:T(8,128)(2,1)}, u32[]{:S(2)}) copy-start(bf16[512,1536]{1,0:T(8,128)(2,1)} %qkv_ref.7) | copy-start | bytes 4718596
  0.7 6.8 %copy-start.6 = (f32[8,64,64]{2,1,0:T(8,128)S(1)}, f32[8,64,64]{2,1,0:T(8,128)}, u32[]{:S(2)}) copy-start(f32[8,64,64]{2,1,0:T(8,128)} %two_ref.4) | copy-start | bytes 393220
  0.7 6.8 %copy-start.5 = (f32[16,64,64]{2,1,0:T(8,128)S(1)}, f32[16,64,64]{2,1,0:T(8,128)}, u32[]{:S(2)}) copy-start(f32[16,64,64]{2,1,0:T(8,128)} %one_ref.1) | copy-start | bytes 786436
  0.7 7.8 %collective-permute-start = (bf16[8,48,512]{2,1,0:T(8,128)(2,1)}, bf16[8,48,512]{2,1,0:T(8,128)(2,1)S(1)}, u32[]{:S(2)}, u32[]{:S(2)}) collective-permute-start(bf16[8,48,512]{2,1,0:T(8,128)(2,1)} %tok_hbm.1), channel_id=1, source_target_pairs={{0,16},{16,0},{32,48},{48,32},{64,80},{80,64},{96,112},{112,96},{1... | collective-permute-start | bytes 1179656 | tf_op jit(solution)/shard_map/ppermute | solution.py:497
  5.0 3.5 %copy-start.3 = (bf16[512,512]{1,0:T(8,128)(2,1)S(1)}, bf16[512,512]{1,0:T(8,128)(2,1)}, u32[]{:S(2)}) copy-start(bf16[512,512]{1,0:T(8,128)(2,1)} %out_ref.6) | copy-start | bytes 1572868
  5.1 5.6 %collective-permute-start.2 = (bf16[200,512]{1,0:T(8,128)(2,1)S(1)}, bf16[200,512]{1,0:T(8,128)(2,1)S(1)}, u32[]{:S(2)}, u32[]{:S(2)}) collective-permute-start(bf16[200,512]{1,0:T(8,128)(2,1)S(1)} %get-tuple-element.26), channel_id=1, source_target_pairs={{0,240},{16,32},{32,16},{48,64},{64,48},{80,96},{96,80},{112,128},... | collective-permute-start | bytes 614408 | tf_op jit(solution)/shard_map/ppermute | solution.py:508
  5.2 3.3 %collective-permute-start.1 = (s32[8,48]{1,0:T(8,128)S(1)}, s32[8,48]{1,0:T(8,128)S(1)}, u32[]{:S(2)}, u32[]{:S(2)}) collective-permute-start(s32[8,48]{1,0:T(8,128)S(1)} %copy-done.7), channel_id=1, source_target_pairs={{0,16},{16,0},{32,48},{48,32},{64,80},{80,64},{96,112},{112,96},{1... | collective-permute-start | bytes 4616 | tf_op jit(solution)/shard_map/ppermute | solution.py:498
  8.5 11.2 %copy-start.2 = (bf16[1024,1536]{1,0:T(8,128)(2,1)S(1)}, bf16[1024,1536]{1,0:T(8,128)(2,1)}, u32[]{:S(2)}) copy-start(bf16[1024,1536]{1,0:T(8,128)(2,1)} %two_ref.7) | copy-start | bytes 9437188
  10.6 9.1 %copy-start = (bf16[2048,1024]{1,0:T(8,128)(2,1)S(1)}, bf16[2048,1024]{1,0:T(8,128)(2,1)}, u32[]{:S(2)}) copy-start(bf16[2048,1024]{1,0:T(8,128)(2,1)} %merge_ref.3) | copy-start | bytes 12582916
  10.7 10.1 %collective-permute-start.3 = (bf16[72,512]{1,0:T(8,128)(2,1)S(1)}, bf16[72,512]{1,0:T(8,128)(2,1)S(1)}, u32[]{:S(2)}, u32[]{:S(2)}) collective-permute-start(bf16[72,512]{1,0:T(8,128)(2,1)S(1)} %get-tuple-element.30), channel_id=1, source_target_pairs={{0,1},{1,0},{2,3},{3,2},{4,5},{5,4},{6,7},{7,6},{8,9},{9,8},{10,11... | collective-permute-start | bytes 221192 | tf_op jit(solution)/shard_map/ppermute | solution.py:533
  12.5 8.2 %collective-permute-start.4 = (bf16[72,512]{1,0:T(8,128)(2,1)S(1)}, bf16[72,512]{1,0:T(8,128)(2,1)S(1)}, u32[]{:S(2)}, u32[]{:S(2)}) collective-permute-start(bf16[72,512]{1,0:T(8,128)(2,1)S(1)} %get-tuple-element.31), channel_id=1, source_target_pairs={{0,15},{1,2},{2,1},{3,4},{4,3},{5,6},{6,5},{7,8},{8,7},{9,10},{10,... | collective-permute-start | bytes 221192 | tf_op jit(solution)/shard_map/ppermute | solution.py:534
  23.8 2.7 %copy-start.4 = (bf16[512,1024]{1,0:T(8,128)(2,1)S(1)}, bf16[512,1024]{1,0:T(8,128)(2,1)}, u32[]{:S(2)}) copy-start(bf16[512,1024]{1,0:T(8,128)(2,1)} %out_ref.7) | copy-start | bytes 3145732
  23.8 2.7 %collective-permute-start.5 = (bf16[96,1024]{1,0:T(8,128)(2,1)S(1)}, bf16[96,1024]{1,0:T(8,128)(2,1)S(1)}, u32[]{:S(2)}, u32[]{:S(2)}) collective-permute-start(bf16[96,1024]{1,0:T(8,128)(2,1)S(1)} %get-tuple-element.42.kv_ref), channel_id=1, source_target_pairs={{0,16},{16,0},{32,48},{48,32},{64,80},{80,64},{96,112},{112,96},{1... | collective-permute-start | bytes 589832 | tf_op jit(solution)/shard_map/ppermute | solution.py:563

commit v4 on v3

--- a/solution.py
+++ b/solution.py
@@ -40,6 +40,15 @@
     return mean, lax.rsqrt(var + EPSILON)
 
 
+def with_ones(x):
+    return jnp.concatenate([x, jnp.ones((16, x.shape[1]), x.dtype)], axis=0)
+
+
+def after_norm(total, mean, factor):
+    count = mean.shape[0]
+    return (total[0:count] - mean * total[count : count + 1]) * factor
+
+
 def lanes_to(x, width):
     return jnp.concatenate([x, jnp.zeros((x.shape[0], width - x.shape[1]), x.dtype)], axis=1)
 
@@ -59,32 +68,31 @@
     return copies
 
 
-def load_kernel(tok_hbm, ids_hbm, cross_ref, tok_ref, ids_ref, sems):
+def load_kernel(tok_hbm, ids_hbm, cross_ref, pair_ref, tok_ref, ids_ref, sems):
     copies = start_all([(ids_hbm, ids_ref), (tok_hbm, tok_ref)], sems)
     copies[0].wait()
-    ids = lanes_to(ids_ref[...].astype(F32), D1)
-    cross_ref[4 * COLS :] = jnp.where(lat_parity() == 0, ids, pltpu.roll(ids, 4, 0)).astype(BF)
+    upper = lanes_to(ids_ref[...].astype(F32), D1)
+    lower = pltpu.roll(upper, 4, 0)
+    even = lat_parity() == 0
+    cross_ref[4 * COLS :] = jnp.where(even, upper, lower).astype(BF)
+    pair_ref[4 * COLS :] = jnp.where(even, lower, upper).astype(BF)
     copies[1].wait()
     for r in range(4):
         cross_ref[r * COLS : (r + 1) * COLS] = tok_ref[4 * lat_parity() + r]
-
-
-def next_row(r):
-    return 4 * lat_parity() + r
+        pair_ref[r * COLS : (r + 1) * COLS] = tok_ref[4 - 4 * lat_parity() + r]
 
 
 def edge_kernel(
-    tok_ref, ids_ref, pair_ref, pair_ids_ref, cross_ref, after_ref, inner_ref, outer_ref, all_ids_ref
+    tok_ref, ids_ref, pair_ref, cross_ref, after_ref, inner_ref, outer_ref, all_ids_ref
 ):
     first = [tok_ref[r, 0:16].astype(F32)[0:4] for r in range(ROWS)]
-    first += [pair_ref[next_row(r), 0:16].astype(F32)[0:4] for r in range(4)]
+    first += [pair_ref[COLS * r : COLS * r + 16].astype(F32)[0:4] for r in range(4)]
     first += [cross_ref[COLS * r : COLS * r + 16].astype(F32)[0:4] for r in range(4)]
     last = [tok_ref[r, 32:48].astype(F32)[12:16] for r in range(ROWS)]
-    last += [pair_ref[next_row(r), 32:48].astype(F32)[12:16] for r in range(4)]
+    last += [pair_ref[COLS * r + 32 : COLS * r + 48].astype(F32)[12:16] for r in range(4)]
     last += [cross_ref[COLS * r + 32 : COLS * r + 48].astype(F32)[12:16] for r in range(4)]
     own = lanes_to(ids_ref[...].astype(F32), 128)
-    pair = lanes_to(pair_ids_ref[...].astype(F32), 128)
-    pair = jnp.where(lat_parity() == 0, pair, pltpu.roll(pair, 4, 0))
+    pair = pair_ref[4 * COLS :, 0:128].astype(F32)
     cross = cross_ref[4 * COLS :, 0:128].astype(F32)
     halo = jnp.concatenate([pair[0:4], cross[0:4]], axis=0)
     all_ids_ref[...] = jnp.concatenate([own, halo], axis=0)
@@ -245,15 +253,13 @@
 
 
 def pair_kernel(
-    pair_ref, pair_ids_ref, ids_ref, inside_ref, qkv_ref, bias_ref, out_ref, add_out, edge_out,
-    normed,
+    pair_ref, ids_ref, inside_ref, qkv_ref, bias_ref, out_ref, add_out, edge_out, normed
 ):
     even = lat_parity() == 0
     own = lanes_to(ids_ref[...].astype(F32), 128)
-    pair = lanes_to(pair_ids_ref[...].astype(F32), 128)
+    pair = pair_ref[4 * COLS :, 0:128].astype(F32)
     own = jnp.where(even, pltpu.roll(own, 4, 0), own)
-    pair = jnp.where(even, pair, pltpu.roll(pair, 4, 0))
-    rows = [pair_ref[next_row(r)].astype(F32) for r in range(4)]
+    rows = [pair_ref[COLS * r : COLS * r + COLS].astype(F32) for r in range(4)]
     add_out[...], edge_out[...] = half_inner(
         1 - lat_parity(), rows, own[0:4], pair[0:4], inside_ref, qkv_ref, bias_ref, out_ref, normed
     )
@@ -273,7 +279,6 @@
 def final_kernel(
     tok_ref, inner_ref, outer_ref, ids_ref, qkv_ref, bias_ref, out_ref, own_edge_ref,
     pair_edge_ref, cross_edge_ref, pair_add_ref, cross_add_ref, merge_ref, two_ref,
-    merge_sum_ref, two_sum_ref,
     one_out, merged_out, kv_out,
     level, parts, done, sem,
 ):
@@ -379,25 +384,19 @@
     order = [(i, slice(8 * w, 8 * w + 8)) for w in range(3) for i in range(4)]
     mean = jnp.concatenate([means[i][at] for i, at in order], axis=0)
     factor = jnp.concatenate([factors[i][at] for i, at in order], axis=0)
-    total = jnp.zeros((96, D2), F32)
+    total = jnp.zeros((112, D2), F32)
     for n in range(4):
         total += jnp.dot(
-            parts[n].reshape(96, D1).astype(BF),
+            with_ones(parts[n].reshape(96, D1).astype(BF)),
             merge_ref[n * D1 : (n + 1) * D1, :],
             preferred_element_type=F32,
         )
-    merged = ((total - mean * merge_sum_ref[0:1]) * factor).astype(BF)
+    merged = after_norm(total, mean, factor).astype(BF)
     merged_out[...] = merged
     mean, factor = row_stats([merged.astype(F32)])
-    total = jnp.dot(merged, two_ref[:, 512:], preferred_element_type=F32)
-    kv_out[...] = ((total - mean * two_sum_ref[0:1, 512:]) * factor).astype(BF)
+    total = jnp.dot(with_ones(merged), two_ref[:, 512:], preferred_element_type=F32)
+    kv_out[...] = after_norm(total, mean, factor).astype(BF)
     store.wait()
-
-
-def sums_kernel(merge_ref, two_ref, after_ref, merge_out, two_out):
-    ones = jnp.ones((16, 4 * D1), BF)
-    merge_out[...] = jnp.dot(ones, merge_ref[...], preferred_element_type=F32)[0:8]
-    two_out[...] = jnp.dot(ones[:, 0:D2], two_ref[...], preferred_element_type=F32)[0:8]
 
 
 TWO_UNITS = [(w, g) for w in range(3) for g in range(2)]
@@ -418,11 +417,11 @@
     ]
 
 
-def query_kernel(merged_ref, kv_ref, bias_ref, two_ref, two_sum_ref, query_out, score_out):
+def query_kernel(merged_ref, kv_ref, bias_ref, two_ref, query_out, score_out):
     merged = merged_ref[...]
     mean, factor = row_stats([merged.astype(F32)])
-    total = jnp.dot(merged, two_ref[:, :512], preferred_element_type=F32)
-    q = ((total - mean * two_sum_ref[0:1, :512]) * factor).astype(BF)
+    total = jnp.dot(with_ones(merged), two_ref[:, :512], preferred_element_type=F32)
+    q = after_norm(total, mean, factor).astype(BF)
     query_out[...] = q
     for n, s in enumerate(scores_two(kv_ref, q, [bias_ref[g, 0:32] for g in range(2)])):
         score_out[n] = s
@@ -494,11 +493,9 @@
     lon_inner = [(i, i ^ 1) for i in range(lons)]
     lon_outer = [(i, (i + (1 if i % 2 else -1)) % lons) for i in range(lons)]
 
-    pair = lax.ppermute(tokens, "lat", lat_inner)
-    pair_ids = lax.ppermute(region_ids, "lat", lat_inner)
-    cross, tokens, region_ids = call(
+    cross, pair, tokens, region_ids = call(
         load_kernel,
-        [((200, D1), BF), ((ROWS, COLS, D1), BF), ((ROWS, COLS), jnp.int32)],
+        [((200, D1), BF), ((200, D1), BF), ((ROWS, COLS, D1), BF), ((ROWS, COLS), jnp.int32)],
         [tokens, region_ids],
         hbm=2,
         scratch=[pltpu.SemaphoreType.DMA((2,))],
@@ -506,6 +503,7 @@
         us=4.0,
     )
     cross = lax.ppermute(cross, "lat", lat_outer)
+    pair = lax.ppermute(pair, "lat", lat_inner)
     inside, own_edge, table_one, table_side, table_two = call(
         own_kernel,
         [
@@ -520,14 +518,14 @@
     pair_add, pair_edge = call(
         pair_kernel,
         [((INSIDE * 32, D1), F32), ((32, 2 * D1), BF)],
-        [pair, pair_ids, region_ids, inside, qkv_one, table_one, out_one],
+        [pair, region_ids, inside, qkv_one, table_one, out_one],
         scratch=[half_shape],
         us=0.3,
     )
     inner, outer, ids = call(
         edge_kernel,
         [((72, D1), BF), ((72, D1), BF), ((2 * ROWS, 128), F32)],
-        [tokens, region_ids, pair, pair_ids, cross, pair_add],
+        [tokens, region_ids, pair, cross, pair_add],
         mib=4,
     )
     inner = lax.ppermute(inner, "lon", lon_inner)
@@ -539,18 +537,12 @@
         scratch=[half_shape],
         us=0.3,
     )
-    merge_sum, two_sum = call(
-        sums_kernel,
-        [((8, D2), F32), ((8, 1536), F32)],
-        [merge_proj, qkv_two, cross_edge],
-        us=0.3,
-    )
     level_one, merged, kv = call(
         final_kernel,
         [((ROWS, COLS, D1), BF), ((96, D2), BF), ((96, 1024), BF)],
         [
             tokens, inner, outer, ids, qkv_one, table_side, out_one, own_edge, pair_edge,
-            cross_edge, pair_add, cross_add, merge_proj, qkv_two, merge_sum, two_sum,
+            cross_edge, pair_add, cross_add, merge_proj, qkv_two,
         ],
         scratch=[
             pltpu.VMEM((4, ROWS, COLS, 128), F32),
@@ -564,7 +556,7 @@
     query, scores = call(
         query_kernel,
         [((96, 512), BF), ((6, 32, 128), F32)],
-        [merged, kv, table_two, qkv_two, two_sum],
+        [merged, kv, table_two, qkv_two],
     )
     (level_two,) = call(
         level_two_kernel,

time: 28.1 us -> 27.4 us (0.975)
  waiting for transfers between devices: 1.26 us -> 3.97 us
  starting transfers between devices: 15 us -> 13.2 us
  Pallas kernels: 10.9 us -> 9.41 us
    ppermute x1, waiting for transfers between devices: 0.72 us -> 3.03 us  [on_device(): cross = lax.ppermute(cross, 'lat', lat_outer)]
    ppermute x2 -> x1, starting transfers between devices: 5.63 us -> 3.33 us  [on_device(): pair = lax.ppermute(pair, 'lat', lat_inner)]
    ppermute x1, starting transfers between devices: 1.63 us -> 3.26 us  [on_device(): other_kv = lax.ppermute(kv, 'lat', lat_inner)]
    pallas_call x9 -> x8, Pallas kernels: 10.9 us -> 9.41 us  [call(): pl.pallas_call(kernel, out_shape=shapes, in_specs=place, out_specs=[pl.Bl...]
    ppermute x1, starting transfers between devices: 1.82 us -> 1.08 us  [on_device(): inner = lax.ppermute(inner, 'lon', lon_inner)]
    ppermute x1, waiting for transfers between devices: 0.01 us -> 0.37 us  [on_device(): outer = lax.ppermute(outer, 'lon', lon_outer)]
    ppermute x1, starting transfers between devices: 5.82 us -> 5.52 us  [on_device(): outer = lax.ppermute(outer, 'lon', lon_outer)]
  transfers between devices with their start and end apart: 6 -> 5, of which waited for: 2 -> 3; matrix products, arithmetic and copies ran while one was open for 0% -> 0% of each run, Pallas kernels for 23% -> 16%
where the time goes in v4:
time: 27.4 us; the launch traced here: 27.3 us
  starting transfers between devices  13.2 us (48%)
  Pallas kernels  9.41 us (34%)
  waiting for transfers between devices  3.97 us (14%)
  between operations  0.72 us (3%)
    pallas_call x8, Pallas kernels, call(): pl.pallas_call(kernel, out_shape=shapes, in_specs=place, out_specs=[pl.Bl...  9.41 us
    ppermute x1, starting transfers between devices, on_device(): outer = lax.ppermute(outer, 'lon', lon_outer)  5.52 us
    ppermute x1, starting transfers between devices, on_device(): pair = lax.ppermute(pair, 'lat', lat_inner)  3.33 us
    ppermute x1, starting transfers between devices, on_device(): other_kv = lax.ppermute(kv, 'lat', lat_inner)  3.26 us
    ppermute x1, waiting for transfers between devices, on_device(): cross = lax.ppermute(cross, 'lat', lat_outer)  3.03 us
    ppermute x1, starting transfers between devices, on_device(): inner = lax.ppermute(inner, 'lon', lon_inner)  1.08 us
  transfers between devices with their start and end apart: 5, of which 3 were waited for; matrix products, arithmetic and copies ran while one was open for 0% of the time, Pallas kernels for 16%

profile of v4, /device:TPU:1, one launch (start us, length us, event | category | flops | bytes accessed | tf_op | source)
XLA Modules:
  0.0 27.3 jit_solution(8846763300974864456)
XLA Ops:
  0.6 0.0 copy-start
  0.6 0.0 copy-start.6
  0.7 0.0 copy-start.5
  0.7 1.2 %load_kernel.1 = (bf16[200,512]{1,0:T(8,128)(2,1)S(1)}, bf16[200,512]{1,0:T(8,128)(2,1)S(1)}, bf16[8,48,512]{2,1,0:T(8,128)(2,1)S(1)}, s32[8,48]{1,0:T(8,128)S(1)}) custom-call(bf16[8,48,512]{2,1,0:T(8,128)(2,1)} %tok_hbm.1, s32[8,48]{1,0:T(8,128)} %ids_hbm.1), custom_call_target="tpu_custom_call" | custom-call | flops 4000000000 | bytes 1000000 | tf_op jit(solution)/shard_map/load_kernel/pallas_call | solution.py:472
  1.9 0.0 copy-start.1
  1.9 3.3 %collective-permute-start = (bf16[200,512]{1,0:T(8,128)(2,1)S(1)}, bf16[200,512]{1,0:T(8,128)(2,1)S(1)}, u32[]{:S(2)}, u32[]{:S(2)}) collective-permute-start(bf16[200,512]{1,0:T(8,128)(2,1)S(1)} %get-tuple-element.25), channel_id=1, source_target_pairs={{0,16},{16,0},{32,48},{48,32},{64,80},{80,64},{96,112},{112,96},{1... | collective-permute-start | bytes 614408 | tf_op jit(solution)/shard_map/ppermute | solution.py:506
  5.2 0.0 collective-permute-start.1
  5.2 0.0 copy-done
  5.2 0.0 copy-done.6
  5.2 0.0 copy-done.5
  5.2 1.0 %own_kernel.1 = (bf16[2,5,32,1536]{3,2,1,0:T(8,128)(2,1)S(1)}, bf16[64,1536]{1,0:T(8,128)(2,1)S(1)}, f32[2,4,64,128]{3,2,1,0:T(8,128)S(1)}, f32[2,2,2,64,128]{4,3,2,1,0:T(8,128)S(1)}, f32[2,64,128]{2,1,0:T(8,128)S(1)}) custom-call(bf16[512,1536]{1,0:T(8,128)(2,1)S(1)} %copy-done, f32[16,64,64]{2,1,0:T(8,128)S(1)} %copy-done.5, f32[8,64,64]{2,1,0:T(8,128)S(1)} %copy-done.6, ...), custom_call_target="tpu_custom_call" | custom-call | flops 1500000000 | bytes 1000000 | tf_op jit(solution)/shard_map/own_kernel/pallas_call | solution.py:472
  6.3 0.0 collective-permute-done.pair_ref
  6.3 0.0 copy-done.1
  6.3 0.0 copy-start.3
  6.3 1.4 %pair_kernel.1 = (f32[160,512]{1,0:T(8,128)S(1)}, bf16[32,1024]{1,0:T(8,128)(2,1)S(1)}) custom-call(bf16[200,512]{1,0:T(8,128)(2,1)S(1)} %collective-permute-done.pair_ref, s32[8,48]{1,0:T(8,128)S(1)} %get-tuple-element.24.ids_ref, bf16[2,5,32,1536]{3,2,1,0:T(8,128)(2,1)S(1)} %get-tuple-element.27.inside_ref, bf16[512,1536]{1,0:T(8,128)(2,1)S(1)} %copy-done, ...), custom_call_target="tpu_custom_call" | custom-call | flops 300000000 | bytes 1000000 | tf_op jit(solution)/shard_map/pair_kernel/pallas_call | solution.py:472
  7.7 3.0 %collective-permute-done.1.cross_ref = bf16[200,512]{1,0:T(8,128)(2,1)S(1)} collective-permute-done((bf16[200,512]{1,0:T(8,128)(2,1)S(1)}, bf16[200,512]{1,0:T(8,128)(2,1)S(1)}, u32[]{:S(2)}, u32[]{:S(2)}) %collective-permute-start.1) | collective-permute-done | bytes 204832 | tf_op jit(solution)/shard_map/ppermute | solution.py:505
  10.7 0.0 copy-start.2
  10.7 0.1 edge_kernel.1
  10.8 1.1 %collective-permute-start.2 = (bf16[72,512]{1,0:T(8,128)(2,1)S(1)}, bf16[72,512]{1,0:T(8,128)(2,1)S(1)}, u32[]{:S(2)}, u32[]{:S(2)}) collective-permute-start(bf16[72,512]{1,0:T(8,128)(2,1)S(1)} %get-tuple-element.30), channel_id=1, source_target_pairs={{0,1},{1,0},{2,3},{3,2},{4,5},{5,4},{6,7},{7,6},{8,9},{9,8},{10,11... | collective-permute-start | bytes 221192 | tf_op jit(solution)/shard_map/ppermute | solution.py:531
  11.9 5.5 %collective-permute-start.3 = (bf16[72,512]{1,0:T(8,128)(2,1)S(1)}, bf16[72,512]{1,0:T(8,128)(2,1)S(1)}, u32[]{:S(2)}, u32[]{:S(2)}) collective-permute-start(bf16[72,512]{1,0:T(8,128)(2,1)S(1)} %get-tuple-element.31), channel_id=1, source_target_pairs={{0,15},{1,2},{2,1},{3,4},{4,3},{5,6},{6,5},{7,8},{8,7},{9,10},{10,... | collective-permute-start | bytes 221192 | tf_op jit(solution)/shard_map/ppermute | solution.py:532
  17.4 1.4 %cross_kernel.1 = (f32[160,512]{1,0:T(8,128)S(1)}, bf16[32,1024]{1,0:T(8,128)(2,1)S(1)}) custom-call(bf16[200,512]{1,0:T(8,128)(2,1)S(1)} %collective-permute-done.1.cross_ref, f32[16,128]{1,0:T(8,128)S(1)} %get-tuple-element.32.ids_ref, bf16[2,5,32,1536]{3,2,1,0:T(8,128)(2,1)S(1)} %get-tuple-element.27.inside_ref, bf16[512,1536]{1,0:T(8,128)(2,1)S(1)} %copy-done, ...), custom_call_target="tpu_custom_call" | custom-call | flops 300000000 | bytes 1000000 | tf_op jit(solution)/shard_map/cross_kernel/pallas_call | solution.py:472
  18.7 0.0 collective-permute-done.2.inner_ref
  18.7 0.4 %collective-permute-done.3.outer_ref = bf16[72,512]{1,0:T(8,128)(2,1)S(1)} collective-permute-done((bf16[72,512]{1,0:T(8,128)(2,1)S(1)}, bf16[72,512]{1,0:T(8,128)(2,1)S(1)}, u32[]{:S(2)}, u32[]{:S(2)}) %collective-permute-start.3) | collective-permute-done | bytes 73760 | tf_op jit(solution)/shard_map/ppermute | solution.py:532
  19.1 0.0 copy-done.3
  19.1 0.0 copy-done.2
  19.1 2.4 %final_kernel.1 = (bf16[8,48,512]{2,1,0:T(8,128)(2,1)}, bf16[96,1024]{1,0:T(8,128)(2,1)S(1)}, bf16[96,1024]{1,0:T(8,128)(2,1)S(1)}) custom-call(bf16[8,48,512]{2,1,0:T(8,128)(2,1)S(1)} %get-tuple-element.23.tok_ref, bf16[72,512]{1,0:T(8,128)(2,1)S(1)} %collective-permute-done.2.inner_ref, bf16[72,512]{1,0:T(8,128)(2,1)S(1)} %collective-permute-done.3.outer_ref, ...), custom_call_target="tpu_custom_call" | custom-call | flops 1000000000 | bytes 1000000 | tf_op jit(solution)/shard_map/final_kernel/pallas_call | solution.py:472
  21.5 0.0 copy-start.4
  21.6 3.3 %collective-permute-start.4 = (bf16[96,1024]{1,0:T(8,128)(2,1)S(1)}, bf16[96,1024]{1,0:T(8,128)(2,1)S(1)}, u32[]{:S(2)}, u32[]{:S(2)}) collective-permute-start(bf16[96,1024]{1,0:T(8,128)(2,1)S(1)} %get-tuple-element.40.kv_ref), channel_id=1, source_target_pairs={{0,16},{16,0},{32,48},{48,32},{64,80},{80,64},{96,112},{112,96},{1... | collective-permute-start | bytes 589832 | tf_op jit(solution)/shard_map/ppermute | solution.py:555
  24.8 0.5 %query_kernel.1 = (bf16[96,512]{1,0:T(8,128)(2,1)S(1)}, f32[6,32,128]{2,1,0:T(8,128)S(1)}) custom-call(bf16[96,1024]{1,0:T(8,128)(2,1)S(1)} %get-tuple-element.39.merged_ref, bf16[96,1024]{1,0:T(8,128)(2,1)S(1)} %get-tuple-element.40.kv_ref, f32[2,64,128]{2,1,0:T(8,128)S(1)} %get-tuple-element.41.bias_ref, bf16[1024,1536]{1,0:T(8,128)(2,1)S(1)} %copy-done.3), custom_call_target="tpu_custom_call" | custom-call | flops 1000000000 | bytes 1000000 | tf_op jit(solution)/shard_map/query_kernel/pallas_call | solution.py:472
  25.4 0.5 %collective-permute-done.4.other_ref = bf16[96,1024]{1,0:T(8,128)(2,1)S(1)} collective-permute-done((bf16[96,1024]{1,0:T(8,128)(2,1)S(1)}, bf16[96,1024]{1,0:T(8,128)(2,1)S(1)}, u32[]{:S(2)}, u32[]{:S(2)}) %collective-permute-start.4) | collective-permute-done | bytes 196640 | tf_op jit(solution)/shard_map/ppermute | solution.py:555
  25.9 0.0 copy-done.4
  25.9 1.4 %level_two_kernel.1 = bf16[4,24,1024]{2,1,0:T(8,128)(2,1)} custom-call(bf16[96,512]{1,0:T(8,128)(2,1)S(1)} %get-tuple-element.42.query_ref, f32[6,32,128]{2,1,0:T(8,128)S(1)} %get-tuple-element.43.score_ref, bf16[96,1024]{1,0:T(8,128)(2,1)S(1)} %get-tuple-element.40.kv_ref, bf16[96,1024]{1,0:T(8,128)(2,1)S(1)} %collective-permute-done.4.other_ref, ...), custom_call_target="tpu_custom_call" | custom-call | flops 1000000000 | bytes 1000000 | tf_op jit(solution)/shard_map/level_two_kernel/pallas_call | solution.py:472
Async XLA Ops:
  0.6 4.6 %copy-start = (bf16[512,1536]{1,0:T(8,128)(2,1)S(1)}, bf16[512,1536]{1,0:T(8,128)(2,1)}, u32[]{:S(2)}) copy-start(bf16[512,1536]{1,0:T(8,128)(2,1)} %qkv_ref.7) | copy-start | bytes 4718596
  0.6 4.6 %copy-start.6 = (f32[8,64,64]{2,1,0:T(8,128)S(1)}, f32[8,64,64]{2,1,0:T(8,128)}, u32[]{:S(2)}) copy-start(f32[8,64,64]{2,1,0:T(8,128)} %two_ref.3) | copy-start | bytes 393220
  0.7 4.6 %copy-start.5 = (f32[16,64,64]{2,1,0:T(8,128)S(1)}, f32[16,64,64]{2,1,0:T(8,128)}, u32[]{:S(2)}) copy-start(f32[16,64,64]{2,1,0:T(8,128)} %one_ref.1) | copy-start | bytes 786436
  1.9 4.4 %copy-start.1 = (bf16[512,512]{1,0:T(8,128)(2,1)S(1)}, bf16[512,512]{1,0:T(8,128)(2,1)}, u32[]{:S(2)}) copy-start(bf16[512,512]{1,0:T(8,128)(2,1)} %out_ref.6) | copy-start | bytes 1572868
  1.9 4.4 %collective-permute-start = (bf16[200,512]{1,0:T(8,128)(2,1)S(1)}, bf16[200,512]{1,0:T(8,128)(2,1)S(1)}, u32[]{:S(2)}, u32[]{:S(2)}) collective-permute-start(bf16[200,512]{1,0:T(8,128)(2,1)S(1)} %get-tuple-element.25), channel_id=1, source_target_pairs={{0,16},{16,0},{32,48},{48,32},{64,80},{80,64},{96,112},{112,96},{1... | collective-permute-start | bytes 614408 | tf_op jit(solution)/shard_map/ppermute | solution.py:506
  5.2 5.5 %collective-permute-start.1 = (bf16[200,512]{1,0:T(8,128)(2,1)S(1)}, bf16[200,512]{1,0:T(8,128)(2,1)S(1)}, u32[]{:S(2)}, u32[]{:S(2)}) collective-permute-start(bf16[200,512]{1,0:T(8,128)(2,1)S(1)} %get-tuple-element.26), channel_id=1, source_target_pairs={{0,240},{16,32},{32,16},{48,64},{64,48},{80,96},{96,80},{112,128},... | collective-permute-start | bytes 614408 | tf_op jit(solution)/shard_map/ppermute | solution.py:505
  6.3 12.8 %copy-start.3 = (bf16[1024,1536]{1,0:T(8,128)(2,1)S(1)}, bf16[1024,1536]{1,0:T(8,128)(2,1)}, u32[]{:S(2)}) copy-start(bf16[1024,1536]{1,0:T(8,128)(2,1)} %two_ref.5) | copy-start | bytes 9437188
  10.7 8.4 %copy-start.2 = (bf16[2048,1024]{1,0:T(8,128)(2,1)S(1)}, bf16[2048,1024]{1,0:T(8,128)(2,1)}, u32[]{:S(2)}) copy-start(bf16[2048,1024]{1,0:T(8,128)(2,1)} %merge_ref.1) | copy-start | bytes 12582916
  10.8 8.0 %collective-permute-start.2 = (bf16[72,512]{1,0:T(8,128)(2,1)S(1)}, bf16[72,512]{1,0:T(8,128)(2,1)S(1)}, u32[]{:S(2)}, u32[]{:S(2)}) collective-permute-start(bf16[72,512]{1,0:T(8,128)(2,1)S(1)} %get-tuple-element.30), channel_id=1, source_target_pairs={{0,1},{1,0},{2,3},{3,2},{4,5},{5,4},{6,7},{7,6},{8,9},{9,8},{10,11... | collective-permute-start | bytes 221192 | tf_op jit(solution)/shard_map/ppermute | solution.py:531
  11.9 7.3 %collective-permute-start.3 = (bf16[72,512]{1,0:T(8,128)(2,1)S(1)}, bf16[72,512]{1,0:T(8,128)(2,1)S(1)}, u32[]{:S(2)}, u32[]{:S(2)}) collective-permute-start(bf16[72,512]{1,0:T(8,128)(2,1)S(1)} %get-tuple-element.31), channel_id=1, source_target_pairs={{0,15},{1,2},{2,1},{3,4},{4,3},{5,6},{6,5},{7,8},{8,7},{9,10},{10,... | collective-permute-start | bytes 221192 | tf_op jit(solution)/shard_map/ppermute | solution.py:532
  21.5 4.3 %copy-start.4 = (bf16[512,1024]{1,0:T(8,128)(2,1)S(1)}, bf16[512,1024]{1,0:T(8,128)(2,1)}, u32[]{:S(2)}) copy-start(bf16[512,1024]{1,0:T(8,128)(2,1)} %out_ref.7) | copy-start | bytes 3145732
  21.6 4.3 %collective-permute-start.4 = (bf16[96,1024]{1,0:T(8,128)(2,1)S(1)}, bf16[96,1024]{1,0:T(8,128)(2,1)S(1)}, u32[]{:S(2)}, u32[]{:S(2)}) collective-permute-start(bf16[96,1024]{1,0:T(8,128)(2,1)S(1)} %get-tuple-element.40.kv_ref), channel_id=1, source_target_pairs={{0,16},{16,0},{32,48},{48,32},{64,80},{80,64},{96,112},{112,96},{1... | collective-permute-start | bytes 589832 | tf_op jit(solution)/shard_map/ppermute | solution.py:555

commit v5 on v4

--- a/solution.py
+++ b/solution.py
@@ -68,18 +68,21 @@
     return copies
 
 
-def load_kernel(tok_hbm, ids_hbm, cross_ref, pair_ref, tok_ref, ids_ref, sems):
-    copies = start_all([(ids_hbm, ids_ref), (tok_hbm, tok_ref)], sems)
+def load_kernel(tok_hbm, ids_hbm, cross_ref, pair_ref, ids_ref, sems):
+    copies = [(ids_hbm, ids_ref)]
+    for r in range(4):
+        row = slice(r * COLS, (r + 1) * COLS)
+        copies.append((tok_hbm.at[4 * lat_parity() + r], cross_ref.at[row]))
+        copies.append((tok_hbm.at[4 - 4 * lat_parity() + r], pair_ref.at[row]))
+    copies = start_all(copies, sems)
     copies[0].wait()
     upper = lanes_to(ids_ref[...].astype(F32), D1)
     lower = pltpu.roll(upper, 4, 0)
     even = lat_parity() == 0
     cross_ref[4 * COLS :] = jnp.where(even, upper, lower).astype(BF)
     pair_ref[4 * COLS :] = jnp.where(even, lower, upper).astype(BF)
-    copies[1].wait()
-    for r in range(4):
-        cross_ref[r * COLS : (r + 1) * COLS] = tok_ref[4 * lat_parity() + r]
-        pair_ref[r * COLS : (r + 1) * COLS] = tok_ref[4 - 4 * lat_parity() + r]
+    for copy in copies[1:]:
+        copy.wait()
 
 
 def edge_kernel(
@@ -493,12 +496,12 @@
     lon_inner = [(i, i ^ 1) for i in range(lons)]
     lon_outer = [(i, (i + (1 if i % 2 else -1)) % lons) for i in range(lons)]
 
-    cross, pair, tokens, region_ids = call(
+    cross, pair, region_ids = call(
         load_kernel,
-        [((200, D1), BF), ((200, D1), BF), ((ROWS, COLS, D1), BF), ((ROWS, COLS), jnp.int32)],
+        [((200, D1), BF), ((200, D1), BF), ((ROWS, COLS), jnp.int32)],
         [tokens, region_ids],
         hbm=2,
-        scratch=[pltpu.SemaphoreType.DMA((2,))],
+        scratch=[pltpu.SemaphoreType.DMA((9,))],
         mib=4,
         us=4.0,
     )

time: 27.4 us -> 27.4 us (level)
  no operation moved by 1% of the time
where the time goes in v5:
time: 27.4 us; the launch traced here: 27.3 us
  starting transfers between devices  13.2 us (48%)
  Pallas kernels  9.42 us (34%)
  waiting for transfers between devices  3.97 us (14%)
  between operations  0.74 us (3%)
    pallas_call x8, Pallas kernels, call(): pl.pallas_call(kernel, out_shape=shapes, in_specs=place, out_specs=[pl.Bl...  9.42 us
    ppermute x1, starting transfers between devices, on_device(): outer = lax.ppermute(outer, 'lon', lon_outer)  5.52 us
    ppermute x1, starting transfers between devices, on_device(): pair = lax.ppermute(pair, 'lat', lat_inner)  3.33 us
    ppermute x1, starting transfers between devices, on_device(): other_kv = lax.ppermute(kv, 'lat', lat_inner)  3.24 us
    ppermute x1, waiting for transfers between devices, on_device(): cross = lax.ppermute(cross, 'lat', lat_outer)  3.03 us
    ppermute x1, starting transfers between devices, on_device(): inner = lax.ppermute(inner, 'lon', lon_inner)  1.08 us
  transfers between devices with their start and end apart: 5, of which 3 were waited for; matrix products, arithmetic and copies ran while one was open for 0% of the time, Pallas kernels for 16%

profile of v5, /device:TPU:1, one launch (start us, length us, event | category | flops | bytes accessed | tf_op | source)
XLA Modules:
  0.0 27.3 jit_solution(10057661959040986580)
XLA Ops:
  0.6 0.0 copy-start.4
  0.6 0.0 copy-start
  0.7 0.0 copy-start.7
  0.7 0.0 copy-start.6
  0.7 1.2 %load_kernel.1 = (bf16[200,512]{1,0:T(8,128)(2,1)S(1)}, bf16[200,512]{1,0:T(8,128)(2,1)S(1)}, s32[8,48]{1,0:T(8,128)S(1)}) custom-call(bf16[8,48,512]{2,1,0:T(8,128)(2,1)} %tok_ref.5, s32[8,48]{1,0:T(8,128)} %ids_hbm.1), custom_call_target="tpu_custom_call" | custom-call | flops 4000000000 | bytes 1000000 | tf_op jit(solution)/shard_map/load_kernel/pallas_call | solution.py:475
  1.9 0.0 copy-start.1
  1.9 3.3 %collective-permute-start = (bf16[200,512]{1,0:T(8,128)(2,1)S(1)}, bf16[200,512]{1,0:T(8,128)(2,1)S(1)}, u32[]{:S(2)}, u32[]{:S(2)}) collective-permute-start(bf16[200,512]{1,0:T(8,128)(2,1)S(1)} %get-tuple-element.23), channel_id=1, source_target_pairs={{0,16},{16,0},{32,48},{48,32},{64,80},{80,64},{96,112},{112,96},{1... | collective-permute-start | bytes 614408 | tf_op jit(solution)/shard_map/ppermute | solution.py:509
  5.2 0.0 collective-permute-start.1
  5.2 0.0 copy-done.4
  5.2 0.0 copy-done
  5.2 0.0 copy-done.7
  5.2 0.0 copy-done.6
  5.3 1.0 %own_kernel.1 = (bf16[2,5,32,1536]{3,2,1,0:T(8,128)(2,1)S(1)}, bf16[64,1536]{1,0:T(8,128)(2,1)S(1)}, f32[2,4,64,128]{3,2,1,0:T(8,128)S(1)}, f32[2,2,2,64,128]{4,3,2,1,0:T(8,128)S(1)}, f32[2,64,128]{2,1,0:T(8,128)S(1)}) custom-call(bf16[512,1536]{1,0:T(8,128)(2,1)S(1)} %copy-done, f32[16,64,64]{2,1,0:T(8,128)S(1)} %copy-done.6, f32[8,64,64]{2,1,0:T(8,128)S(1)} %copy-done.7, ...), custom_call_target="tpu_custom_call" | custom-call | flops 1500000000 | bytes 1000000 | tf_op jit(solution)/shard_map/own_kernel/pallas_call | solution.py:475
  6.3 0.0 collective-permute-done.pair_ref
  6.3 0.0 copy-done.1
  6.3 0.0 copy-start.3
  6.3 1.4 %pair_kernel.1 = (f32[160,512]{1,0:T(8,128)S(1)}, bf16[32,1024]{1,0:T(8,128)(2,1)S(1)}) custom-call(bf16[200,512]{1,0:T(8,128)(2,1)S(1)} %collective-permute-done.pair_ref, s32[8,48]{1,0:T(8,128)S(1)} %get-tuple-element.22.ids_ref, bf16[2,5,32,1536]{3,2,1,0:T(8,128)(2,1)S(1)} %get-tuple-element.25.inside_ref, bf16[512,1536]{1,0:T(8,128)(2,1)S(1)} %copy-done, ...), custom_call_target="tpu_custom_call" | custom-call | flops 300000000 | bytes 1000000 | tf_op jit(solution)/shard_map/pair_kernel/pallas_call | solution.py:475
  7.7 3.0 %collective-permute-done.1.cross_ref = bf16[200,512]{1,0:T(8,128)(2,1)S(1)} collective-permute-done((bf16[200,512]{1,0:T(8,128)(2,1)S(1)}, bf16[200,512]{1,0:T(8,128)(2,1)S(1)}, u32[]{:S(2)}, u32[]{:S(2)}) %collective-permute-start.1) | collective-permute-done | bytes 204832 | tf_op jit(solution)/shard_map/ppermute | solution.py:508
  10.7 0.0 copy-start.2
  10.7 0.1 edge_kernel.1
  10.8 1.1 %collective-permute-start.2 = (bf16[72,512]{1,0:T(8,128)(2,1)S(1)}, bf16[72,512]{1,0:T(8,128)(2,1)S(1)}, u32[]{:S(2)}, u32[]{:S(2)}) collective-permute-start(bf16[72,512]{1,0:T(8,128)(2,1)S(1)} %get-tuple-element.28), channel_id=1, source_target_pairs={{0,1},{1,0},{2,3},{3,2},{4,5},{5,4},{6,7},{7,6},{8,9},{9,8},{10,11... | collective-permute-start | bytes 221192 | tf_op jit(solution)/shard_map/ppermute | solution.py:534
  11.9 5.5 %collective-permute-start.3 = (bf16[72,512]{1,0:T(8,128)(2,1)S(1)}, bf16[72,512]{1,0:T(8,128)(2,1)S(1)}, u32[]{:S(2)}, u32[]{:S(2)}) collective-permute-start(bf16[72,512]{1,0:T(8,128)(2,1)S(1)} %get-tuple-element.29), channel_id=1, source_target_pairs={{0,15},{1,2},{2,1},{3,4},{4,3},{5,6},{6,5},{7,8},{8,7},{9,10},{10,... | collective-permute-start | bytes 221192 | tf_op jit(solution)/shard_map/ppermute | solution.py:535
  17.4 1.4 %cross_kernel.1 = (f32[160,512]{1,0:T(8,128)S(1)}, bf16[32,1024]{1,0:T(8,128)(2,1)S(1)}) custom-call(bf16[200,512]{1,0:T(8,128)(2,1)S(1)} %collective-permute-done.1.cross_ref, f32[16,128]{1,0:T(8,128)S(1)} %get-tuple-element.30.ids_ref, bf16[2,5,32,1536]{3,2,1,0:T(8,128)(2,1)S(1)} %get-tuple-element.25.inside_ref, bf16[512,1536]{1,0:T(8,128)(2,1)S(1)} %copy-done, ...), custom_call_target="tpu_custom_call" | custom-call | flops 300000000 | bytes 1000000 | tf_op jit(solution)/shard_map/cross_kernel/pallas_call | solution.py:475
  18.7 0.0 collective-permute-done.2.inner_ref
  18.8 0.4 %collective-permute-done.3.outer_ref = bf16[72,512]{1,0:T(8,128)(2,1)S(1)} collective-permute-done((bf16[72,512]{1,0:T(8,128)(2,1)S(1)}, bf16[72,512]{1,0:T(8,128)(2,1)S(1)}, u32[]{:S(2)}, u32[]{:S(2)}) %collective-permute-start.3) | collective-permute-done | bytes 73760 | tf_op jit(solution)/shard_map/ppermute | solution.py:535
  19.1 0.0 copy-done.3
  19.1 0.0 copy-done.2
  19.1 2.4 %final_kernel.1 = (bf16[8,48,512]{2,1,0:T(8,128)(2,1)}, bf16[96,1024]{1,0:T(8,128)(2,1)S(1)}, bf16[96,1024]{1,0:T(8,128)(2,1)S(1)}) custom-call(bf16[8,48,512]{2,1,0:T(8,128)(2,1)S(1)} %copy-done.4, bf16[72,512]{1,0:T(8,128)(2,1)S(1)} %collective-permute-done.2.inner_ref, bf16[72,512]{1,0:T(8,128)(2,1)S(1)} %collective-permute-done.3.outer_ref, ...), custom_call_target="tpu_custom_call" | custom-call | flops 1000000000 | bytes 1000000 | tf_op jit(solution)/shard_map/final_kernel/pallas_call | solution.py:475
  21.6 0.0 copy-start.5
  21.6 3.2 %collective-permute-start.4 = (bf16[96,1024]{1,0:T(8,128)(2,1)S(1)}, bf16[96,1024]{1,0:T(8,128)(2,1)S(1)}, u32[]{:S(2)}, u32[]{:S(2)}) collective-permute-start(bf16[96,1024]{1,0:T(8,128)(2,1)S(1)} %get-tuple-element.38.kv_ref), channel_id=1, source_target_pairs={{0,16},{16,0},{32,48},{48,32},{64,80},{80,64},{96,112},{112,96},{1... | collective-permute-start | bytes 589832 | tf_op jit(solution)/shard_map/ppermute | solution.py:558
  24.8 0.5 %query_kernel.1 = (bf16[96,512]{1,0:T(8,128)(2,1)S(1)}, f32[6,32,128]{2,1,0:T(8,128)S(1)}) custom-call(bf16[96,1024]{1,0:T(8,128)(2,1)S(1)} %get-tuple-element.37.merged_ref, bf16[96,1024]{1,0:T(8,128)(2,1)S(1)} %get-tuple-element.38.kv_ref, f32[2,64,128]{2,1,0:T(8,128)S(1)} %get-tuple-element.39.bias_ref, bf16[1024,1536]{1,0:T(8,128)(2,1)S(1)} %copy-done.3), custom_call_target="tpu_custom_call" | custom-call | flops 1000000000 | bytes 1000000 | tf_op jit(solution)/shard_map/query_kernel/pallas_call | solution.py:475
  25.4 0.5 %collective-permute-done.4.other_ref = bf16[96,1024]{1,0:T(8,128)(2,1)S(1)} collective-permute-done((bf16[96,1024]{1,0:T(8,128)(2,1)S(1)}, bf16[96,1024]{1,0:T(8,128)(2,1)S(1)}, u32[]{:S(2)}, u32[]{:S(2)}) %collective-permute-start.4) | collective-permute-done | bytes 196640 | tf_op jit(solution)/shard_map/ppermute | solution.py:558
  25.9 0.0 copy-done.5
  25.9 1.4 %level_two_kernel.1 = bf16[4,24,1024]{2,1,0:T(8,128)(2,1)} custom-call(bf16[96,512]{1,0:T(8,128)(2,1)S(1)} %get-tuple-element.40.query_ref, f32[6,32,128]{2,1,0:T(8,128)S(1)} %get-tuple-element.41.score_ref, bf16[96,1024]{1,0:T(8,128)(2,1)S(1)} %get-tuple-element.38.kv_ref, bf16[96,1024]{1,0:T(8,128)(2,1)S(1)} %collective-permute-done.4.other_ref, ...), custom_call_target="tpu_custom_call" | custom-call | flops 1000000000 | bytes 1000000 | tf_op jit(solution)/shard_map/level_two_kernel/pallas_call | solution.py:475
Async XLA Ops:
  0.6 4.6 %copy-start.4 = (bf16[8,48,512]{2,1,0:T(8,128)(2,1)S(1)}, bf16[8,48,512]{2,1,0:T(8,128)(2,1)}, u32[]{:S(2)}) copy-start(bf16[8,48,512]{2,1,0:T(8,128)(2,1)} %tok_ref.5) | copy-start | bytes 1179652
  0.6 4.6 %copy-start = (bf16[512,1536]{1,0:T(8,128)(2,1)S(1)}, bf16[512,1536]{1,0:T(8,128)(2,1)}, u32[]{:S(2)}) copy-start(bf16[512,1536]{1,0:T(8,128)(2,1)} %qkv_ref.7) | copy-start | bytes 4718596
  0.7 4.6 %copy-start.7 = (f32[8,64,64]{2,1,0:T(8,128)S(1)}, f32[8,64,64]{2,1,0:T(8,128)}, u32[]{:S(2)}) copy-start(f32[8,64,64]{2,1,0:T(8,128)} %two_ref.3) | copy-start | bytes 393220
  0.7 4.6 %copy-start.6 = (f32[16,64,64]{2,1,0:T(8,128)S(1)}, f32[16,64,64]{2,1,0:T(8,128)}, u32[]{:S(2)}) copy-start(f32[16,64,64]{2,1,0:T(8,128)} %one_ref.1) | copy-start | bytes 786436
  1.9 4.4 %copy-start.1 = (bf16[512,512]{1,0:T(8,128)(2,1)S(1)}, bf16[512,512]{1,0:T(8,128)(2,1)}, u32[]{:S(2)}) copy-start(bf16[512,512]{1,0:T(8,128)(2,1)} %out_ref.6) | copy-start | bytes 1572868
  1.9 4.4 %collective-permute-start = (bf16[200,512]{1,0:T(8,128)(2,1)S(1)}, bf16[200,512]{1,0:T(8,128)(2,1)S(1)}, u32[]{:S(2)}, u32[]{:S(2)}) collective-permute-start(bf16[200,512]{1,0:T(8,128)(2,1)S(1)} %get-tuple-element.23), channel_id=1, source_target_pairs={{0,16},{16,0},{32,48},{48,32},{64,80},{80,64},{96,112},{112,96},{1... | collective-permute-start | bytes 614408 | tf_op jit(solution)/shard_map/ppermute | solution.py:509
  5.2 5.5 %collective-permute-start.1 = (bf16[200,512]{1,0:T(8,128)(2,1)S(1)}, bf16[200,512]{1,0:T(8,128)(2,1)S(1)}, u32[]{:S(2)}, u32[]{:S(2)}) collective-permute-start(bf16[200,512]{1,0:T(8,128)(2,1)S(1)} %get-tuple-element.24), channel_id=1, source_target_pairs={{0,240},{16,32},{32,16},{48,64},{64,48},{80,96},{96,80},{112,128},... | collective-permute-start | bytes 614408 | tf_op jit(solution)/shard_map/ppermute | solution.py:508
  6.3 12.8 %copy-start.3 = (bf16[1024,1536]{1,0:T(8,128)(2,1)S(1)}, bf16[1024,1536]{1,0:T(8,128)(2,1)}, u32[]{:S(2)}) copy-start(bf16[1024,1536]{1,0:T(8,128)(2,1)} %two_ref.5) | copy-start | bytes 9437188
  10.7 8.4 %copy-start.2 = (bf16[2048,1024]{1,0:T(8,128)(2,1)S(1)}, bf16[2048,1024]{1,0:T(8,128)(2,1)}, u32[]{:S(2)}) copy-start(bf16[2048,1024]{1,0:T(8,128)(2,1)} %merge_ref.1) | copy-start | bytes 12582916
  10.8 8.0 %collective-permute-start.2 = (bf16[72,512]{1,0:T(8,128)(2,1)S(1)}, bf16[72,512]{1,0:T(8,128)(2,1)S(1)}, u32[]{:S(2)}, u32[]{:S(2)}) collective-permute-start(bf16[72,512]{1,0:T(8,128)(2,1)S(1)} %get-tuple-element.28), channel_id=1, source_target_pairs={{0,1},{1,0},{2,3},{3,2},{4,5},{5,4},{6,7},{7,6},{8,9},{9,8},{10,11... | collective-permute-start | bytes 221192 | tf_op jit(solution)/shard_map/ppermute | solution.py:534
  11.9 7.3 %collective-permute-start.3 = (bf16[72,512]{1,0:T(8,128)(2,1)S(1)}, bf16[72,512]{1,0:T(8,128)(2,1)S(1)}, u32[]{:S(2)}, u32[]{:S(2)}) collective-permute-start(bf16[72,512]{1,0:T(8,128)(2,1)S(1)} %get-tuple-element.29), channel_id=1, source_target_pairs={{0,15},{1,2},{2,1},{3,4},{4,3},{5,6},{6,5},{7,8},{8,7},{9,10},{10,... | collective-permute-start | bytes 221192 | tf_op jit(solution)/shard_map/ppermute | solution.py:535
  21.6 4.3 %copy-start.5 = (bf16[512,1024]{1,0:T(8,128)(2,1)S(1)}, bf16[512,1024]{1,0:T(8,128)(2,1)}, u32[]{:S(2)}) copy-start(bf16[512,1024]{1,0:T(8,128)(2,1)} %out_ref.7) | copy-start | bytes 3145732
  21.6 4.3 %collective-permute-start.4 = (bf16[96,1024]{1,0:T(8,128)(2,1)S(1)}, bf16[96,1024]{1,0:T(8,128)(2,1)S(1)}, u32[]{:S(2)}, u32[]{:S(2)}) collective-permute-start(bf16[96,1024]{1,0:T(8,128)(2,1)S(1)} %get-tuple-element.38.kv_ref), channel_id=1, source_target_pairs={{0,16},{16,0},{32,48},{48,32},{64,80},{80,64},{96,112},{112,96},{1... | collective-permute-start | bytes 589832 | tf_op jit(solution)/shard_map/ppermute | solution.py:558
